TPU v7x, 256 devices: a whole 4x4x8 slice. The times are simulated.
256 devices in a mesh: segment: 4 (over x), tm: 2 (over core), space: 32 (over z, y).
Axes of the slice: x: 4, y: 4, z: 8, core: 2. Of those that a mesh axis runs over, the one named last changes fastest.
Arguments:
- inputs: bfloat16 [4, 8, 256, 16, 128], P(None, 'tm', 'space'), may hold values from -6 to 6
- weights: bfloat16 [4, 3456, 128], P('segment'), may hold values from -0.109375 to 0.109375
- cotangent: bfloat16 [4, 8, 256, 16, 128], P(None, 'tm', 'space'), may hold values from -0.023925781 to 0.023925781
Outputs:
- weight_grads: float32 [4, 3456, 128], P('segment')
All inputs are finite; a program needn't handle non-finite values.
Results may differ from a plain program's by a relative error of at most 0.009.
Values may be sent and summed in bfloat16 or wider, within the bound.
No kernel may reach another device: no remote copies, remote signals or barrier semaphores. Data moves between devices by JAX's collectives and lax.ppermute only.
A program may use at most 64 MiB of HBM per device.

v0:
```python
import jax
import jax.numpy as jnp
from jax import lax
from jax.sharding import PartitionSpec as P


def from_behind(array, axis, by):
    count = lax.axis_size(axis)
    pairs = [(i, i + by) for i in range(count) if 0 <= i + by < count]
    return lax.ppermute(array, axis, pairs)


def with_halo(array, sides, width):
    for axis, dim in sides:
        count, length = (lax.axis_size(axis), array.shape[dim])
        up = [(i, (i + 1) % count) for i in range(count - 1)]
        down = [(j, i) for i, j in up]
        last = lax.slice_in_dim(array, length - width, length, axis=dim)
        leading = lax.slice_in_dim(array, 0, width, axis=dim)
        before = lax.ppermute(last, axis, up)
        after = lax.ppermute(leading, axis, down)
        array = jnp.concatenate([before, array, after], axis=dim)
    return array


def frame_shift(window_in, offset):
    return from_behind(window_in, "tm", offset)


def segment_shift(window_in, offset):
    return from_behind(window_in, "segment", offset)


def bands(extended):
    widened = with_halo(extended, (("space", 1),), 1)
    return jnp.pad(widened, ((0, 0), (0, 0), (1, 1), (0, 0)))


def causal_ext(hidden):
    return bands(jnp.concatenate([frame_shift(hidden[-2:], 1), hidden], 0))


def ahead_ext(delta_z):
    return bands(jnp.concatenate([delta_z, frame_shift(delta_z[:2], -1)], 0))


def taps(extended, frame_count, row_count, col_count, flipped):
    pieces = []
    for lag_t in range(3):
        for lag_r in range(3):
            for lag_c in range(3):
                if flipped:
                    start_t, start_r, start_c = (2 - lag_t, 2 - lag_r, 2 - lag_c)
                else:
                    start_t, start_r, start_c = (lag_t, lag_r, lag_c)
                pieces.append(
                    extended[
                        start_t : start_t + frame_count,
                        start_r : start_r + row_count,
                        start_c : start_c + col_count,
                    ]
                )
    joined = jnp.concatenate(pieces, -1)
    return joined.reshape(frame_count * row_count * col_count, -1)


def flip_matrix(matrix):
    channels = matrix.shape[1]
    return (
        matrix.reshape(27, channels, channels).transpose(0, 2, 1).reshape(27 * channels, channels)
    )


def layer_forward(hidden, extended, matrix):
    frame_count, row_count, col_count, channels = hidden.shape
    cells = frame_count * row_count * col_count
    pre_act = jnp.dot(
        taps(extended, frame_count, row_count, col_count, False),
        matrix,
        preferred_element_type=jnp.float32,
    )
    output = hidden.reshape(cells, channels).astype(jnp.float32) + jax.nn.silu(pre_act)
    return output.astype(jnp.bfloat16).reshape(hidden.shape)


def layer_backward(extended, delta_y, matrix, flip_weight, is_valid):
    frame_count, row_count, col_count, channels = delta_y.shape
    cells = frame_count * row_count * col_count
    patches = taps(extended, frame_count, row_count, col_count, False)
    pre_act = jnp.dot(patches, matrix, preferred_element_type=jnp.float32)
    sig_val = jax.nn.sigmoid(pre_act)
    delta_z = (
        delta_y.reshape(cells, channels).astype(jnp.float32)
        * sig_val
        * (1.0 + pre_act * (1.0 - sig_val))
    )
    delta_z = jnp.where(is_valid, delta_z, 0.0).astype(jnp.bfloat16)
    partial_value = lax.dot_general(
        patches, delta_z, (((0,), (0,)), ((), ())), preferred_element_type=jnp.float32
    )
    ahead = ahead_ext(delta_z.reshape(delta_y.shape))
    adjoint = jnp.dot(
        taps(ahead, frame_count, row_count, col_count, True),
        flip_weight,
        preferred_element_type=jnp.float32,
    )
    delta_x = (
        (delta_y.reshape(cells, channels).astype(jnp.float32) + adjoint)
        .astype(jnp.bfloat16)
        .reshape(delta_y.shape)
    )
    return (partial_value, delta_x)


def body(inputs, weights, cotangent):
    segment_at = lax.axis_index("segment")
    segments = lax.axis_size("segment")
    micro_count = inputs.shape[0]
    frame_count, row_count, col_count, channels = inputs.shape[1:]
    matrix = weights[0]
    flip_weight = flip_matrix(matrix)
    saved = jnp.zeros(
        (micro_count, frame_count + 2, row_count + 2, col_count + 2, channels), jnp.bfloat16
    )
    incoming = jnp.zeros(inputs.shape[1:], jnp.bfloat16)
    for moment in range(micro_count + segments - 1):
        entering = inputs[min(moment, micro_count - 1)]
        hidden = jnp.where(segment_at == 0, entering, incoming)
        extended = causal_ext(hidden)
        output = layer_forward(hidden, extended, matrix)
        slot_index = moment - segment_at
        is_valid = (slot_index >= 0) & (slot_index < micro_count)
        position = jnp.clip(slot_index, 0, micro_count - 1)
        saved = jnp.where(
            is_valid, lax.dynamic_update_index_in_dim(saved, extended, position, 0), saved
        )
        incoming = segment_shift(output, 1)
    own_grad = jnp.zeros((matrix.shape[0], channels), jnp.float32)
    incoming = jnp.zeros(inputs.shape[1:], jnp.bfloat16)
    for moment in range(micro_count + segments - 1):
        slot_index = moment - (segments - 1 - segment_at)
        is_valid = (slot_index >= 0) & (slot_index < micro_count)
        position = jnp.clip(slot_index, 0, micro_count - 1)
        seeded = cotangent[min(moment, micro_count - 1)]
        delta_y = jnp.where(segment_at == segments - 1, seeded, incoming)
        extended = lax.dynamic_index_in_dim(saved, position, 0, keepdims=False)
        partial_value, delta_x = layer_backward(extended, delta_y, matrix, flip_weight, is_valid)
        own_grad = own_grad + partial_value
        incoming = segment_shift(delta_x, -1)
    own_grad = own_grad[None]
    return lax.psum(own_grad, ("tm", "space"))


def solution(mesh):
    return jax.shard_map(
        body,
        mesh=mesh,
        in_specs=(
            P(None, "tm", "space", None, None),
            P("segment", None, None),
            P(None, "tm", "space", None, None),
        ),
        out_specs=P("segment", None, None),
        check_vma=False,
    )
```

profile of v0, /device:TPU:1, one launch (start us, length us, event | category | flops | bytes accessed | tf_op | source)
XLA Modules:
  0.0 527.5 jit_solution(17892061705482073975)
XLA Ops:
  14.0 4.1 collective-permute-start.1
  31.2 4.6 collective-permute-start.5
  39.3 4.1 collective-permute-start.7
  50.5 4.6 collective-permute-start.9
  69.9 4.6 collective-permute-start.13
  89.3 6.5 %collective-permute-start.17 = (bf16[6,1,16,128]{3,2,1,0:T(8,128)(2,1)S(1)}, bf16[6,1,16,128]{3,2,1,0:T(8,128)(2,1)S(1)}, u32[]{:S(2)}, u32[]{:S(2)}) collective-permute-start(bf16[6,1,16,128]{3,2,1,0:T(8,128)(2,1)S(1)} %get-tuple-element.200), channel_id=1, source_target_pairs={{0,1},{1,2},{2,3},{3,4},{4,5},{5,6},{6,7},{7,8},{8,9},{9,10},{10,1... | collective-permute-start | bytes 73736 | tf_op jit(solution)/shard_map/ppermute | solution.py:20
  100.2 4.1 collective-permute-start.19
  111.4 6.7 %collective-permute-start.21 = (bf16[6,1,16,128]{3,2,1,0:T(8,128)(2,1)S(1)}, bf16[6,1,16,128]{3,2,1,0:T(8,128)(2,1)S(1)}, u32[]{:S(2)}, u32[]{:S(2)}) collective-permute-start(bf16[6,1,16,128]{3,2,1,0:T(8,128)(2,1)S(1)} %get-tuple-element.196), channel_id=1, source_target_pairs={{0,1},{1,2},{2,3},{3,4},{4,5},{5,6},{6,7},{7,8},{8,9},{9,10},{10,1... | collective-permute-start | bytes 73736 | tf_op jit(solution)/shard_map/ppermute | solution.py:20
  121.7 4.1 collective-permute-start.23
  132.9 6.7 %collective-permute-start.25 = (bf16[6,1,16,128]{3,2,1,0:T(8,128)(2,1)S(1)}, bf16[6,1,16,128]{3,2,1,0:T(8,128)(2,1)S(1)}, u32[]{:S(2)}, u32[]{:S(2)}) collective-permute-start(bf16[6,1,16,128]{3,2,1,0:T(8,128)(2,1)S(1)} %get-tuple-element.192), channel_id=1, source_target_pairs={{0,1},{1,2},{2,3},{3,4},{4,5},{5,6},{6,7},{7,8},{8,9},{9,10},{10,1... | collective-permute-start | bytes 73736 | tf_op jit(solution)/shard_map/ppermute | solution.py:20
  158.9 6.7 %collective-permute-start.28 = (bf16[6,1,16,128]{3,2,1,0:T(8,128)(2,1)S(1)}, bf16[6,1,16,128]{3,2,1,0:T(8,128)(2,1)S(1)}, u32[]{:S(2)}, u32[]{:S(2)}) collective-permute-start(bf16[6,1,16,128]{3,2,1,0:T(8,128)(2,1)S(1)} %get-tuple-element.190), channel_id=1, source_target_pairs={{0,1},{1,2},{2,3},{3,4},{4,5},{5,6},{6,7},{7,8},{8,9},{9,10},{10,1... | collective-permute-start | bytes 73736 | tf_op jit(solution)/shard_map/ppermute | solution.py:20
  170.9 6.4 %collective-permute-done.30 = bf16[4,8,16,128]{3,2,1,0:T(8,128)(2,1)S(1)} collective-permute-done((bf16[4,8,16,128]{3,2,1,0:T(8,128)(2,1)S(1)}, bf16[4,8,16,128]{3,2,1,0:T(8,128)(2,1)S(1)}, u32[]{:S(2)}, u32[]{:S(2)}) %collective-permute-start.30) | collective-permute-done | bytes 131104 | tf_op jit(solution)/shard_map/ppermute | solution.py:10
  183.4 6.5 %collective-permute-start.32 = (bf16[6,1,16,128]{3,2,1,0:T(8,128)(2,1)S(1)}, bf16[6,1,16,128]{3,2,1,0:T(8,128)(2,1)S(1)}, u32[]{:S(2)}, u32[]{:S(2)}) collective-permute-start(bf16[6,1,16,128]{3,2,1,0:T(8,128)(2,1)S(1)} %get-tuple-element.184), channel_id=1, source_target_pairs={{0,1},{1,2},{2,3},{3,4},{4,5},{5,6},{6,7},{7,8},{8,9},{9,10},{10,1... | collective-permute-start | bytes 73736 | tf_op jit(solution)/shard_map/ppermute | solution.py:20
  195.0 4.3 collective-permute-done.34
  200.5 4.3 collective-permute-start.35
  206.9 6.7 %collective-permute-start.36 = (bf16[6,1,16,128]{3,2,1,0:T(8,128)(2,1)S(1)}, bf16[6,1,16,128]{3,2,1,0:T(8,128)(2,1)S(1)}, u32[]{:S(2)}, u32[]{:S(2)}) collective-permute-start(bf16[6,1,16,128]{3,2,1,0:T(8,128)(2,1)S(1)} %get-tuple-element.178), channel_id=1, source_target_pairs={{0,1},{1,2},{2,3},{3,4},{4,5},{5,6},{6,7},{7,8},{8,9},{9,10},{10,1... | collective-permute-start | bytes 73736 | tf_op jit(solution)/shard_map/ppermute | solution.py:20
  218.8 4.3 collective-permute-done.38
  224.4 4.3 collective-permute-start.39
  230.8 6.7 %collective-permute-start.40 = (bf16[6,1,16,128]{3,2,1,0:T(8,128)(2,1)S(1)}, bf16[6,1,16,128]{3,2,1,0:T(8,128)(2,1)S(1)}, u32[]{:S(2)}, u32[]{:S(2)}) collective-permute-start(bf16[6,1,16,128]{3,2,1,0:T(8,128)(2,1)S(1)} %get-tuple-element.172), channel_id=1, source_target_pairs={{0,1},{1,2},{2,3},{3,4},{4,5},{5,6},{6,7},{7,8},{8,9},{9,10},{10,1... | collective-permute-start | bytes 73736 | tf_op jit(solution)/shard_map/ppermute | solution.py:20
  248.3 4.5 collective-permute-start.43
  255.2 6.6 %collective-permute-start.44 = (bf16[6,1,16,128]{3,2,1,0:T(8,128)(2,1)S(1)}, bf16[6,1,16,128]{3,2,1,0:T(8,128)(2,1)S(1)}, u32[]{:S(2)}, u32[]{:S(2)}) collective-permute-start(bf16[6,1,16,128]{3,2,1,0:T(8,128)(2,1)S(1)} %get-tuple-element.166), channel_id=1, source_target_pairs={{0,1},{1,2},{2,3},{3,4},{4,5},{5,6},{6,7},{7,8},{8,9},{9,10},{10,1... | collective-permute-start | bytes 73736 | tf_op jit(solution)/shard_map/ppermute | solution.py:20
  279.0 6.7 %collective-permute-start.48 = (bf16[6,1,16,128]{3,2,1,0:T(8,128)(2,1)S(1)}, bf16[6,1,16,128]{3,2,1,0:T(8,128)(2,1)S(1)}, u32[]{:S(2)}, u32[]{:S(2)}) collective-permute-start(bf16[6,1,16,128]{3,2,1,0:T(8,128)(2,1)S(1)} %get-tuple-element.160), channel_id=1, source_target_pairs={{0,1},{1,2},{2,3},{3,4},{4,5},{5,6},{6,7},{7,8},{8,9},{9,10},{10,1... | collective-permute-start | bytes 73736 | tf_op jit(solution)/shard_map/ppermute | solution.py:20
  296.0 6.8 %fusion = f32[1,3456,128]{2,1,0:T(8,128)} fusion(f32[3456,128]{1,0:T(8,128)} %convolution_add_fusion.1, bf16[512,3456]{1,0:T(8,128)(2,1)S(1)} %bitcast.388, bf16[512,128]{1,0:T(8,128)(2,1)} %bitcast.432, bf16[1,3456,128]{2,1,0:T(8,128)(2,1)} %param.4, pred[]{:T(512)S(6)} %and.56), kind=kOutput, calls=%fused_computation.6 | convolution fusion | flops 907132928 | bytes 8093697 | tf_op jit(solution)/shard_map/dot_general | solution.py:98
  302.8 214.7 %all-reduce.15.cloned.1.call-done = f32[1,3456,128]{2,1,0:T(8,128)} async-done(((f32[1,3456,128]{2,1,0:T(8,128)}), f32[1,3456,128]{2,1,0:T(8,128)}) %all-reduce.15.cloned.1.call-update) | async-done | bytes 1769488 | tf_op jit(solution)/shard_map/psum | solution.py:151
  (726 shorter events, 169.6 us)
Async XLA Ops:
  6.5 510.9 %all-reduce.15.cloned.1.call-start = ((), (), s32[]{:S(2)}) async-start(), calls=%async_computation | async-start | bytes 3538944 | tf_op jit(solution)/shard_map/psum | solution.py:151
  88.1 9.5 %collective-permute-start.18 = (bf16[6,1,16,128]{3,2,1,0:T(8,128)(2,1)S(1)}, bf16[6,1,16,128]{3,2,1,0:T(8,128)(2,1)S(1)}, u32[]{:S(2)}, u32[]{:S(2)}) collective-permute-start(bf16[6,1,16,128]{3,2,1,0:T(8,128)(2,1)S(1)} %get-tuple-element.201), channel_id=1, source_target_pairs={{1,0},{2,1},{3,2},{4,3},{5,4},{6,5},{7,6},{8,7},{9,8},{10,9},{11,1... | collective-permute-start | bytes 73736 | tf_op jit(solution)/shard_map/ppermute | solution.py:21
  89.3 8.2 %collective-permute-start.17 = (bf16[6,1,16,128]{3,2,1,0:T(8,128)(2,1)S(1)}, bf16[6,1,16,128]{3,2,1,0:T(8,128)(2,1)S(1)}, u32[]{:S(2)}, u32[]{:S(2)}) collective-permute-start(bf16[6,1,16,128]{3,2,1,0:T(8,128)(2,1)S(1)} %get-tuple-element.200), channel_id=1, source_target_pairs={{0,1},{1,2},{2,3},{3,4},{4,5},{5,6},{6,7},{7,8},{8,9},{9,10},{10,1... | collective-permute-start | bytes 73736 | tf_op jit(solution)/shard_map/ppermute | solution.py:20
  100.2 6.5 %collective-permute-start.19 = (bf16[4,8,16,128]{3,2,1,0:T(8,128)(2,1)S(1)}, bf16[4,8,16,128]{3,2,1,0:T(8,128)(2,1)S(1)}, u32[]{:S(2)}, u32[]{:S(2)}) collective-permute-start(bf16[4,8,16,128]{3,2,1,0:T(8,128)(2,1)S(1)} %bitcast.622), channel_id=1, source_target_pairs={{0,64},{64,128},{128,192},{1,65},{65,129},{129,193},{2,66},{66,130... | collective-permute-start | bytes 393224 | tf_op jit(solution)/shard_map/ppermute | solution.py:10
  110.1 8.2 %collective-permute-start.22 = (bf16[6,1,16,128]{3,2,1,0:T(8,128)(2,1)S(1)}, bf16[6,1,16,128]{3,2,1,0:T(8,128)(2,1)S(1)}, u32[]{:S(2)}, u32[]{:S(2)}) collective-permute-start(bf16[6,1,16,128]{3,2,1,0:T(8,128)(2,1)S(1)} %get-tuple-element.197), channel_id=1, source_target_pairs={{1,0},{2,1},{3,2},{4,3},{5,4},{6,5},{7,6},{8,7},{9,8},{10,9},{11,1... | collective-permute-start | bytes 73736 | tf_op jit(solution)/shard_map/ppermute | solution.py:21
  111.4 7.6 %collective-permute-start.21 = (bf16[6,1,16,128]{3,2,1,0:T(8,128)(2,1)S(1)}, bf16[6,1,16,128]{3,2,1,0:T(8,128)(2,1)S(1)}, u32[]{:S(2)}, u32[]{:S(2)}) collective-permute-start(bf16[6,1,16,128]{3,2,1,0:T(8,128)(2,1)S(1)} %get-tuple-element.196), channel_id=1, source_target_pairs={{0,1},{1,2},{2,3},{3,4},{4,5},{5,6},{6,7},{7,8},{8,9},{9,10},{10,1... | collective-permute-start | bytes 73736 | tf_op jit(solution)/shard_map/ppermute | solution.py:20
  121.7 6.0 %collective-permute-start.23 = (bf16[4,8,16,128]{3,2,1,0:T(8,128)(2,1)S(1)}, bf16[4,8,16,128]{3,2,1,0:T(8,128)(2,1)S(1)}, u32[]{:S(2)}, u32[]{:S(2)}) collective-permute-start(bf16[4,8,16,128]{3,2,1,0:T(8,128)(2,1)S(1)} %bitcast.614), channel_id=1, source_target_pairs={{0,64},{64,128},{128,192},{1,65},{65,129},{129,193},{2,66},{66,130... | collective-permute-start | bytes 393224 | tf_op jit(solution)/shard_map/ppermute | solution.py:10
  131.6 8.2 %collective-permute-start.26 = (bf16[6,1,16,128]{3,2,1,0:T(8,128)(2,1)S(1)}, bf16[6,1,16,128]{3,2,1,0:T(8,128)(2,1)S(1)}, u32[]{:S(2)}, u32[]{:S(2)}) collective-permute-start(bf16[6,1,16,128]{3,2,1,0:T(8,128)(2,1)S(1)} %get-tuple-element.193), channel_id=1, source_target_pairs={{1,0},{2,1},{3,2},{4,3},{5,4},{6,5},{7,6},{8,7},{9,8},{10,9},{11,1... | collective-permute-start | bytes 73736 | tf_op jit(solution)/shard_map/ppermute | solution.py:21
  132.9 7.6 %collective-permute-start.25 = (bf16[6,1,16,128]{3,2,1,0:T(8,128)(2,1)S(1)}, bf16[6,1,16,128]{3,2,1,0:T(8,128)(2,1)S(1)}, u32[]{:S(2)}, u32[]{:S(2)}) collective-permute-start(bf16[6,1,16,128]{3,2,1,0:T(8,128)(2,1)S(1)} %get-tuple-element.192), channel_id=1, source_target_pairs={{0,1},{1,2},{2,3},{3,4},{4,5},{5,6},{6,7},{7,8},{8,9},{9,10},{10,1... | collective-permute-start | bytes 73736 | tf_op jit(solution)/shard_map/ppermute | solution.py:20
  146.7 10.9 %collective-permute-start.27 = (bf16[2,8,16,128]{3,2,1,0:T(8,128)(2,1)S(1)}, bf16[2,8,16,128]{3,2,1,0:T(8,128)(2,1)S(1)}, u32[]{:S(2)}, u32[]{:S(2)}) collective-permute-start(bf16[2,8,16,128]{3,2,1,0:T(8,128)(2,1)S(1)} %bitcast.602), channel_id=1, source_target_pairs={{32,0},{33,1},{34,2},{35,3},{36,4},{37,5},{38,6},{39,7},{40,8},{41... | collective-permute-start | bytes 196616 | tf_op jit(solution)/shard_map/ppermute | solution.py:10
  157.6 8.0 %collective-permute-start.29 = (bf16[6,1,16,128]{3,2,1,0:T(8,128)(2,1)S(1)}, bf16[6,1,16,128]{3,2,1,0:T(8,128)(2,1)S(1)}, u32[]{:S(2)}, u32[]{:S(2)}) collective-permute-start(bf16[6,1,16,128]{3,2,1,0:T(8,128)(2,1)S(1)} %get-tuple-element.191), channel_id=1, source_target_pairs={{1,0},{2,1},{3,2},{4,3},{5,4},{6,5},{7,6},{8,7},{9,8},{10,9},{11,1... | collective-permute-start | bytes 73736 | tf_op jit(solution)/shard_map/ppermute | solution.py:21
  158.9 7.6 %collective-permute-start.28 = (bf16[6,1,16,128]{3,2,1,0:T(8,128)(2,1)S(1)}, bf16[6,1,16,128]{3,2,1,0:T(8,128)(2,1)S(1)}, u32[]{:S(2)}, u32[]{:S(2)}) collective-permute-start(bf16[6,1,16,128]{3,2,1,0:T(8,128)(2,1)S(1)} %get-tuple-element.190), channel_id=1, source_target_pairs={{0,1},{1,2},{2,3},{3,4},{4,5},{5,6},{6,7},{7,8},{8,9},{9,10},{10,1... | collective-permute-start | bytes 73736 | tf_op jit(solution)/shard_map/ppermute | solution.py:20
  169.6 7.8 %collective-permute-start.30 = (bf16[4,8,16,128]{3,2,1,0:T(8,128)(2,1)S(1)}, bf16[4,8,16,128]{3,2,1,0:T(8,128)(2,1)S(1)}, u32[]{:S(2)}, u32[]{:S(2)}) collective-permute-start(bf16[4,8,16,128]{3,2,1,0:T(8,128)(2,1)S(1)} %bitcast.618), channel_id=1, source_target_pairs={{64,0},{128,64},{192,128},{65,1},{129,65},{193,129},{66,2},{130,66... | collective-permute-start | bytes 393224 | tf_op jit(solution)/shard_map/ppermute | solution.py:10
  182.1 7.9 %collective-permute-start.33 = (bf16[6,1,16,128]{3,2,1,0:T(8,128)(2,1)S(1)}, bf16[6,1,16,128]{3,2,1,0:T(8,128)(2,1)S(1)}, u32[]{:S(2)}, u32[]{:S(2)}) collective-permute-start(bf16[6,1,16,128]{3,2,1,0:T(8,128)(2,1)S(1)} %get-tuple-element.185), channel_id=1, source_target_pairs={{1,0},{2,1},{3,2},{4,3},{5,4},{6,5},{7,6},{8,7},{9,8},{10,9},{11,1... | collective-permute-start | bytes 73736 | tf_op jit(solution)/shard_map/ppermute | solution.py:21
  183.4 7.3 %collective-permute-start.32 = (bf16[6,1,16,128]{3,2,1,0:T(8,128)(2,1)S(1)}, bf16[6,1,16,128]{3,2,1,0:T(8,128)(2,1)S(1)}, u32[]{:S(2)}, u32[]{:S(2)}) collective-permute-start(bf16[6,1,16,128]{3,2,1,0:T(8,128)(2,1)S(1)} %get-tuple-element.184), channel_id=1, source_target_pairs={{0,1},{1,2},{2,3},{3,4},{4,5},{5,6},{6,7},{7,8},{8,9},{9,10},{10,1... | collective-permute-start | bytes 73736 | tf_op jit(solution)/shard_map/ppermute | solution.py:20
  205.7 8.0 %collective-permute-start.37 = (bf16[6,1,16,128]{3,2,1,0:T(8,128)(2,1)S(1)}, bf16[6,1,16,128]{3,2,1,0:T(8,128)(2,1)S(1)}, u32[]{:S(2)}, u32[]{:S(2)}) collective-permute-start(bf16[6,1,16,128]{3,2,1,0:T(8,128)(2,1)S(1)} %get-tuple-element.179), channel_id=1, source_target_pairs={{1,0},{2,1},{3,2},{4,3},{5,4},{6,5},{7,6},{8,7},{9,8},{10,9},{11,1... | collective-permute-start | bytes 73736 | tf_op jit(solution)/shard_map/ppermute | solution.py:21
  206.9 7.6 %collective-permute-start.36 = (bf16[6,1,16,128]{3,2,1,0:T(8,128)(2,1)S(1)}, bf16[6,1,16,128]{3,2,1,0:T(8,128)(2,1)S(1)}, u32[]{:S(2)}, u32[]{:S(2)}) collective-permute-start(bf16[6,1,16,128]{3,2,1,0:T(8,128)(2,1)S(1)} %get-tuple-element.178), channel_id=1, source_target_pairs={{0,1},{1,2},{2,3},{3,4},{4,5},{5,6},{6,7},{7,8},{8,9},{9,10},{10,1... | collective-permute-start | bytes 73736 | tf_op jit(solution)/shard_map/ppermute | solution.py:20
  229.5 8.0 %collective-permute-start.41 = (bf16[6,1,16,128]{3,2,1,0:T(8,128)(2,1)S(1)}, bf16[6,1,16,128]{3,2,1,0:T(8,128)(2,1)S(1)}, u32[]{:S(2)}, u32[]{:S(2)}) collective-permute-start(bf16[6,1,16,128]{3,2,1,0:T(8,128)(2,1)S(1)} %get-tuple-element.173), channel_id=1, source_target_pairs={{1,0},{2,1},{3,2},{4,3},{5,4},{6,5},{7,6},{8,7},{9,8},{10,9},{11,1... | collective-permute-start | bytes 73736 | tf_op jit(solution)/shard_map/ppermute | solution.py:21
  230.8 7.6 %collective-permute-start.40 = (bf16[6,1,16,128]{3,2,1,0:T(8,128)(2,1)S(1)}, bf16[6,1,16,128]{3,2,1,0:T(8,128)(2,1)S(1)}, u32[]{:S(2)}, u32[]{:S(2)}) collective-permute-start(bf16[6,1,16,128]{3,2,1,0:T(8,128)(2,1)S(1)} %get-tuple-element.172), channel_id=1, source_target_pairs={{0,1},{1,2},{2,3},{3,4},{4,5},{5,6},{6,7},{7,8},{8,9},{9,10},{10,1... | collective-permute-start | bytes 73736 | tf_op jit(solution)/shard_map/ppermute | solution.py:20
  253.9 8.0 %collective-permute-start.45 = (bf16[6,1,16,128]{3,2,1,0:T(8,128)(2,1)S(1)}, bf16[6,1,16,128]{3,2,1,0:T(8,128)(2,1)S(1)}, u32[]{:S(2)}, u32[]{:S(2)}) collective-permute-start(bf16[6,1,16,128]{3,2,1,0:T(8,128)(2,1)S(1)} %get-tuple-element.167), channel_id=1, source_target_pairs={{1,0},{2,1},{3,2},{4,3},{5,4},{6,5},{7,6},{8,7},{9,8},{10,9},{11,1... | collective-permute-start | bytes 73736 | tf_op jit(solution)/shard_map/ppermute | solution.py:21
  255.2 7.5 %collective-permute-start.44 = (bf16[6,1,16,128]{3,2,1,0:T(8,128)(2,1)S(1)}, bf16[6,1,16,128]{3,2,1,0:T(8,128)(2,1)S(1)}, u32[]{:S(2)}, u32[]{:S(2)}) collective-permute-start(bf16[6,1,16,128]{3,2,1,0:T(8,128)(2,1)S(1)} %get-tuple-element.166), channel_id=1, source_target_pairs={{0,1},{1,2},{2,3},{3,4},{4,5},{5,6},{6,7},{7,8},{8,9},{9,10},{10,1... | collective-permute-start | bytes 73736 | tf_op jit(solution)/shard_map/ppermute | solution.py:20
  265.7 6.2 %collective-permute-start.46 = (bf16[4,8,16,128]{3,2,1,0:T(8,128)(2,1)S(1)}, bf16[4,8,16,128]{3,2,1,0:T(8,128)(2,1)S(1)}, u32[]{:S(2)}, u32[]{:S(2)}) collective-permute-start(bf16[4,8,16,128]{3,2,1,0:T(8,128)(2,1)S(1)} %bitcast.617), channel_id=1, source_target_pairs={{64,0},{128,64},{192,128},{65,1},{129,65},{193,129},{66,2},{130,66... | collective-permute-start | bytes 393224 | tf_op jit(solution)/shard_map/ppermute | solution.py:10
  277.7 8.0 %collective-permute-start.49 = (bf16[6,1,16,128]{3,2,1,0:T(8,128)(2,1)S(1)}, bf16[6,1,16,128]{3,2,1,0:T(8,128)(2,1)S(1)}, u32[]{:S(2)}, u32[]{:S(2)}) collective-permute-start(bf16[6,1,16,128]{3,2,1,0:T(8,128)(2,1)S(1)} %get-tuple-element.161), channel_id=1, source_target_pairs={{1,0},{2,1},{3,2},{4,3},{5,4},{6,5},{7,6},{8,7},{9,8},{10,9},{11,1... | collective-permute-start | bytes 73736 | tf_op jit(solution)/shard_map/ppermute | solution.py:21
  279.0 7.6 %collective-permute-start.48 = (bf16[6,1,16,128]{3,2,1,0:T(8,128)(2,1)S(1)}, bf16[6,1,16,128]{3,2,1,0:T(8,128)(2,1)S(1)}, u32[]{:S(2)}, u32[]{:S(2)}) collective-permute-start(bf16[6,1,16,128]{3,2,1,0:T(8,128)(2,1)S(1)} %get-tuple-element.160), channel_id=1, source_target_pairs={{0,1},{1,2},{2,3},{3,4},{4,5},{5,6},{6,7},{7,8},{8,9},{9,10},{10,1... | collective-permute-start | bytes 73736 | tf_op jit(solution)/shard_map/ppermute | solution.py:20
  (33 other events, 165.3 us)
Sparse Core Ops, SparseCore 0:
  302.9 214.4 all-reduce.14
where the time goes:
time: 537 us; the launch traced here: 528 us
  waiting for transfers between devices  280 us (52%)
  starting transfers between devices  156 us (29%)
  matrix products  34.8 us (6%)
  local copies, waits for them, and re-layouts  30.1 us (6%)
  between operations  18.5 us (3%)
  other arithmetic  7.69 us (1%)
    psum x1, waiting for transfers between devices, body(): return lax.psum(own_grad, ('tm', 'space'))  215 us
    ppermute x13, starting transfers between devices, with_halo(): before = lax.ppermute(last, axis, up)  77.5 us
    ppermute x25, starting transfers between devices, from_behind(): return lax.ppermute(array, axis, pairs)  61.8 us
    ppermute x25, waiting for transfers between devices, from_behind(): return lax.ppermute(array, axis, pairs)  55.6 us
    unnamed x489, local copies, waits for them, and re-layouts  23.7 us
    ppermute x13, starting transfers between devices, with_halo(): after = lax.ppermute(leading, axis, down)  16.7 us
    dot_general x7, matrix products, layer_backward(): lax.dot_general(patches, delta_z, (((0,), (0,)), ((), ())), preferred_ele...  14.8 us
  transfers between devices with their start and end apart: 52, of which 35 were waited for; matrix products, arithmetic and copies ran while one was open for 4% of the time, Pallas kernels for 0%

commit v1 on v0

v1 whole, which is shorter than its diff:
```python
import functools

import jax
import jax.numpy as jnp
from jax import lax
from jax.experimental import pallas as pl
from jax.experimental.pallas import tpu as pltpu
from jax.sharding import Mesh
from jax.sharding import PartitionSpec as P

BF16 = jnp.bfloat16
F32 = jnp.float32
CH = 128
COLS = 16
FR = 8
LAYERS = 4
TAPS = 27
KC = TAPS * CH
HALF = KC // 2
PLANE = 9 * CH
OWN = 4
HALO = 7
CHALO = 3
HID = FR * (OWN + 2) * COLS
PART = HID + FR * OWN * COLS


def shifted(x):
    cells = x.shape[0]
    col = lax.broadcasted_iota(jnp.int32, x.shape, 0) % COLS
    before = jnp.where(col == 0, 0.0, pltpu.roll(x, 1, 0))
    after = jnp.where(col == COLS - 1, 0.0, pltpu.roll(x, cells - 1, 0))
    return before.astype(BF16), x.astype(BF16), after.astype(BF16)


def spread(src, im, rows):
    cells = rows * COLS

    @pl.loop(0, FR)
    def _(t):
        for lag_c, v in enumerate(shifted(src[t, : cells + 2 * COLS])):
            for lag_r in range(3):
                at = pl.multiple_of((t + 2) * PLANE + (lag_r * 3 + lag_c) * CH, CH)
                im[:cells, pl.ds(at, CH)] = v[lag_r * COLS : lag_r * COLS + cells]


def inside(first, rows, total):
    row = first + lax.broadcasted_iota(jnp.int32, (rows * COLS, CH), 0) // COLS
    return (row >= 0) & (row < total)


def layers_kernel(
    total, pos, mine, other, w0, r1, r2, r3, q1, q2, q3, o0, o1, o2, o3, wt, wb, im, hid, fac, grad, dz, part
):
    seg, tm, first = pos[0], pos[1], pos[2]
    zero = jnp.zeros((PLANE, CH), BF16)
    for l in range(LAYERS):
        wt[l, KC:, :CH] = zero
        wt[l, :PLANE, CH:] = zero
    wb[KC:, :CH] = zero
    wb[:PLANE, CH:] = zero
    cells = im.shape[0]
    im[:, : 2 * PLANE] = jnp.zeros((cells, 2 * PLANE), BF16)
    im[:, (FR + 2) * PLANE :] = jnp.zeros((cells, 2 * PLANE), BF16)
    own = w0[...]
    wt[seg, :KC, :CH] = own
    wt[seg, PLANE:, CH:] = own
    for d, (r, q) in enumerate(((r1, q1), (r2, q2), (r3, q3)), 1):
        l = lax.rem(seg + LAYERS - d, LAYERS)
        for ref, half in ((r, tm), (q, 1 - tm)):
            at = pl.multiple_of(half * HALF, CH // 2)
            wt[l, pl.ds(at, HALF), :CH] = ref[...]
            wt[l, pl.ds(PLANE + at, HALF), CH:] = ref[...]

    span = OWN + 2 * HALO
    half_fr = FR // 2
    for ref, which in ((mine, tm), (other, 1 - tm)):

        @pl.loop(0, half_fr)
        def _(t):
            rows = ref[t, pl.ds(tm * OWN, span)]
            hid[0, which * half_fr + t, : span * COLS] = rows.reshape(span * COLS, CH).astype(F32)
            at = 2 * HALO + 2 * OWN + tm * OWN
            rows = ref[t, pl.ds(at, OWN + 2 * CHALO)]
            grad[which * half_fr + t] = rows.reshape(-1, CH).astype(F32)

    for l in range(LAYERS):
        rows = span - 2 * (l + 1)
        cells = rows * COLS
        spread(hid.at[l], im, rows)
        keep = slice((6 - 2 * l) * COLS, 10 * COLS)
        kept = (OWN + 2 * l) * COLS

        @pl.loop(0, FR // 2)
        def _(p):
            at = pl.multiple_of(2 * p * PLANE, CH)
            pre2 = jnp.dot(im[:cells, pl.ds(at, 4 * PLANE)], wt[l], preferred_element_type=F32)
            valid = inside(first - HALO + l + 1, rows, total)
            for e in range(2):
                t = 2 * p + e
                pre = pre2[:, e * CH : (e + 1) * CH]
                s = jax.nn.sigmoid(pre)
                if l + 1 < LAYERS:
                    new = hid[l, t, COLS : COLS + cells] + pre * s
                    new = new.astype(BF16).astype(F32)
                    hid[l + 1, t, :cells] = jnp.where(valid, new, 0.0)
                s, pre = s[keep], pre[keep]
                fac[l, t, :kept] = s * (1.0 + pre * (1.0 - s))

    for l in reversed(range(LAYERS)):
        rows = OWN + 2 * l
        cells = rows * COLS
        width = (OWN + 2) * COLS
        own_cells = OWN * COLS

        @pl.loop(0, FR)
        def _(t):
            valid = inside(first - l, rows, total)
            delta = jnp.where(valid, grad[t, :cells] * fac[l, t, :cells], 0.0).astype(BF16)
            at = pl.multiple_of(HID + t * own_cells, own_cells)
            part[l, pl.ds(at, own_cells)] = delta[l * COLS : l * COLS + own_cells]
            at = pl.multiple_of(t * width, width)
            part[l, pl.ds(at, width)] = hid[l, t, (6 - l) * COLS : (6 - l) * COLS + width].astype(
                BF16
            )
            if l > 0:
                dz[t, :cells] = delta.astype(F32)

        if l > 0:
            inner = cells - 2 * COLS
            spread(dz, im, rows - 2)

            @pl.loop(0, TAPS)
            def _(k):
                at = pl.multiple_of((TAPS - 1 - k) * CH, CH)
                block = wt[l, pl.ds(at, CH), :CH].T
                at = pl.multiple_of(k * CH, CH)
                wb[pl.ds(at, CH), :CH] = block
                wb[pl.ds(PLANE + at, CH), CH:] = block

            @pl.loop(0, FR // 2)
            def _(p):
                at = pl.multiple_of((2 * p + 2) * PLANE, CH)
                adjoint = jnp.dot(
                    im[:inner, pl.ds(at, 4 * PLANE)], wb[...], preferred_element_type=F32
                )
                for e in range(2):
                    t = 2 * p + e
                    new = grad[t, COLS : COLS + inner] + adjoint[:, e * CH : (e + 1) * CH]
                    grad[t, :inner] = new.astype(BF16).astype(F32)

    for d, out in enumerate((o0, o1, o2, o3)):
        out[...] = part[lax.rem(seg + d, LAYERS)]


def kernel_grad_kernel(pos, e0, e1, e2, e3, keep, send, x9, d3, wg):
    tm = pos[1]
    cells = OWN * COLS
    width = cells + 2 * COLS
    nothing = jnp.zeros((cells, CH), BF16)
    for m, e in enumerate((e0, e1, e2, e3)):
        for t in range(FR):
            at = (m * FR + t) * cells
            frame = e[t * width : (t + 1) * width].astype(F32)
            for lag_c, v in enumerate(shifted(frame)):
                for lag_r in range(3):
                    tap = (lag_r * 3 + lag_c) * CH
                    x9[at : at + cells, tap : tap + CH] = v[lag_r * COLS : lag_r * COLS + cells]
            for lag_t in range(3):
                src = t + 2 - lag_t
                row = HID + src * cells
                d3[at : at + cells, lag_t * CH : (lag_t + 1) * CH] = (
                    e[row : row + cells] if src < FR else nothing
                )
    out = lax.dot_general(
        d3[...], x9[...], (((0,), (0,)), ((), ())), preferred_element_type=F32
    )
    for lag_t in range(3):
        for tap in range(9):
            at = (lag_t * 9 + tap) * CH
            wg[at : at + CH] = out[lag_t * CH : (lag_t + 1) * CH, tap * CH : (tap + 1) * CH].T
    keep[...] = wg[pl.ds(pl.multiple_of(tm * HALF, CH // 2), HALF)]
    send[...] = wg[pl.ds(pl.multiple_of((1 - tm) * HALF, CH // 2), HALF)].astype(BF16)


def in_vmem(n):
    return [pl.BlockSpec(memory_space=pltpu.SMEM)] + [pl.BlockSpec(memory_space=pltpu.VMEM)] * n


def run_layers(total, pos, *arrays):
    span = OWN + 2 * HALO
    out = jax.ShapeDtypeStruct((PART, CH), BF16)
    return pl.pallas_call(
        functools.partial(layers_kernel, total),
        out_shape=(out,) * LAYERS,
        in_specs=in_vmem(len(arrays)),
        out_specs=(pl.BlockSpec(memory_space=pltpu.VMEM),) * LAYERS,
        scratch_shapes=[
            pltpu.VMEM((LAYERS, 4 * PLANE, 2 * CH), BF16),
            pltpu.VMEM((4 * PLANE, 2 * CH), BF16),
            pltpu.VMEM(((span - 2) * COLS, (FR + 4) * PLANE), BF16),
            pltpu.VMEM((LAYERS, FR, span * COLS, CH), F32),
            pltpu.VMEM((LAYERS, FR, (OWN + 2 * CHALO) * COLS, CH), F32),
            pltpu.VMEM((FR, (OWN + 2 * CHALO) * COLS, CH), F32),
            pltpu.VMEM((FR, (OWN + 2 * CHALO) * COLS, CH), F32),
            pltpu.VMEM((LAYERS, PART, CH), BF16),
        ],
        compiler_params=pltpu.CompilerParams(vmem_limit_bytes=44 * 2**20),
        cost_estimate=pl.CostEstimate(
            flops=9_000_000_000, bytes_accessed=6_000_000, transcendentals=1_000_000
        ),
        name="layers",
    )(pos, *arrays)


def run_kernel_grad(pos, *arrays):
    cells = LAYERS * FR * OWN * COLS
    return pl.pallas_call(
        kernel_grad_kernel,
        out_shape=(
            jax.ShapeDtypeStruct((HALF, CH), F32),
            jax.ShapeDtypeStruct((HALF, CH), BF16),
        ),
        in_specs=in_vmem(len(arrays)),
        out_specs=(pl.BlockSpec(memory_space=pltpu.VMEM),) * 2,
        scratch_shapes=[
            pltpu.VMEM((cells, PLANE), BF16),
            pltpu.VMEM((cells, 3 * CH), BF16),
            pltpu.VMEM((KC, CH), F32),
        ],
        compiler_params=pltpu.CompilerParams(vmem_limit_bytes=32 * 2**20),
        cost_estimate=pl.CostEstimate(
            flops=1_800_000_000, bytes_accessed=4_000_000, transcendentals=0
        ),
        name="kernel_grad",
    )(pos, *arrays)


def ring(count, by):
    return [(i, (i + by) % count) for i in range(count)]


def swap(x):
    return lax.ppermute(x, "tm", [(0, 1), (1, 0)])


def body(inputs, weights, cotangent):
    seg, tm = lax.axis_index("segment"), lax.axis_index("tm")
    space = lax.axis_index(("z", "y"))
    spaces = lax.axis_size(("z", "y"))
    ny, nz = lax.axis_size("y"), lax.axis_size("z")
    rows = inputs.shape[2]
    pos = jnp.stack([seg, tm, space * rows + tm * OWN]).astype(jnp.int32)

    w = weights[0]
    half = lax.dynamic_slice_in_dim(w, tm * HALF, HALF, 0)
    got = [lax.ppermute(half, "segment", ring(LAYERS, d)) for d in (1, 2, 3)]
    crossed = [swap(g) for g in got]

    x = lax.dynamic_index_in_dim(inputs, seg, 0, keepdims=False)
    c = lax.dynamic_index_in_dim(cotangent, seg, 0, keepdims=False)
    down = [(i, i + 1) for i in range(spaces - 1)]
    up = [(i + 1, i) for i in range(spaces - 1)]
    before = lax.ppermute(
        jnp.concatenate([x[:, rows - HALO :], c[:, rows - CHALO :]], 1), ("z", "y"), down
    )
    after = lax.ppermute(jnp.concatenate([x[:, :HALO], c[:, :CHALO]], 1), ("z", "y"), up)
    mine = jnp.concatenate(
        [before[:, :HALO], x, after[:, :HALO], before[:, HALO:], c, after[:, HALO:]], 1
    )
    other = swap(mine)

    parts = run_layers(spaces * rows, pos, mine, other, w, *got, *crossed)
    moved = [lax.ppermute(parts[d], "segment", ring(LAYERS, d)) for d in (1, 2, 3)]
    keep, send = run_kernel_grad(pos, parts[0], *moved)

    total = (keep + swap(send).astype(F32)).astype(BF16)
    rows_y = HALF // ny
    pieces = lax.all_to_all(total.reshape(ny, rows_y, CH), "y", 0, 0)
    total = jnp.sum(pieces.astype(F32), 0).astype(BF16)
    rows_z = -(-rows_y // (16 * nz)) * 16
    total = jnp.pad(total, ((0, nz * rows_z - rows_y), (0, 0)))
    pieces = lax.all_to_all(total.reshape(nz, rows_z, CH), "z", 0, 0)
    total = jnp.sum(pieces.astype(F32), 0).astype(BF16)
    whole = lax.all_to_all(jnp.broadcast_to(total, (nz, rows_z, CH)), "z", 0, 0)
    whole = whole.reshape(nz * rows_z, CH)[:rows_y]
    whole = lax.all_to_all(jnp.broadcast_to(whole, (ny, rows_y, CH)), "y", 0, 0)
    whole = whole.reshape(HALF, CH)
    theirs = swap(whole)
    low = jnp.where(tm == 0, whole, theirs)
    high = jnp.where(tm == 0, theirs, whole)
    return jnp.concatenate([low, high], 0).astype(F32)[None]


def solution(mesh):
    segments, cores, spaces = mesh.devices.shape
    ny = 4 if spaces % 4 == 0 else 1
    fine = Mesh(
        mesh.devices.reshape(segments, cores, spaces // ny, ny), ("segment", "tm", "z", "y")
    )
    spec = P(None, "tm", ("z", "y"), None, None)
    return jax.shard_map(
        body,
        mesh=fine,
        in_specs=(spec, P("segment", None, None), spec),
        out_specs=P("segment", None, None),
        check_vma=False,
    )
```

time: 537 us -> 144 us (0.27); the launches traced: 528 us -> 143 us
  waiting for transfers between devices: 280 us -> 27.3 us
  starting transfers between devices: 156 us -> 31.3 us
  blocking collectives: 0 us -> 46.8 us
  matrix products: 34.8 us -> 0 us
  Pallas kernels: 0 us -> 34.6 us
  local copies, waits for them, and re-layouts: 30.1 us -> 1.33 us
  between operations: 18.5 us -> 0.2 us
  other arithmetic: 7.69 us -> 1.73 us
    psum x1 -> x0, waiting for transfers between devices: 215 us -> none  [body(): return lax.psum(own_grad, ('tm', 'space'))]
    ppermute x51 -> x14, starting transfers between devices: 156 us -> 31.3 us  [the longest x6 19.6 us: swap(): return lax.ppermute(x, 'tm', [(0, 1), (1, 0)])]
    all_to_all x0 -> x4, blocking collectives: none -> 46.8 us  [the longest x1 15.8 us: body(): pieces = lax.all_to_all(total.reshape(nz, rows_z, CH), 'z', 0, 0)]
    ppermute x51 -> x14, waiting for transfers between devices: 65.8 us -> 27.3 us  [the longest x3 14.8 us: body(): lax.ppermute(parts[d], 'segment', ring(LAYERS, d))]
    dot_general x25 -> x0, matrix products: 34.8 us -> none  [the longest x7 14.8 us: layer_backward(): lax.dot_general(patches, delta_z, (((0,), (0,)), ((), ())), preferred_ele...]
    pallas_call x0 -> x2, Pallas kernels: none -> 34.6 us  [the longest x1 31.1 us: run_layers(): pl.pallas_call(functools.partial(layers_kernel, total), out_shape=(out,)...]
    unnamed x489 -> x7, local copies, waits for them, and re-layouts: 23.7 us -> 0.08 us
  transfers between devices with their start and end apart: 52 -> 14, of which waited for: 35 -> 8; matrix products, arithmetic and copies ran while one was open for 4% -> 0% of each run, Pallas kernels for 0% -> 0%
where the time goes in v1:
time: 144 us; the launch traced here: 143 us
  blocking collectives  46.8 us (32%)
  Pallas kernels  34.6 us (24%)
  starting transfers between devices  31.3 us (22%)
  waiting for transfers between devices  27.3 us (19%)
  other arithmetic  1.73 us (1%)
    pallas_call x1, Pallas kernels, run_layers(): pl.pallas_call(functools.partial(layers_kernel, total), out_shape=(out,)...  31.1 us
    ppermute x6, starting transfers between devices, swap(): return lax.ppermute(x, 'tm', [(0, 1), (1, 0)])  19.6 us
    all_to_all x1, blocking collectives, body(): pieces = lax.all_to_all(total.reshape(nz, rows_z, CH), 'z', 0, 0)  15.8 us
    ppermute x3, waiting for transfers between devices, body(): lax.ppermute(parts[d], 'segment', ring(LAYERS, d))  14.8 us
    all_to_all x1, blocking collectives, body(): pieces = lax.all_to_all(total.reshape(ny, rows_y, CH), 'y', 0, 0)  11.8 us
    all_to_all x1, blocking collectives, body(): whole = lax.all_to_all(jnp.broadcast_to(total, (nz, rows_z, CH)), 'z', 0, 0)  10.3 us
    all_to_all x1, blocking collectives, body(): whole = lax.all_to_all(jnp.broadcast_to(whole, (ny, rows_y, CH)), 'y', 0, 0)  8.87 us
    ppermute x1, waiting for transfers between devices, body(): lax.ppermute(jnp.concatenate([x[:, :HALO], c[:, :CHALO]], 1), ('z', 'y'),...  5 us
  transfers between devices with their start and end apart: 14, of which 8 were waited for; matrix products, arithmetic and copies ran while one was open for 0% of the time, Pallas kernels for 0%

profile of v1, /device:TPU:1, one launch (start us, length us, event | category | flops | bytes accessed | tf_op | source)
XLA Modules:
  0.0 143.4 jit_solution(5997274375383527531)
XLA Ops:
  0.0 1.1 dynamic-slice_bitcast_fusion.1
  1.2 4.0 %collective-permute-start = (bf16[4,10,16,128]{3,2,1,0:T(8,128)(2,1)S(1)}, bf16[4,10,16,128]{3,2,1,0:T(8,128)(2,1)S(1)}, u32[]{:S(2)}, u32[]{:S(2)}) collective-permute-start(bf16[4,10,16,128]{3,2,1,0:T(8,128)(2,1)S(1)} %pad_maximum_fusion), channel_id=1, source_target_pairs={{0,1},{1,2},{2,3},{3,4},{4,5},{5,6},{6,7},{7,8},{8,9},{9,10},{10,1... | collective-permute-start | bytes 491528 | tf_op jit(solution)/shard_map/ppermute | solution.py:264
  5.3 2.6 %collective-permute-start.5 = (bf16[1728,128]{1,0:T(8,128)(2,1)S(1)}, bf16[1728,128]{1,0:T(8,128)(2,1)S(1)}, u32[]{:S(2)}, u32[]{:S(2)}) collective-permute-start(bf16[1728,128]{1,0:T(8,128)(2,1)S(1)} %dynamic-slice_bitcast_fusion), channel_id=1, source_target_pairs={{0,192},{64,0},{128,64},{192,128},{1,193},{65,1},{129,65},{193,129... | collective-permute-start | bytes 1327112 | tf_op jit(solution)/shard_map/ppermute | solution.py:257
  9.0 1.3 collective-permute-start.1
  10.3 5.0 %collective-permute-done.1 = bf16[4,10,16,128]{3,2,1,0:T(8,128)(2,1)S(1)} collective-permute-done((bf16[4,10,16,128]{3,2,1,0:T(8,128)(2,1)S(1)}, bf16[4,10,16,128]{3,2,1,0:T(8,128)(2,1)S(1)}, u32[]{:S(2)}, u32[]{:S(2)}) %collective-permute-start.1) | collective-permute-done | bytes 163872 | tf_op jit(solution)/shard_map/ppermute | solution.py:267
  15.4 2.7 %collective-permute-start.2 = (bf16[4,36,16,128]{3,2,1,0:T(8,128)(2,1)S(1)}, bf16[4,36,16,128]{3,2,1,0:T(8,128)(2,1)S(1)}, u32[]{:S(2)}, u32[]{:S(2)}) collective-permute-start(bf16[4,36,16,128]{3,2,1,0:T(8,128)(2,1)S(1)} %slice_dynamic-update-slice_fusion.2.mine), channel_id=1, source_target_pairs={{0,32},{32,0},{1,33},{33,1},{2,34},{34,2},{3,35},{35,3},{4,36},{36... | collective-permute-start | bytes 1769480 | tf_op jit(solution)/shard_map/ppermute | solution.py:244
  18.1 9.6 %collective-permute-start.8 = (bf16[1728,128]{1,0:T(8,128)(2,1)S(1)}, bf16[1728,128]{1,0:T(8,128)(2,1)}, u32[]{:S(2)}, u32[]{:S(2)}) collective-permute-start(bf16[1728,128]{1,0:T(8,128)(2,1)S(1)} %collective-permute-done.5.r3), channel_id=1, source_target_pairs={{0,32},{32,0},{1,33},{33,1},{2,34},{34,2},{3,35},{35,3},{4,36},{36... | collective-permute-start | bytes 1327112 | tf_op jit(solution)/shard_map/ppermute | solution.py:244
  27.7 3.2 %collective-permute-done.3.r1 = bf16[1728,128]{1,0:T(8,128)(2,1)S(1)} collective-permute-done((bf16[1728,128]{1,0:T(8,128)(2,1)S(1)}, bf16[1728,128]{1,0:T(8,128)(2,1)S(1)}, u32[]{:S(2)}, u32[]{:S(2)}) %collective-permute-start.3) | collective-permute-done | bytes 442400 | tf_op jit(solution)/shard_map/ppermute | solution.py:257
  31.5 1.5 %collective-permute-done.6.q1 = bf16[1728,128]{1,0:T(8,128)(2,1)} collective-permute-done((bf16[1728,128]{1,0:T(8,128)(2,1)S(1)}, bf16[1728,128]{1,0:T(8,128)(2,1)}, u32[]{:S(2)}, u32[]{:S(2)}) %collective-permute-start.6) | collective-permute-done | bytes 442400 | tf_op jit(solution)/shard_map/ppermute | solution.py:244
  32.9 31.1 %layers.1 = (bf16[1280,128]{1,0:T(8,128)(2,1)S(1)}, bf16[1280,128]{1,0:T(8,128)(2,1)S(1)}, bf16[1280,128]{1,0:T(8,128)(2,1)S(1)}, bf16[1280,128]{1,0:T(8,128)(2,1)S(1)}) custom-call(s32[3]{0:T(128)S(1)} %pad_add_fusion.pos, bf16[4,36,16,128]{3,2,1,0:T(8,128)(2,1)S(1)} %slice_dynamic-update-slice_fusion.2.mine, ...), custom_call_target="tpu_custom_call" | custom-call | flops 8999999488 | bytes 6000000 | tf_op jit(solution)/shard_map/layers/pallas_call | solution.py:193
  64.2 2.1 %collective-permute-start.10 = (bf16[1280,128]{1,0:T(8,128)(2,1)S(1)}, bf16[1280,128]{1,0:T(8,128)(2,1)S(1)}, u32[]{:S(2)}, u32[]{:S(2)}) collective-permute-start(bf16[1280,128]{1,0:T(8,128)(2,1)S(1)} %get-tuple-element.13), channel_id=1, source_target_pairs={{0,128},{64,192},{128,0},{192,64},{1,129},{65,193},{129,1},{193,65... | collective-permute-start | bytes 983048 | tf_op jit(solution)/shard_map/ppermute | solution.py:274
  66.8 8.0 %collective-permute-done.9.e1 = bf16[1280,128]{1,0:T(8,128)(2,1)S(1)} collective-permute-done((bf16[1280,128]{1,0:T(8,128)(2,1)S(1)}, bf16[1280,128]{1,0:T(8,128)(2,1)S(1)}, u32[]{:S(2)}, u32[]{:S(2)}) %collective-permute-start.9) | collective-permute-done | bytes 327712 | tf_op jit(solution)/shard_map/ppermute | solution.py:274
  74.8 6.0 %collective-permute-done.10.e2 = bf16[1280,128]{1,0:T(8,128)(2,1)S(1)} collective-permute-done((bf16[1280,128]{1,0:T(8,128)(2,1)S(1)}, bf16[1280,128]{1,0:T(8,128)(2,1)S(1)}, u32[]{:S(2)}, u32[]{:S(2)}) %collective-permute-start.10) | collective-permute-done | bytes 327712 | tf_op jit(solution)/shard_map/ppermute | solution.py:274
  80.8 0.8 collective-permute-done.11.e3
  81.7 3.5 %kernel_grad.1 = (f32[1728,128]{1,0:T(8,128)S(1)}, bf16[1728,128]{1,0:T(8,128)(2,1)S(1)}) custom-call(s32[3]{0:T(128)S(1)} %pad_add_fusion.pos, bf16[1280,128]{1,0:T(8,128)(2,1)S(1)} %get-tuple-element.11.e0, bf16[1280,128]{1,0:T(8,128)(2,1)S(1)} %collective-permute-done.9.e1, bf16[1280,128]{1,0:T(8,128)(2,1)S(1)} %collective-permute-done.10.e2, ...), custom_call_target="tpu_custom_call" | custom-call | flops 1800000000 | bytes 4000000 | tf_op jit(solution)/shard_map/kernel_grad/pallas_call | solution.py:218
  85.2 1.6 %collective-permute-start.12 = (bf16[1728,128]{1,0:T(8,128)(2,1)S(1)}, bf16[1728,128]{1,0:T(8,128)(2,1)S(1)}, u32[]{:S(2)}, u32[]{:S(2)}) collective-permute-start(bf16[1728,128]{1,0:T(8,128)(2,1)S(1)} %get-tuple-element.16), channel_id=1, source_target_pairs={{0,32},{32,0},{1,33},{33,1},{2,34},{34,2},{3,35},{35,3},{4,36},{36... | collective-permute-start | bytes 1327112 | tf_op jit(solution)/shard_map/ppermute | solution.py:244
  86.7 1.4 collective-permute-done.12
  88.3 11.8 %all_to_all.20 = bf16[4,432,128]{2,1,0:T(8,128)(2,1)S(1)} all-to-all(bf16[4,432,128]{2,1,0:T(8,128)(2,1)S(1)} %bitcast.21), channel_id=1, replica_groups=mesh['segment'=4,'tm'=2,'z'=8,'y'=4] {'y'}, dimensions={0} | all-to-all | bytes 884736 | tf_op jit(solution)/shard_map/all_to_all | solution.py:279
  100.2 15.8 %all_to_all.21 = bf16[8,64,128]{2,1,0:T(8,128)(2,1)S(1)} all-to-all(bf16[8,64,128]{2,1,0:T(8,128)(2,1)S(1)} %bitcast.23), channel_id=1, replica_groups=mesh['segment'=4,'tm'=2,'z'=8,'y'=4] {'z'}, dimensions={0} | all-to-all | bytes 262144 | tf_op jit(solution)/shard_map/all_to_all | solution.py:283
  116.1 10.3 %all_to_all.22 = bf16[8,64,128]{2,1,0:T(8,128)(2,1)S(1)} all-to-all(bf16[8,64,128]{2,1,0:T(8,128)(2,1)S(1)} %broadcast_in_dim.7), channel_id=1, replica_groups=mesh['segment'=4,'tm'=2,'z'=8,'y'=4] {'z'}, dimensions={0} | all-to-all | bytes 262144 | tf_op jit(solution)/shard_map/all_to_all | solution.py:285
  126.5 8.9 %all_to_all.23 = bf16[4,432,128]{2,1,0:T(8,128)(2,1)S(1)} all-to-all(bf16[4,432,128]{2,1,0:T(8,128)(2,1)S(1)} %broadcast_in_dim.8), channel_id=1, replica_groups=mesh['segment'=4,'tm'=2,'z'=8,'y'=4] {'y'}, dimensions={0} | all-to-all | bytes 884736 | tf_op jit(solution)/shard_map/all_to_all | solution.py:287
  135.3 5.2 %collective-permute-start.13 = (bf16[1728,128]{1,0:T(8,128)(2,1)S(1)}, bf16[1728,128]{1,0:T(8,128)(2,1)S(1)}, u32[]{:S(2)}, u32[]{:S(2)}) collective-permute-start(bf16[1728,128]{1,0:T(8,128)(2,1)S(1)} %bitcast.22), channel_id=1, source_target_pairs={{0,32},{32,0},{1,33},{33,1},{2,34},{34,2},{3,35},{35,3},{4,36},{36... | collective-permute-start | bytes 1327112 | tf_op jit(solution)/shard_map/ppermute | solution.py:244
  140.6 1.4 collective-permute-done.13
  142.1 1.3 maximum_convert_fusion
  (34 shorter events, 2.9 us)
Async XLA Ops:
  0.0 5.2 %copy-start = (bf16[1,3456,128]{2,1,0:T(8,128)(2,1)S(1)}, bf16[1,3456,128]{2,1,0:T(8,128)(2,1)}, u32[]{:S(2)}) copy-start(bf16[1,3456,128]{2,1,0:T(8,128)(2,1)} %param.4) | copy-start | bytes 2654212
  1.2 9.1 %collective-permute-start = (bf16[4,10,16,128]{3,2,1,0:T(8,128)(2,1)S(1)}, bf16[4,10,16,128]{3,2,1,0:T(8,128)(2,1)S(1)}, u32[]{:S(2)}, u32[]{:S(2)}) collective-permute-start(bf16[4,10,16,128]{3,2,1,0:T(8,128)(2,1)S(1)} %pad_maximum_fusion), channel_id=1, source_target_pairs={{0,1},{1,2},{2,3},{3,4},{4,5},{5,6},{6,7},{7,8},{8,9},{9,10},{10,1... | collective-permute-start | bytes 491528 | tf_op jit(solution)/shard_map/ppermute | solution.py:264
  5.3 12.9 %collective-permute-start.5 = (bf16[1728,128]{1,0:T(8,128)(2,1)S(1)}, bf16[1728,128]{1,0:T(8,128)(2,1)S(1)}, u32[]{:S(2)}, u32[]{:S(2)}) collective-permute-start(bf16[1728,128]{1,0:T(8,128)(2,1)S(1)} %dynamic-slice_bitcast_fusion), channel_id=1, source_target_pairs={{0,192},{64,0},{128,64},{192,128},{1,193},{65,1},{129,65},{193,129... | collective-permute-start | bytes 1327112 | tf_op jit(solution)/shard_map/ppermute | solution.py:257
  7.8 19.9 %collective-permute-start.4 = (bf16[1728,128]{1,0:T(8,128)(2,1)S(1)}, bf16[1728,128]{1,0:T(8,128)(2,1)S(1)}, u32[]{:S(2)}, u32[]{:S(2)}) collective-permute-start(bf16[1728,128]{1,0:T(8,128)(2,1)S(1)} %dynamic-slice_bitcast_fusion), channel_id=1, source_target_pairs={{0,128},{64,192},{128,0},{192,64},{1,129},{65,193},{129,1},{193,65... | collective-permute-start | bytes 1327112 | tf_op jit(solution)/shard_map/ppermute | solution.py:257
  8.3 22.6 %collective-permute-start.3 = (bf16[1728,128]{1,0:T(8,128)(2,1)S(1)}, bf16[1728,128]{1,0:T(8,128)(2,1)S(1)}, u32[]{:S(2)}, u32[]{:S(2)}) collective-permute-start(bf16[1728,128]{1,0:T(8,128)(2,1)S(1)} %dynamic-slice_bitcast_fusion), channel_id=1, source_target_pairs={{0,64},{64,128},{128,192},{192,0},{1,65},{65,129},{129,193},{193,1... | collective-permute-start | bytes 1327112 | tf_op jit(solution)/shard_map/ppermute | solution.py:257
  9.0 6.4 %collective-permute-start.1 = (bf16[4,10,16,128]{3,2,1,0:T(8,128)(2,1)S(1)}, bf16[4,10,16,128]{3,2,1,0:T(8,128)(2,1)S(1)}, u32[]{:S(2)}, u32[]{:S(2)}) collective-permute-start(bf16[4,10,16,128]{3,2,1,0:T(8,128)(2,1)S(1)} %pad_maximum_fusion.1), channel_id=1, source_target_pairs={{1,0},{2,1},{3,2},{4,3},{5,4},{6,5},{7,6},{8,7},{9,8},{10,9},{11,1... | collective-permute-start | bytes 491528 | tf_op jit(solution)/shard_map/ppermute | solution.py:267
  15.4 16.1 %collective-permute-start.2 = (bf16[4,36,16,128]{3,2,1,0:T(8,128)(2,1)S(1)}, bf16[4,36,16,128]{3,2,1,0:T(8,128)(2,1)S(1)}, u32[]{:S(2)}, u32[]{:S(2)}) collective-permute-start(bf16[4,36,16,128]{3,2,1,0:T(8,128)(2,1)S(1)} %slice_dynamic-update-slice_fusion.2.mine), channel_id=1, source_target_pairs={{0,32},{32,0},{1,33},{33,1},{2,34},{34,2},{3,35},{35,3},{4,36},{36... | collective-permute-start | bytes 1769480 | tf_op jit(solution)/shard_map/ppermute | solution.py:244
  18.1 13.3 %collective-permute-start.8 = (bf16[1728,128]{1,0:T(8,128)(2,1)S(1)}, bf16[1728,128]{1,0:T(8,128)(2,1)}, u32[]{:S(2)}, u32[]{:S(2)}) collective-permute-start(bf16[1728,128]{1,0:T(8,128)(2,1)S(1)} %collective-permute-done.5.r3), channel_id=1, source_target_pairs={{0,32},{32,0},{1,33},{33,1},{2,34},{34,2},{3,35},{35,3},{4,36},{36... | collective-permute-start | bytes 1327112 | tf_op jit(solution)/shard_map/ppermute | solution.py:244
  27.7 3.8 %collective-permute-start.7 = (bf16[1728,128]{1,0:T(8,128)(2,1)S(1)}, bf16[1728,128]{1,0:T(8,128)(2,1)}, u32[]{:S(2)}, u32[]{:S(2)}) collective-permute-start(bf16[1728,128]{1,0:T(8,128)(2,1)S(1)} %collective-permute-done.4.r2), channel_id=1, source_target_pairs={{0,32},{32,0},{1,33},{33,1},{2,34},{34,2},{3,35},{35,3},{4,36},{36... | collective-permute-start | bytes 1327112 | tf_op jit(solution)/shard_map/ppermute | solution.py:244
  30.9 2.0 %collective-permute-start.6 = (bf16[1728,128]{1,0:T(8,128)(2,1)S(1)}, bf16[1728,128]{1,0:T(8,128)(2,1)}, u32[]{:S(2)}, u32[]{:S(2)}) collective-permute-start(bf16[1728,128]{1,0:T(8,128)(2,1)S(1)} %collective-permute-done.3.r1), channel_id=1, source_target_pairs={{0,32},{32,0},{1,33},{33,1},{2,34},{34,2},{3,35},{35,3},{4,36},{36... | collective-permute-start | bytes 1327112 | tf_op jit(solution)/shard_map/ppermute | solution.py:244
  64.1 10.7 %collective-permute-start.9 = (bf16[1280,128]{1,0:T(8,128)(2,1)S(1)}, bf16[1280,128]{1,0:T(8,128)(2,1)S(1)}, u32[]{:S(2)}, u32[]{:S(2)}) collective-permute-start(bf16[1280,128]{1,0:T(8,128)(2,1)S(1)} %get-tuple-element.12), channel_id=1, source_target_pairs={{0,64},{64,128},{128,192},{192,0},{1,65},{65,129},{129,193},{193,1... | collective-permute-start | bytes 983048 | tf_op jit(solution)/shard_map/ppermute | solution.py:274
  64.2 16.7 %collective-permute-start.10 = (bf16[1280,128]{1,0:T(8,128)(2,1)S(1)}, bf16[1280,128]{1,0:T(8,128)(2,1)S(1)}, u32[]{:S(2)}, u32[]{:S(2)}) collective-permute-start(bf16[1280,128]{1,0:T(8,128)(2,1)S(1)} %get-tuple-element.13), channel_id=1, source_target_pairs={{0,128},{64,192},{128,0},{192,64},{1,129},{65,193},{129,1},{193,65... | collective-permute-start | bytes 983048 | tf_op jit(solution)/shard_map/ppermute | solution.py:274
  66.3 15.3 %collective-permute-start.11 = (bf16[1280,128]{1,0:T(8,128)(2,1)S(1)}, bf16[1280,128]{1,0:T(8,128)(2,1)S(1)}, u32[]{:S(2)}, u32[]{:S(2)}) collective-permute-start(bf16[1280,128]{1,0:T(8,128)(2,1)S(1)} %get-tuple-element.14), channel_id=1, source_target_pairs={{0,192},{64,0},{128,64},{192,128},{1,193},{65,1},{129,65},{193,129... | collective-permute-start | bytes 983048 | tf_op jit(solution)/shard_map/ppermute | solution.py:274
  85.2 3.0 %collective-permute-start.12 = (bf16[1728,128]{1,0:T(8,128)(2,1)S(1)}, bf16[1728,128]{1,0:T(8,128)(2,1)S(1)}, u32[]{:S(2)}, u32[]{:S(2)}) collective-permute-start(bf16[1728,128]{1,0:T(8,128)(2,1)S(1)} %get-tuple-element.16), channel_id=1, source_target_pairs={{0,32},{32,0},{1,33},{33,1},{2,34},{34,2},{3,35},{35,3},{4,36},{36... | collective-permute-start | bytes 1327112 | tf_op jit(solution)/shard_map/ppermute | solution.py:244
  135.3 6.6 %collective-permute-start.13 = (bf16[1728,128]{1,0:T(8,128)(2,1)S(1)}, bf16[1728,128]{1,0:T(8,128)(2,1)S(1)}, u32[]{:S(2)}, u32[]{:S(2)}) collective-permute-start(bf16[1728,128]{1,0:T(8,128)(2,1)S(1)} %bitcast.22), channel_id=1, source_target_pairs={{0,32},{32,0},{1,33},{33,1},{2,34},{34,2},{3,35},{35,3},{4,36},{36... | collective-permute-start | bytes 1327112 | tf_op jit(solution)/shard_map/ppermute | solution.py:244

commit v2 on v1

--- a/solution.py
+++ b/solution.py
@@ -33,44 +33,47 @@
     return before.astype(BF16), x.astype(BF16), after.astype(BF16)
 
 
-def spread(src, im, rows):
-    cells = rows * COLS
-
-    @pl.loop(0, FR)
-    def _(t):
-        for lag_c, v in enumerate(shifted(src[t, : cells + 2 * COLS])):
-            for lag_r in range(3):
-                at = pl.multiple_of((t + 2) * PLANE + (lag_r * 3 + lag_c) * CH, CH)
-                im[:cells, pl.ds(at, CH)] = v[lag_r * COLS : lag_r * COLS + cells]
-
-
 def inside(first, rows, total):
     row = first + lax.broadcasted_iota(jnp.int32, (rows * COLS, CH), 0) // COLS
     return (row >= 0) & (row < total)
 
 
+def taps_of(cols, frames, cells):
+    return jnp.concatenate(
+        [
+            cols[t * 3 + lag_c, lag_r * COLS : lag_r * COLS + cells]
+            for t in frames
+            for lag_r in range(3)
+            for lag_c in range(3)
+        ],
+        1,
+    )
+
+
+def pair_kernel(ref, base, first):
+    rows = (4 - first) * PLANE
+    at = base + first * PLANE
+    return jnp.concatenate(
+        [ref[pl.ds(at + PLANE, rows)], ref[pl.ds(at, rows)]],
+        1,
+    )
+
+
 def layers_kernel(
-    total, pos, mine, other, w0, r1, r2, r3, q1, q2, q3, o0, o1, o2, o3, wt, wb, im, hid, fac, grad, dz, part
+    total, pos, mine, other, w0, r1, r2, r3, q1, q2, q3, o0, o1, o2, o3, wz, wb, cols, fac, grad, part
 ):
     seg, tm, first = pos[0], pos[1], pos[2]
+    step = PLANE + KC
     zero = jnp.zeros((PLANE, CH), BF16)
+    for l in range(LAYERS + 1):
+        wz[l * step : l * step + PLANE] = zero
     for l in range(LAYERS):
-        wt[l, KC:, :CH] = zero
-        wt[l, :PLANE, CH:] = zero
-    wb[KC:, :CH] = zero
-    wb[:PLANE, CH:] = zero
-    cells = im.shape[0]
-    im[:, : 2 * PLANE] = jnp.zeros((cells, 2 * PLANE), BF16)
-    im[:, (FR + 2) * PLANE :] = jnp.zeros((cells, 2 * PLANE), BF16)
-    own = w0[...]
-    wt[seg, :KC, :CH] = own
-    wt[seg, PLANE:, CH:] = own
+        wb[l * step : l * step + PLANE] = zero
+    wz[pl.ds(pl.multiple_of(seg * step + PLANE, CH), KC)] = w0[...]
     for d, (r, q) in enumerate(((r1, q1), (r2, q2), (r3, q3)), 1):
-        l = lax.rem(seg + LAYERS - d, LAYERS)
-        for ref, half in ((r, tm), (q, 1 - tm)):
-            at = pl.multiple_of(half * HALF, CH // 2)
-            wt[l, pl.ds(at, HALF), :CH] = ref[...]
-            wt[l, pl.ds(PLANE + at, HALF), CH:] = ref[...]
+        at = lax.rem(seg + LAYERS - d, LAYERS) * step + PLANE
+        wz[pl.ds(pl.multiple_of(at + tm * HALF, CH // 2), HALF)] = r[...]
+        wz[pl.ds(pl.multiple_of(at + (1 - tm) * HALF, CH // 2), HALF)] = q[...]
 
     span = OWN + 2 * HALO
     half_fr = FR // 2
@@ -78,76 +81,82 @@
 
         @pl.loop(0, half_fr)
         def _(t):
+            frame = which * half_fr + t
             rows = ref[t, pl.ds(tm * OWN, span)]
-            hid[0, which * half_fr + t, : span * COLS] = rows.reshape(span * COLS, CH).astype(F32)
+            for lag_c, v in enumerate(shifted(rows.reshape(span * COLS, CH).astype(F32))):
+                cols[0, frame * 3 + lag_c] = v
             at = 2 * HALO + 2 * OWN + tm * OWN
             rows = ref[t, pl.ds(at, OWN + 2 * CHALO)]
-            grad[which * half_fr + t] = rows.reshape(-1, CH).astype(F32)
+            grad[frame] = rows.reshape(-1, CH).astype(F32)
+
+    width = (OWN + 2) * COLS
+    own_cells = OWN * COLS
+
+    def set_delta(l, t, value, to):
+        cells = value.shape[0]
+        valid = inside(first - l, OWN + 2 * l, total)
+        delta = jnp.where(valid, value, 0.0).astype(BF16)
+        at = HID + t * own_cells
+        part[l, at : at + own_cells] = delta[l * COLS : l * COLS + own_cells]
+        if l > 0:
+            for lag_c, v in enumerate(shifted(delta.astype(F32))):
+                to[t * 3 + lag_c, :cells] = v
 
     for l in range(LAYERS):
         rows = span - 2 * (l + 1)
         cells = rows * COLS
-        spread(hid.at[l], im, rows)
+        src, dst = cols.at[l % 2], cols.at[(l + 1) % 2]
+        for t in range(FR):
+            at = (6 - l) * COLS
+            part[l, t * width : (t + 1) * width] = src[t * 3 + 1, at : at + width]
+        if l > 0:
+            for k in range(TAPS):
+                at = l * step + PLANE + (TAPS - 1 - k) * CH
+                to = (l - 1) * step + PLANE + k * CH
+                wb[to : to + CH] = wz[at : at + CH].T
         keep = slice((6 - 2 * l) * COLS, 10 * COLS)
         kept = (OWN + 2 * l) * COLS
-
-        @pl.loop(0, FR // 2)
-        def _(p):
-            at = pl.multiple_of(2 * p * PLANE, CH)
-            pre2 = jnp.dot(im[:cells, pl.ds(at, 4 * PLANE)], wt[l], preferred_element_type=F32)
-            valid = inside(first - HALO + l + 1, rows, total)
+        valid = inside(first - HALO + l + 1, rows, total)
+        for p in range(FR // 2):
+            lo = max(0, 2 * p - 2)
+            pre2 = jnp.dot(
+                taps_of(src, range(lo, 2 * p + 2), cells),
+                pair_kernel(wz, l * step, 0 if p else 2),
+                preferred_element_type=F32,
+            )
             for e in range(2):
                 t = 2 * p + e
                 pre = pre2[:, e * CH : (e + 1) * CH]
                 s = jax.nn.sigmoid(pre)
                 if l + 1 < LAYERS:
-                    new = hid[l, t, COLS : COLS + cells] + pre * s
-                    new = new.astype(BF16).astype(F32)
-                    hid[l + 1, t, :cells] = jnp.where(valid, new, 0.0)
+                    new = src[t * 3 + 1, COLS : COLS + cells].astype(F32) + pre * s
+                    new = jnp.where(valid, new, 0.0).astype(BF16).astype(F32)
+                    for lag_c, v in enumerate(shifted(new)):
+                        dst[t * 3 + lag_c, :cells] = v
                 s, pre = s[keep], pre[keep]
-                fac[l, t, :kept] = s * (1.0 + pre * (1.0 - s))
-
-    for l in reversed(range(LAYERS)):
-        rows = OWN + 2 * l
-        cells = rows * COLS
-        width = (OWN + 2) * COLS
-        own_cells = OWN * COLS
-
-        @pl.loop(0, FR)
-        def _(t):
-            valid = inside(first - l, rows, total)
-            delta = jnp.where(valid, grad[t, :cells] * fac[l, t, :cells], 0.0).astype(BF16)
-            at = pl.multiple_of(HID + t * own_cells, own_cells)
-            part[l, pl.ds(at, own_cells)] = delta[l * COLS : l * COLS + own_cells]
-            at = pl.multiple_of(t * width, width)
-            part[l, pl.ds(at, width)] = hid[l, t, (6 - l) * COLS : (6 - l) * COLS + width].astype(
-                BF16
-            )
-            if l > 0:
-                dz[t, :cells] = delta.astype(F32)
-
-        if l > 0:
-            inner = cells - 2 * COLS
-            spread(dz, im, rows - 2)
-
-            @pl.loop(0, TAPS)
-            def _(k):
-                at = pl.multiple_of((TAPS - 1 - k) * CH, CH)
-                block = wt[l, pl.ds(at, CH), :CH].T
-                at = pl.multiple_of(k * CH, CH)
-                wb[pl.ds(at, CH), :CH] = block
-                wb[pl.ds(PLANE + at, CH), CH:] = block
-
-            @pl.loop(0, FR // 2)
-            def _(p):
-                at = pl.multiple_of((2 * p + 2) * PLANE, CH)
-                adjoint = jnp.dot(
-                    im[:inner, pl.ds(at, 4 * PLANE)], wb[...], preferred_element_type=F32
-                )
+                slope = s * (1.0 + pre * (1.0 - s))
+                if l + 1 < LAYERS:
+                    fac[l, t, :kept] = slope
+                else:
+                    set_delta(l, t, grad[t] * slope, dst)
+
+    for l in reversed(range(1, LAYERS)):
+        cells = (OWN + 2 * (l - 1)) * COLS
+        src, dst = cols.at[(l + 1) % 2], cols.at[l % 2]
+        for pairs in ((0, 1, 2), (3,)):
+            hi = 4 if len(pairs) > 1 else 2
+            lhs = [taps_of(src, range(2 * p, 2 * p + hi), cells) for p in pairs]
+            kernel = pair_kernel(wb, (l - 1) * step, 0)[: hi * PLANE]
+            adjoint = jnp.dot(jnp.concatenate(lhs, 0), kernel, preferred_element_type=F32)
+            for i, p in enumerate(pairs):
                 for e in range(2):
                     t = 2 * p + e
-                    new = grad[t, COLS : COLS + inner] + adjoint[:, e * CH : (e + 1) * CH]
-                    grad[t, :inner] = new.astype(BF16).astype(F32)
+                    mine_of = adjoint[i * cells : (i + 1) * cells, e * CH : (e + 1) * CH]
+                    new = grad[t, COLS : COLS + cells] + mine_of
+                    new = new.astype(BF16).astype(F32)
+                    if l > 1:
+                        grad[t, :cells] = new
+                    set_delta(l - 1, t, new * fac[l - 1, t, :cells], dst)
 
     for d, out in enumerate((o0, o1, o2, o3)):
         out[...] = part[lax.rem(seg + d, LAYERS)]
@@ -196,12 +205,10 @@
         in_specs=in_vmem(len(arrays)),
         out_specs=(pl.BlockSpec(memory_space=pltpu.VMEM),) * LAYERS,
         scratch_shapes=[
-            pltpu.VMEM((LAYERS, 4 * PLANE, 2 * CH), BF16),
-            pltpu.VMEM((4 * PLANE, 2 * CH), BF16),
-            pltpu.VMEM(((span - 2) * COLS, (FR + 4) * PLANE), BF16),
-            pltpu.VMEM((LAYERS, FR, span * COLS, CH), F32),
-            pltpu.VMEM((LAYERS, FR, (OWN + 2 * CHALO) * COLS, CH), F32),
-            pltpu.VMEM((FR, (OWN + 2 * CHALO) * COLS, CH), F32),
+            pltpu.VMEM((PLANE + LAYERS * (PLANE + KC), CH), BF16),
+            pltpu.VMEM((PLANE + (LAYERS - 1) * (PLANE + KC), CH), BF16),
+            pltpu.VMEM((2, FR * 3, span * COLS, CH), BF16),
+            pltpu.VMEM((LAYERS - 1, FR, (OWN + 2 * CHALO) * COLS, CH), F32),
             pltpu.VMEM((FR, (OWN + 2 * CHALO) * COLS, CH), F32),
             pltpu.VMEM((LAYERS, PART, CH), BF16),
         ],

time: 144 us -> 127 us (0.88)
  Pallas kernels: 34.6 us -> 17.6 us
    pallas_call x1, Pallas kernels: 31.1 us -> 14.1 us  [run_layers(): pl.pallas_call(functools.partial(layers_kernel, total), out_shape=(out,)...]
where the time goes in v2:
time: 127 us; the launch traced here: 126 us
  blocking collectives  46.8 us (37%)
  starting transfers between devices  31.4 us (25%)
  waiting for transfers between devices  27.3 us (21%)
  Pallas kernels  17.6 us (14%)
  other arithmetic  1.73 us (1%)
  local copies, waits for them, and re-layouts  1.33 us (1%)
    ppermute x6, starting transfers between devices, swap(): return lax.ppermute(x, 'tm', [(0, 1), (1, 0)])  19.6 us
    all_to_all x1, blocking collectives, body(): pieces = lax.all_to_all(total.reshape(nz, rows_z, CH), 'z', 0, 0)  15.8 us
    ppermute x3, waiting for transfers between devices, body(): lax.ppermute(parts[d], 'segment', ring(LAYERS, d))  14.8 us
    pallas_call x1, Pallas kernels, run_layers(): pl.pallas_call(functools.partial(layers_kernel, total), out_shape=(out,)...  14.1 us
    all_to_all x1, blocking collectives, body(): pieces = lax.all_to_all(total.reshape(ny, rows_y, CH), 'y', 0, 0)  11.8 us
    all_to_all x1, blocking collectives, body(): whole = lax.all_to_all(jnp.broadcast_to(total, (nz, rows_z, CH)), 'z', 0, 0)  10.3 us
    all_to_all x1, blocking collectives, body(): whole = lax.all_to_all(jnp.broadcast_to(whole, (ny, rows_y, CH)), 'y', 0, 0)  8.87 us
    ppermute x1, waiting for transfers between devices, body(): lax.ppermute(jnp.concatenate([x[:, :HALO], c[:, :CHALO]], 1), ('z', 'y'),...  5 us
  transfers between devices with their start and end apart: 14, of which 8 were waited for; matrix products, arithmetic and copies ran while one was open for 0% of the time, Pallas kernels for 0%

profile of v2, /device:TPU:1, one launch (start us, length us, event | category | flops | bytes accessed | tf_op | source)
XLA Modules:
  0.0 126.3 jit_solution(1301673901795220863)
XLA Ops:
  0.0 1.1 dynamic-slice_bitcast_fusion.1
  1.2 4.0 %collective-permute-start = (bf16[4,10,16,128]{3,2,1,0:T(8,128)(2,1)S(1)}, bf16[4,10,16,128]{3,2,1,0:T(8,128)(2,1)S(1)}, u32[]{:S(2)}, u32[]{:S(2)}) collective-permute-start(bf16[4,10,16,128]{3,2,1,0:T(8,128)(2,1)S(1)} %pad_maximum_fusion), channel_id=1, source_target_pairs={{0,1},{1,2},{2,3},{3,4},{4,5},{5,6},{6,7},{7,8},{8,9},{9,10},{10,1... | collective-permute-start | bytes 491528 | tf_op jit(solution)/shard_map/ppermute | solution.py:271
  5.3 2.6 %collective-permute-start.5 = (bf16[1728,128]{1,0:T(8,128)(2,1)S(1)}, bf16[1728,128]{1,0:T(8,128)(2,1)S(1)}, u32[]{:S(2)}, u32[]{:S(2)}) collective-permute-start(bf16[1728,128]{1,0:T(8,128)(2,1)S(1)} %dynamic-slice_bitcast_fusion), channel_id=1, source_target_pairs={{0,192},{64,0},{128,64},{192,128},{1,193},{65,1},{129,65},{193,129... | collective-permute-start | bytes 1327112 | tf_op jit(solution)/shard_map/ppermute | solution.py:264
  9.0 1.3 %collective-permute-start.1 = (bf16[4,10,16,128]{3,2,1,0:T(8,128)(2,1)S(1)}, bf16[4,10,16,128]{3,2,1,0:T(8,128)(2,1)S(1)}, u32[]{:S(2)}, u32[]{:S(2)}) collective-permute-start(bf16[4,10,16,128]{3,2,1,0:T(8,128)(2,1)S(1)} %pad_maximum_fusion.1), channel_id=1, source_target_pairs={{1,0},{2,1},{3,2},{4,3},{5,4},{6,5},{7,6},{8,7},{9,8},{10,9},{11,1... | collective-permute-start | bytes 491528 | tf_op jit(solution)/shard_map/ppermute | solution.py:274
  10.3 5.0 %collective-permute-done.1 = bf16[4,10,16,128]{3,2,1,0:T(8,128)(2,1)S(1)} collective-permute-done((bf16[4,10,16,128]{3,2,1,0:T(8,128)(2,1)S(1)}, bf16[4,10,16,128]{3,2,1,0:T(8,128)(2,1)S(1)}, u32[]{:S(2)}, u32[]{:S(2)}) %collective-permute-start.1) | collective-permute-done | bytes 163872 | tf_op jit(solution)/shard_map/ppermute | solution.py:274
  15.4 2.7 %collective-permute-start.2 = (bf16[4,36,16,128]{3,2,1,0:T(8,128)(2,1)S(1)}, bf16[4,36,16,128]{3,2,1,0:T(8,128)(2,1)S(1)}, u32[]{:S(2)}, u32[]{:S(2)}) collective-permute-start(bf16[4,36,16,128]{3,2,1,0:T(8,128)(2,1)S(1)} %slice_dynamic-update-slice_fusion.2.mine), channel_id=1, source_target_pairs={{0,32},{32,0},{1,33},{33,1},{2,34},{34,2},{3,35},{35,3},{4,36},{36... | collective-permute-start | bytes 1769480 | tf_op jit(solution)/shard_map/ppermute | solution.py:251
  18.1 9.6 %collective-permute-start.8 = (bf16[1728,128]{1,0:T(8,128)(2,1)S(1)}, bf16[1728,128]{1,0:T(8,128)(2,1)}, u32[]{:S(2)}, u32[]{:S(2)}) collective-permute-start(bf16[1728,128]{1,0:T(8,128)(2,1)S(1)} %collective-permute-done.5.r3), channel_id=1, source_target_pairs={{0,32},{32,0},{1,33},{33,1},{2,34},{34,2},{3,35},{35,3},{4,36},{36... | collective-permute-start | bytes 1327112 | tf_op jit(solution)/shard_map/ppermute | solution.py:251
  27.7 3.2 %collective-permute-done.3.r1 = bf16[1728,128]{1,0:T(8,128)(2,1)S(1)} collective-permute-done((bf16[1728,128]{1,0:T(8,128)(2,1)S(1)}, bf16[1728,128]{1,0:T(8,128)(2,1)S(1)}, u32[]{:S(2)}, u32[]{:S(2)}) %collective-permute-start.3) | collective-permute-done | bytes 442400 | tf_op jit(solution)/shard_map/ppermute | solution.py:264
  31.5 1.5 %collective-permute-done.6.q1 = bf16[1728,128]{1,0:T(8,128)(2,1)} collective-permute-done((bf16[1728,128]{1,0:T(8,128)(2,1)S(1)}, bf16[1728,128]{1,0:T(8,128)(2,1)}, u32[]{:S(2)}, u32[]{:S(2)}) %collective-permute-start.6) | collective-permute-done | bytes 442400 | tf_op jit(solution)/shard_map/ppermute | solution.py:251
  32.9 14.1 %layers.1 = (bf16[1280,128]{1,0:T(8,128)(2,1)S(1)}, bf16[1280,128]{1,0:T(8,128)(2,1)S(1)}, bf16[1280,128]{1,0:T(8,128)(2,1)S(1)}, bf16[1280,128]{1,0:T(8,128)(2,1)S(1)}) custom-call(s32[3]{0:T(128)S(1)} %pad_add_fusion.pos, bf16[4,36,16,128]{3,2,1,0:T(8,128)(2,1)S(1)} %slice_dynamic-update-slice_fusion.2.mine, ...), custom_call_target="tpu_custom_call" | custom-call | flops 8999999488 | bytes 6000000 | tf_op jit(solution)/shard_map/layers/pallas_call | solution.py:202
  47.1 2.1 %collective-permute-start.10 = (bf16[1280,128]{1,0:T(8,128)(2,1)S(1)}, bf16[1280,128]{1,0:T(8,128)(2,1)S(1)}, u32[]{:S(2)}, u32[]{:S(2)}) collective-permute-start(bf16[1280,128]{1,0:T(8,128)(2,1)S(1)} %get-tuple-element.13), channel_id=1, source_target_pairs={{0,128},{64,192},{128,0},{192,64},{1,129},{65,193},{129,1},{193,65... | collective-permute-start | bytes 983048 | tf_op jit(solution)/shard_map/ppermute | solution.py:281
  49.8 8.0 %collective-permute-done.9.e1 = bf16[1280,128]{1,0:T(8,128)(2,1)S(1)} collective-permute-done((bf16[1280,128]{1,0:T(8,128)(2,1)S(1)}, bf16[1280,128]{1,0:T(8,128)(2,1)S(1)}, u32[]{:S(2)}, u32[]{:S(2)}) %collective-permute-start.9) | collective-permute-done | bytes 327712 | tf_op jit(solution)/shard_map/ppermute | solution.py:281
  57.7 6.0 %collective-permute-done.10.e2 = bf16[1280,128]{1,0:T(8,128)(2,1)S(1)} collective-permute-done((bf16[1280,128]{1,0:T(8,128)(2,1)S(1)}, bf16[1280,128]{1,0:T(8,128)(2,1)S(1)}, u32[]{:S(2)}, u32[]{:S(2)}) %collective-permute-start.10) | collective-permute-done | bytes 327712 | tf_op jit(solution)/shard_map/ppermute | solution.py:281
  63.8 0.8 collective-permute-done.11.e3
  64.6 3.5 %kernel_grad.1 = (f32[1728,128]{1,0:T(8,128)S(1)}, bf16[1728,128]{1,0:T(8,128)(2,1)S(1)}) custom-call(s32[3]{0:T(128)S(1)} %pad_add_fusion.pos, bf16[1280,128]{1,0:T(8,128)(2,1)S(1)} %get-tuple-element.11.e0, bf16[1280,128]{1,0:T(8,128)(2,1)S(1)} %collective-permute-done.9.e1, bf16[1280,128]{1,0:T(8,128)(2,1)S(1)} %collective-permute-done.10.e2, ...), custom_call_target="tpu_custom_call" | custom-call | flops 1800000000 | bytes 4000000 | tf_op jit(solution)/shard_map/kernel_grad/pallas_call | solution.py:225
  68.1 1.6 %collective-permute-start.12 = (bf16[1728,128]{1,0:T(8,128)(2,1)S(1)}, bf16[1728,128]{1,0:T(8,128)(2,1)S(1)}, u32[]{:S(2)}, u32[]{:S(2)}) collective-permute-start(bf16[1728,128]{1,0:T(8,128)(2,1)S(1)} %get-tuple-element.16), channel_id=1, source_target_pairs={{0,32},{32,0},{1,33},{33,1},{2,34},{34,2},{3,35},{35,3},{4,36},{36... | collective-permute-start | bytes 1327112 | tf_op jit(solution)/shard_map/ppermute | solution.py:251
  69.7 1.4 %collective-permute-done.12 = bf16[1728,128]{1,0:T(8,128)(2,1)S(1)} collective-permute-done((bf16[1728,128]{1,0:T(8,128)(2,1)S(1)}, bf16[1728,128]{1,0:T(8,128)(2,1)S(1)}, u32[]{:S(2)}, u32[]{:S(2)}) %collective-permute-start.12) | collective-permute-done | bytes 442400 | tf_op jit(solution)/shard_map/ppermute | solution.py:251
  71.2 11.8 %all_to_all.20 = bf16[4,432,128]{2,1,0:T(8,128)(2,1)S(1)} all-to-all(bf16[4,432,128]{2,1,0:T(8,128)(2,1)S(1)} %bitcast.21), channel_id=1, replica_groups=mesh['segment'=4,'tm'=2,'z'=8,'y'=4] {'y'}, dimensions={0} | all-to-all | bytes 884736 | tf_op jit(solution)/shard_map/all_to_all | solution.py:286
  83.1 15.8 %all_to_all.21 = bf16[8,64,128]{2,1,0:T(8,128)(2,1)S(1)} all-to-all(bf16[8,64,128]{2,1,0:T(8,128)(2,1)S(1)} %bitcast.23), channel_id=1, replica_groups=mesh['segment'=4,'tm'=2,'z'=8,'y'=4] {'z'}, dimensions={0} | all-to-all | bytes 262144 | tf_op jit(solution)/shard_map/all_to_all | solution.py:290
  99.0 10.3 %all_to_all.22 = bf16[8,64,128]{2,1,0:T(8,128)(2,1)S(1)} all-to-all(bf16[8,64,128]{2,1,0:T(8,128)(2,1)S(1)} %broadcast_in_dim.7), channel_id=1, replica_groups=mesh['segment'=4,'tm'=2,'z'=8,'y'=4] {'z'}, dimensions={0} | all-to-all | bytes 262144 | tf_op jit(solution)/shard_map/all_to_all | solution.py:292
  109.4 8.9 %all_to_all.23 = bf16[4,432,128]{2,1,0:T(8,128)(2,1)S(1)} all-to-all(bf16[4,432,128]{2,1,0:T(8,128)(2,1)S(1)} %broadcast_in_dim.8), channel_id=1, replica_groups=mesh['segment'=4,'tm'=2,'z'=8,'y'=4] {'y'}, dimensions={0} | all-to-all | bytes 884736 | tf_op jit(solution)/shard_map/all_to_all | solution.py:294
  118.3 5.2 %collective-permute-start.13 = (bf16[1728,128]{1,0:T(8,128)(2,1)S(1)}, bf16[1728,128]{1,0:T(8,128)(2,1)S(1)}, u32[]{:S(2)}, u32[]{:S(2)}) collective-permute-start(bf16[1728,128]{1,0:T(8,128)(2,1)S(1)} %bitcast.22), channel_id=1, source_target_pairs={{0,32},{32,0},{1,33},{33,1},{2,34},{34,2},{3,35},{35,3},{4,36},{36... | collective-permute-start | bytes 1327112 | tf_op jit(solution)/shard_map/ppermute | solution.py:251
  123.5 1.4 %collective-permute-done.13 = bf16[1728,128]{1,0:T(8,128)(2,1)S(1)} collective-permute-done((bf16[1728,128]{1,0:T(8,128)(2,1)S(1)}, bf16[1728,128]{1,0:T(8,128)(2,1)S(1)}, u32[]{:S(2)}, u32[]{:S(2)}) %collective-permute-start.13) | collective-permute-done | bytes 442400 | tf_op jit(solution)/shard_map/ppermute | solution.py:251
  125.0 1.3 %maximum_convert_fusion = f32[1,3456,128]{2,1,0:T(8,128)} fusion(bf16[1,1728,128]{2,1,0:T(8,128)(2,1)S(1)} %get-tuple-element.18, bf16[1,1728,128]{2,1,0:T(8,128)(2,1)S(1)} %get-tuple-element.17), kind=kLoop, calls=%fused_computation | loop fusion | flops 1769472 | bytes 2654208 | tf_op jit(solution)/shard_map/convert_element_type | solution.py:299
  (34 shorter events, 2.9 us)
Async XLA Ops:
  0.0 5.2 %copy-start = (bf16[1,3456,128]{2,1,0:T(8,128)(2,1)S(1)}, bf16[1,3456,128]{2,1,0:T(8,128)(2,1)}, u32[]{:S(2)}) copy-start(bf16[1,3456,128]{2,1,0:T(8,128)(2,1)} %param.4) | copy-start | bytes 2654212
  1.2 9.1 %collective-permute-start = (bf16[4,10,16,128]{3,2,1,0:T(8,128)(2,1)S(1)}, bf16[4,10,16,128]{3,2,1,0:T(8,128)(2,1)S(1)}, u32[]{:S(2)}, u32[]{:S(2)}) collective-permute-start(bf16[4,10,16,128]{3,2,1,0:T(8,128)(2,1)S(1)} %pad_maximum_fusion), channel_id=1, source_target_pairs={{0,1},{1,2},{2,3},{3,4},{4,5},{5,6},{6,7},{7,8},{8,9},{9,10},{10,1... | collective-permute-start | bytes 491528 | tf_op jit(solution)/shard_map/ppermute | solution.py:271
  5.3 12.9 %collective-permute-start.5 = (bf16[1728,128]{1,0:T(8,128)(2,1)S(1)}, bf16[1728,128]{1,0:T(8,128)(2,1)S(1)}, u32[]{:S(2)}, u32[]{:S(2)}) collective-permute-start(bf16[1728,128]{1,0:T(8,128)(2,1)S(1)} %dynamic-slice_bitcast_fusion), channel_id=1, source_target_pairs={{0,192},{64,0},{128,64},{192,128},{1,193},{65,1},{129,65},{193,129... | collective-permute-start | bytes 1327112 | tf_op jit(solution)/shard_map/ppermute | solution.py:264
  7.8 19.9 %collective-permute-start.4 = (bf16[1728,128]{1,0:T(8,128)(2,1)S(1)}, bf16[1728,128]{1,0:T(8,128)(2,1)S(1)}, u32[]{:S(2)}, u32[]{:S(2)}) collective-permute-start(bf16[1728,128]{1,0:T(8,128)(2,1)S(1)} %dynamic-slice_bitcast_fusion), channel_id=1, source_target_pairs={{0,128},{64,192},{128,0},{192,64},{1,129},{65,193},{129,1},{193,65... | collective-permute-start | bytes 1327112 | tf_op jit(solution)/shard_map/ppermute | solution.py:264
  8.3 22.6 %collective-permute-start.3 = (bf16[1728,128]{1,0:T(8,128)(2,1)S(1)}, bf16[1728,128]{1,0:T(8,128)(2,1)S(1)}, u32[]{:S(2)}, u32[]{:S(2)}) collective-permute-start(bf16[1728,128]{1,0:T(8,128)(2,1)S(1)} %dynamic-slice_bitcast_fusion), channel_id=1, source_target_pairs={{0,64},{64,128},{128,192},{192,0},{1,65},{65,129},{129,193},{193,1... | collective-permute-start | bytes 1327112 | tf_op jit(solution)/shard_map/ppermute | solution.py:264
  9.0 6.4 %collective-permute-start.1 = (bf16[4,10,16,128]{3,2,1,0:T(8,128)(2,1)S(1)}, bf16[4,10,16,128]{3,2,1,0:T(8,128)(2,1)S(1)}, u32[]{:S(2)}, u32[]{:S(2)}) collective-permute-start(bf16[4,10,16,128]{3,2,1,0:T(8,128)(2,1)S(1)} %pad_maximum_fusion.1), channel_id=1, source_target_pairs={{1,0},{2,1},{3,2},{4,3},{5,4},{6,5},{7,6},{8,7},{9,8},{10,9},{11,1... | collective-permute-start | bytes 491528 | tf_op jit(solution)/shard_map/ppermute | solution.py:274
  15.4 16.1 %collective-permute-start.2 = (bf16[4,36,16,128]{3,2,1,0:T(8,128)(2,1)S(1)}, bf16[4,36,16,128]{3,2,1,0:T(8,128)(2,1)S(1)}, u32[]{:S(2)}, u32[]{:S(2)}) collective-permute-start(bf16[4,36,16,128]{3,2,1,0:T(8,128)(2,1)S(1)} %slice_dynamic-update-slice_fusion.2.mine), channel_id=1, source_target_pairs={{0,32},{32,0},{1,33},{33,1},{2,34},{34,2},{3,35},{35,3},{4,36},{36... | collective-permute-start | bytes 1769480 | tf_op jit(solution)/shard_map/ppermute | solution.py:251
  18.1 13.3 %collective-permute-start.8 = (bf16[1728,128]{1,0:T(8,128)(2,1)S(1)}, bf16[1728,128]{1,0:T(8,128)(2,1)}, u32[]{:S(2)}, u32[]{:S(2)}) collective-permute-start(bf16[1728,128]{1,0:T(8,128)(2,1)S(1)} %collective-permute-done.5.r3), channel_id=1, source_target_pairs={{0,32},{32,0},{1,33},{33,1},{2,34},{34,2},{3,35},{35,3},{4,36},{36... | collective-permute-start | bytes 1327112 | tf_op jit(solution)/shard_map/ppermute | solution.py:251
  27.7 3.8 %collective-permute-start.7 = (bf16[1728,128]{1,0:T(8,128)(2,1)S(1)}, bf16[1728,128]{1,0:T(8,128)(2,1)}, u32[]{:S(2)}, u32[]{:S(2)}) collective-permute-start(bf16[1728,128]{1,0:T(8,128)(2,1)S(1)} %collective-permute-done.4.r2), channel_id=1, source_target_pairs={{0,32},{32,0},{1,33},{33,1},{2,34},{34,2},{3,35},{35,3},{4,36},{36... | collective-permute-start | bytes 1327112 | tf_op jit(solution)/shard_map/ppermute | solution.py:251
  30.9 2.0 %collective-permute-start.6 = (bf16[1728,128]{1,0:T(8,128)(2,1)S(1)}, bf16[1728,128]{1,0:T(8,128)(2,1)}, u32[]{:S(2)}, u32[]{:S(2)}) collective-permute-start(bf16[1728,128]{1,0:T(8,128)(2,1)S(1)} %collective-permute-done.3.r1), channel_id=1, source_target_pairs={{0,32},{32,0},{1,33},{33,1},{2,34},{34,2},{3,35},{35,3},{4,36},{36... | collective-permute-start | bytes 1327112 | tf_op jit(solution)/shard_map/ppermute | solution.py:251
  47.0 10.7 %collective-permute-start.9 = (bf16[1280,128]{1,0:T(8,128)(2,1)S(1)}, bf16[1280,128]{1,0:T(8,128)(2,1)S(1)}, u32[]{:S(2)}, u32[]{:S(2)}) collective-permute-start(bf16[1280,128]{1,0:T(8,128)(2,1)S(1)} %get-tuple-element.12), channel_id=1, source_target_pairs={{0,64},{64,128},{128,192},{192,0},{1,65},{65,129},{129,193},{193,1... | collective-permute-start | bytes 983048 | tf_op jit(solution)/shard_map/ppermute | solution.py:281
  47.1 16.7 %collective-permute-start.10 = (bf16[1280,128]{1,0:T(8,128)(2,1)S(1)}, bf16[1280,128]{1,0:T(8,128)(2,1)S(1)}, u32[]{:S(2)}, u32[]{:S(2)}) collective-permute-start(bf16[1280,128]{1,0:T(8,128)(2,1)S(1)} %get-tuple-element.13), channel_id=1, source_target_pairs={{0,128},{64,192},{128,0},{192,64},{1,129},{65,193},{129,1},{193,65... | collective-permute-start | bytes 983048 | tf_op jit(solution)/shard_map/ppermute | solution.py:281
  49.3 15.3 %collective-permute-start.11 = (bf16[1280,128]{1,0:T(8,128)(2,1)S(1)}, bf16[1280,128]{1,0:T(8,128)(2,1)S(1)}, u32[]{:S(2)}, u32[]{:S(2)}) collective-permute-start(bf16[1280,128]{1,0:T(8,128)(2,1)S(1)} %get-tuple-element.14), channel_id=1, source_target_pairs={{0,192},{64,0},{128,64},{192,128},{1,193},{65,1},{129,65},{193,129... | collective-permute-start | bytes 983048 | tf_op jit(solution)/shard_map/ppermute | solution.py:281
  68.1 3.0 %collective-permute-start.12 = (bf16[1728,128]{1,0:T(8,128)(2,1)S(1)}, bf16[1728,128]{1,0:T(8,128)(2,1)S(1)}, u32[]{:S(2)}, u32[]{:S(2)}) collective-permute-start(bf16[1728,128]{1,0:T(8,128)(2,1)S(1)} %get-tuple-element.16), channel_id=1, source_target_pairs={{0,32},{32,0},{1,33},{33,1},{2,34},{34,2},{3,35},{35,3},{4,36},{36... | collective-permute-start | bytes 1327112 | tf_op jit(solution)/shard_map/ppermute | solution.py:251
  118.3 6.6 %collective-permute-start.13 = (bf16[1728,128]{1,0:T(8,128)(2,1)S(1)}, bf16[1728,128]{1,0:T(8,128)(2,1)S(1)}, u32[]{:S(2)}, u32[]{:S(2)}) collective-permute-start(bf16[1728,128]{1,0:T(8,128)(2,1)S(1)} %bitcast.22), channel_id=1, source_target_pairs={{0,32},{32,0},{1,33},{33,1},{2,34},{34,2},{3,35},{35,3},{4,36},{36... | collective-permute-start | bytes 1327112 | tf_op jit(solution)/shard_map/ppermute | solution.py:251

commit v3 on v2

--- a/solution.py
+++ b/solution.py
@@ -60,8 +60,9 @@
 
 
 def layers_kernel(
-    total, pos, mine, other, w0, r1, r2, r3, q1, q2, q3, o0, o1, o2, o3, wz, wb, cols, fac, grad, part
+    total, pos, mine, other, w0, r1, r3, ra, rb, q1, q3, qa, qb, *rest
 ):
+    o0, o1, oa, ob, o3, wz, wb, cols, fac, grad, part = rest
     seg, tm, first = pos[0], pos[1], pos[2]
     step = PLANE + KC
     zero = jnp.zeros((PLANE, CH), BF16)
@@ -70,10 +71,10 @@
     for l in range(LAYERS):
         wb[l * step : l * step + PLANE] = zero
     wz[pl.ds(pl.multiple_of(seg * step + PLANE, CH), KC)] = w0[...]
-    for d, (r, q) in enumerate(((r1, q1), (r2, q2), (r3, q3)), 1):
-        at = lax.rem(seg + LAYERS - d, LAYERS) * step + PLANE
-        wz[pl.ds(pl.multiple_of(at + tm * HALF, CH // 2), HALF)] = r[...]
-        wz[pl.ds(pl.multiple_of(at + (1 - tm) * HALF, CH // 2), HALF)] = q[...]
+    for d, skip, r, q in ((1, 0, r1, q1), (3, 0, r3, q3), (2, 0, ra, qa), (2, HALF // 2, rb, qb)):
+        at = lax.rem(seg + LAYERS - d, LAYERS) * step + PLANE + skip
+        for ref, half in ((r, tm), (q, 1 - tm)):
+            wz[pl.ds(pl.multiple_of(at + half * HALF, 32), ref.shape[0])] = ref[...]
 
     span = OWN + 2 * HALO
     half_fr = FR // 2
@@ -158,12 +159,14 @@
                         grad[t, :cells] = new
                     set_delta(l - 1, t, new * fac[l - 1, t, :cells], dst)
 
-    for d, out in enumerate((o0, o1, o2, o3)):
-        out[...] = part[lax.rem(seg + d, LAYERS)]
-
-
-def kernel_grad_kernel(pos, e0, e1, e2, e3, keep, send, x9, d3, wg):
+    for d, lo, out in ((0, 0, o0), (1, 0, o1), (2, 0, oa), (2, PART // 2, ob), (3, 0, o3)):
+        out[...] = part[lax.rem(seg + d, LAYERS), lo : lo + out.shape[0]]
+
+
+def kernel_grad_kernel(pos, e0, e1, e3, ea, eb, keep, send, e2, x9, d3, wg):
     tm = pos[1]
+    e2[: PART // 2] = ea[...]
+    e2[PART // 2 :] = eb[...]
     cells = OWN * COLS
     width = cells + 2 * COLS
     nothing = jnp.zeros((cells, CH), BF16)
@@ -198,12 +201,12 @@
 
 def run_layers(total, pos, *arrays):
     span = OWN + 2 * HALO
-    out = jax.ShapeDtypeStruct((PART, CH), BF16)
+    lengths = (PART, PART, PART // 2, PART // 2, PART)
     return pl.pallas_call(
         functools.partial(layers_kernel, total),
-        out_shape=(out,) * LAYERS,
+        out_shape=tuple(jax.ShapeDtypeStruct((n, CH), BF16) for n in lengths),
         in_specs=in_vmem(len(arrays)),
-        out_specs=(pl.BlockSpec(memory_space=pltpu.VMEM),) * LAYERS,
+        out_specs=(pl.BlockSpec(memory_space=pltpu.VMEM),) * len(lengths),
         scratch_shapes=[
             pltpu.VMEM((PLANE + LAYERS * (PLANE + KC), CH), BF16),
             pltpu.VMEM((PLANE + (LAYERS - 1) * (PLANE + KC), CH), BF16),
@@ -231,6 +234,7 @@
         in_specs=in_vmem(len(arrays)),
         out_specs=(pl.BlockSpec(memory_space=pltpu.VMEM),) * 2,
         scratch_shapes=[
+            pltpu.VMEM((PART, CH), BF16),
             pltpu.VMEM((cells, PLANE), BF16),
             pltpu.VMEM((cells, 3 * CH), BF16),
             pltpu.VMEM((KC, CH), F32),
@@ -247,6 +251,10 @@
     return [(i, (i + by) % count) for i in range(count)]
 
 
+def along(x, by):
+    return lax.ppermute(x, "segment", ring(LAYERS, by))
+
+
 def swap(x):
     return lax.ppermute(x, "tm", [(0, 1), (1, 0)])
 
@@ -261,7 +269,8 @@
 
     w = weights[0]
     half = lax.dynamic_slice_in_dim(w, tm * HALF, HALF, 0)
-    got = [lax.ppermute(half, "segment", ring(LAYERS, d)) for d in (1, 2, 3)]
+    left, right = along(half, 1), along(half, -1)
+    got = [left, right, along(left[: HALF // 2], 1), along(right[HALF // 2 :], -1)]
     crossed = [swap(g) for g in got]
 
     x = lax.dynamic_index_in_dim(inputs, seg, 0, keepdims=False)
@@ -278,8 +287,9 @@
     other = swap(mine)
 
     parts = run_layers(spaces * rows, pos, mine, other, w, *got, *crossed)
-    moved = [lax.ppermute(parts[d], "segment", ring(LAYERS, d)) for d in (1, 2, 3)]
-    keep, send = run_kernel_grad(pos, parts[0], *moved)
+    far_a, far_b = along(parts[2], 1), along(parts[3], -1)
+    near = [along(parts[1], 1), along(parts[4], -1)]
+    keep, send = run_kernel_grad(pos, parts[0], *near, along(far_a, 1), along(far_b, -1))
 
     total = (keep + swap(send).astype(F32)).astype(BF16)
     rows_y = HALF // ny

time: 127 us -> 126 us (level)
  waiting for transfers between devices: 27.3 us -> 19.3 us
  starting transfers between devices: 31.4 us -> 36.5 us
  blocking collectives: 46.8 us -> 48.3 us
    ppermute x6 -> x10, waiting for transfers between devices: 18 us -> 10.1 us  [along(): return lax.ppermute(x, 'segment', ring(LAYERS, by))]
    ppermute x6 -> x10, starting transfers between devices: 6.43 us -> 14 us  [along(): return lax.ppermute(x, 'segment', ring(LAYERS, by))]
    ppermute x6 -> x7, starting transfers between devices: 19.6 us -> 17.1 us  [swap(): return lax.ppermute(x, 'tm', [(0, 1), (1, 0)])]
    all_to_all x1, blocking collectives: 11.8 us -> 13.4 us  [body(): pieces = lax.all_to_all(total.reshape(ny, rows_y, CH), 'y', 0, 0)]
    ppermute x6 -> x7, waiting for transfers between devices: 4.31 us -> 4.21 us  [swap(): return lax.ppermute(x, 'tm', [(0, 1), (1, 0)])]
  transfers between devices with their start and end apart: 14 -> 19, of which waited for: 8 -> 8; matrix products, arithmetic and copies ran while one was open for 0% -> 0% of each run, Pallas kernels for 0% -> 0%
where the time goes in v3:
time: 126 us; the launch traced here: 125 us
  blocking collectives  48.3 us (38%)
  starting transfers between devices  36.5 us (29%)
  waiting for transfers between devices  19.3 us (15%)
  Pallas kernels  17.8 us (14%)
  other arithmetic  1.73 us (1%)
  local copies, waits for them, and re-layouts  1.36 us (1%)
    ppermute x7, starting transfers between devices, swap(): return lax.ppermute(x, 'tm', [(0, 1), (1, 0)])  17.1 us
    all_to_all x1, blocking collectives, body(): pieces = lax.all_to_all(total.reshape(nz, rows_z, CH), 'z', 0, 0)  15.7 us
    pallas_call x1, Pallas kernels, run_layers(): pl.pallas_call(functools.partial(layers_kernel, total), out_shape=tuple((...  14.2 us
    ppermute x10, starting transfers between devices, along(): return lax.ppermute(x, 'segment', ring(LAYERS, by))  14 us
    all_to_all x1, blocking collectives, body(): pieces = lax.all_to_all(total.reshape(ny, rows_y, CH), 'y', 0, 0)  13.4 us
    all_to_all x1, blocking collectives, body(): whole = lax.all_to_all(jnp.broadcast_to(total, (nz, rows_z, CH)), 'z', 0, 0)  10.3 us
    ppermute x10, waiting for transfers between devices, along(): return lax.ppermute(x, 'segment', ring(LAYERS, by))  10.1 us
    all_to_all x1, blocking collectives, body(): whole = lax.all_to_all(jnp.broadcast_to(whole, (ny, rows_y, CH)), 'y', 0, 0)  8.87 us
  transfers between devices with their start and end apart: 19, of which 8 were waited for; matrix products, arithmetic and copies ran while one was open for 0% of the time, Pallas kernels for 0%

profile of v3, /device:TPU:1, one launch (start us, length us, event | category | flops | bytes accessed | tf_op | source)
XLA Modules:
  0.0 125.3 jit_solution(8900498569941472134)
XLA Ops:
  1.2 4.0 %collective-permute-start = (bf16[4,10,16,128]{3,2,1,0:T(8,128)(2,1)S(1)}, bf16[4,10,16,128]{3,2,1,0:T(8,128)(2,1)S(1)}, u32[]{:S(2)}, u32[]{:S(2)}) collective-permute-start(bf16[4,10,16,128]{3,2,1,0:T(8,128)(2,1)S(1)} %pad_maximum_fusion), channel_id=1, source_target_pairs={{0,1},{1,2},{2,3},{3,4},{4,5},{5,6},{6,7},{7,8},{8,9},{9,10},{10,1... | collective-permute-start | bytes 491528 | tf_op jit(solution)/shard_map/ppermute | solution.py:280
  5.3 2.6 %collective-permute-start.4 = (bf16[1728,128]{1,0:T(8,128)(2,1)S(1)}, bf16[1728,128]{1,0:T(8,128)(2,1)S(1)}, u32[]{:S(2)}, u32[]{:S(2)}) collective-permute-start(bf16[1728,128]{1,0:T(8,128)(2,1)S(1)} %dynamic-slice_bitcast_fusion), channel_id=1, source_target_pairs={{0,192},{64,0},{128,64},{192,128},{1,193},{65,1},{129,65},{193,129... | collective-permute-start | bytes 1327112 | tf_op jit(solution)/shard_map/ppermute | solution.py:255
  7.8 1.3 %collective-permute-start.1 = (bf16[4,10,16,128]{3,2,1,0:T(8,128)(2,1)S(1)}, bf16[4,10,16,128]{3,2,1,0:T(8,128)(2,1)S(1)}, u32[]{:S(2)}, u32[]{:S(2)}) collective-permute-start(bf16[4,10,16,128]{3,2,1,0:T(8,128)(2,1)S(1)} %pad_maximum_fusion.1), channel_id=1, source_target_pairs={{1,0},{2,1},{3,2},{4,3},{5,4},{6,5},{7,6},{8,7},{9,8},{10,9},{11,1... | collective-permute-start | bytes 491528 | tf_op jit(solution)/shard_map/ppermute | solution.py:283
  9.2 5.0 %collective-permute-done.1 = bf16[4,10,16,128]{3,2,1,0:T(8,128)(2,1)S(1)} collective-permute-done((bf16[4,10,16,128]{3,2,1,0:T(8,128)(2,1)S(1)}, bf16[4,10,16,128]{3,2,1,0:T(8,128)(2,1)S(1)}, u32[]{:S(2)}, u32[]{:S(2)}) %collective-permute-start.1) | collective-permute-done | bytes 163872 | tf_op jit(solution)/shard_map/ppermute | solution.py:283
  14.3 2.2 %collective-permute-start.2 = (bf16[4,36,16,128]{3,2,1,0:T(8,128)(2,1)S(1)}, bf16[4,36,16,128]{3,2,1,0:T(8,128)(2,1)S(1)}, u32[]{:S(2)}, u32[]{:S(2)}) collective-permute-start(bf16[4,36,16,128]{3,2,1,0:T(8,128)(2,1)S(1)} %slice_dynamic-update-slice_fusion.2.mine), channel_id=1, source_target_pairs={{0,32},{32,0},{1,33},{33,1},{2,34},{34,2},{3,35},{35,3},{4,36},{36... | collective-permute-start | bytes 1769480 | tf_op jit(solution)/shard_map/ppermute | solution.py:259
  16.5 3.3 %collective-permute-start.6 = (bf16[864,128]{1,0:T(8,128)(2,1)S(1)}, bf16[864,128]{1,0:T(8,128)(2,1)}, u32[]{:S(2)}, u32[]{:S(2)}) collective-permute-start(bf16[864,128]{1,0:T(8,128)(2,1)S(1)} %slice.53), channel_id=1, source_target_pairs={{0,192},{64,0},{128,64},{192,128},{1,193},{65,1},{129,65},{193,129... | collective-permute-start | bytes 663560 | tf_op jit(solution)/shard_map/ppermute | solution.py:255
  20.0 2.2 %collective-permute-start.8 = (bf16[1728,128]{1,0:T(8,128)(2,1)S(1)}, bf16[1728,128]{1,0:T(8,128)(2,1)S(1)}, u32[]{:S(2)}, u32[]{:S(2)}) collective-permute-start(bf16[1728,128]{1,0:T(8,128)(2,1)S(1)} %collective-permute-done.4.r3), channel_id=1, source_target_pairs={{0,32},{32,0},{1,33},{33,1},{2,34},{34,2},{3,35},{35,3},{4,36},{36... | collective-permute-start | bytes 1327112 | tf_op jit(solution)/shard_map/ppermute | solution.py:259
  22.7 2.8 %collective-permute-start.10 = (bf16[864,128]{1,0:T(8,128)(2,1)}, bf16[864,128]{1,0:T(8,128)(2,1)}, u32[]{:S(2)}, u32[]{:S(2)}) collective-permute-start(bf16[864,128]{1,0:T(8,128)(2,1)} %collective-permute-done.6.rb), channel_id=1, source_target_pairs={{0,32},{32,0},{1,33},{33,1},{2,34},{34,2},{3,35},{35,3},{4,36},{36... | collective-permute-start | bytes 663560 | tf_op jit(solution)/shard_map/ppermute | solution.py:259
  26.0 3.3 %collective-permute-start.9 = (bf16[864,128]{1,0:T(8,128)(2,1)}, bf16[864,128]{1,0:T(8,128)(2,1)}, u32[]{:S(2)}, u32[]{:S(2)}) collective-permute-start(bf16[864,128]{1,0:T(8,128)(2,1)} %collective-permute-done.5.ra), channel_id=1, source_target_pairs={{0,32},{32,0},{1,33},{33,1},{2,34},{34,2},{3,35},{35,3},{4,36},{36... | collective-permute-start | bytes 663560 | tf_op jit(solution)/shard_map/ppermute | solution.py:259
  29.4 1.4 %collective-permute-done.9.qa = bf16[864,128]{1,0:T(8,128)(2,1)} collective-permute-done((bf16[864,128]{1,0:T(8,128)(2,1)}, bf16[864,128]{1,0:T(8,128)(2,1)}, u32[]{:S(2)}, u32[]{:S(2)}) %collective-permute-start.9) | collective-permute-done | bytes 221216 | tf_op jit(solution)/shard_map/ppermute | solution.py:259
  30.8 14.2 %layers.1 = (bf16[1280,128]{1,0:T(8,128)(2,1)S(1)}, bf16[1280,128]{1,0:T(8,128)(2,1)S(1)}, bf16[640,128]{1,0:T(8,128)(2,1)S(1)}, bf16[640,128]{1,0:T(8,128)(2,1)S(1)}, bf16[1280,128]{1,0:T(8,128)(2,1)S(1)}) custom-call(s32[3]{0:T(128)S(1)} %pad_add_fusion.pos, bf16[4,36,16,128]{3,2,1,0:T(8,128)(2,1)S(1)} %slice_dynamic-update-slice_fusion.2.mine, ...), custom_call_target="tpu_custom_call" | custom-call | flops 8999999488 | bytes 6000000 | tf_op jit(solution)/shard_map/layers/pallas_call | solution.py:205
  45.1 2.7 %collective-permute-start.15 = (bf16[640,128]{1,0:T(8,128)(2,1)S(1)}, bf16[640,128]{1,0:T(8,128)(2,1)S(1)}, u32[]{:S(2)}, u32[]{:S(2)}) collective-permute-start(bf16[640,128]{1,0:T(8,128)(2,1)S(1)} %get-tuple-element.16), channel_id=1, source_target_pairs={{0,192},{64,0},{128,64},{192,128},{1,193},{65,1},{129,65},{193,129... | collective-permute-start | bytes 491528 | tf_op jit(solution)/shard_map/ppermute | solution.py:255
  47.7 2.7 %collective-permute-start.12 = (bf16[1280,128]{1,0:T(8,128)(2,1)S(1)}, bf16[1280,128]{1,0:T(8,128)(2,1)S(1)}, u32[]{:S(2)}, u32[]{:S(2)}) collective-permute-start(bf16[1280,128]{1,0:T(8,128)(2,1)S(1)} %get-tuple-element.14), channel_id=1, source_target_pairs={{0,192},{64,0},{128,64},{192,128},{1,193},{65,1},{129,65},{193,129... | collective-permute-start | bytes 983048 | tf_op jit(solution)/shard_map/ppermute | solution.py:255
  51.7 2.7 %collective-permute-start.16 = (bf16[640,128]{1,0:T(8,128)(2,1)S(1)}, bf16[640,128]{1,0:T(8,128)(2,1)S(1)}, u32[]{:S(2)}, u32[]{:S(2)}) collective-permute-start(bf16[640,128]{1,0:T(8,128)(2,1)S(1)} %collective-permute-done.15), channel_id=1, source_target_pairs={{0,192},{64,0},{128,64},{192,128},{1,193},{65,1},{129,65},{193,129... | collective-permute-start | bytes 491528 | tf_op jit(solution)/shard_map/ppermute | solution.py:255
  54.4 7.9 %collective-permute-done.14.ea = bf16[640,128]{1,0:T(8,128)(2,1)S(1)} collective-permute-done((bf16[640,128]{1,0:T(8,128)(2,1)S(1)}, bf16[640,128]{1,0:T(8,128)(2,1)S(1)}, u32[]{:S(2)}, u32[]{:S(2)}) %collective-permute-start.14) | collective-permute-done | bytes 163872 | tf_op jit(solution)/shard_map/ppermute | solution.py:255
  62.2 3.6 %kernel_grad.1 = (f32[1728,128]{1,0:T(8,128)S(1)}, bf16[1728,128]{1,0:T(8,128)(2,1)S(1)}) custom-call(s32[3]{0:T(128)S(1)} %pad_add_fusion.pos, bf16[1280,128]{1,0:T(8,128)(2,1)S(1)} %get-tuple-element.12.e0, bf16[1280,128]{1,0:T(8,128)(2,1)S(1)} %collective-permute-done.11.e1, bf16[1280,128]{1,0:T(8,128)(2,1)S(1)} %collective-permute-done.12.e3, ...), custom_call_target="tpu_custom_call" | custom-call | flops 1800000000 | bytes 4000000 | tf_op jit(solution)/shard_map/kernel_grad/pallas_call | solution.py:228
  67.1 1.4 %collective-permute-done.17 = bf16[1728,128]{1,0:T(8,128)(2,1)S(1)} collective-permute-done((bf16[1728,128]{1,0:T(8,128)(2,1)S(1)}, bf16[1728,128]{1,0:T(8,128)(2,1)S(1)}, u32[]{:S(2)}, u32[]{:S(2)}) %collective-permute-start.17) | collective-permute-done | bytes 442400 | tf_op jit(solution)/shard_map/ppermute | solution.py:259
  68.6 13.4 %all_to_all.20 = bf16[4,432,128]{2,1,0:T(8,128)(2,1)S(1)} all-to-all(bf16[4,432,128]{2,1,0:T(8,128)(2,1)S(1)} %bitcast.21), channel_id=1, replica_groups=mesh['segment'=4,'tm'=2,'z'=8,'y'=4] {'y'}, dimensions={0} | all-to-all | bytes 884736 | tf_op jit(solution)/shard_map/all_to_all | solution.py:296
  82.1 15.7 %all_to_all.21 = bf16[8,64,128]{2,1,0:T(8,128)(2,1)S(1)} all-to-all(bf16[8,64,128]{2,1,0:T(8,128)(2,1)S(1)} %bitcast.23), channel_id=1, replica_groups=mesh['segment'=4,'tm'=2,'z'=8,'y'=4] {'z'}, dimensions={0} | all-to-all | bytes 262144 | tf_op jit(solution)/shard_map/all_to_all | solution.py:300
  97.9 10.3 %all_to_all.22 = bf16[8,64,128]{2,1,0:T(8,128)(2,1)S(1)} all-to-all(bf16[8,64,128]{2,1,0:T(8,128)(2,1)S(1)} %broadcast_in_dim.7), channel_id=1, replica_groups=mesh['segment'=4,'tm'=2,'z'=8,'y'=4] {'z'}, dimensions={0} | all-to-all | bytes 262144 | tf_op jit(solution)/shard_map/all_to_all | solution.py:302
  108.3 8.9 %all_to_all.23 = bf16[4,432,128]{2,1,0:T(8,128)(2,1)S(1)} all-to-all(bf16[4,432,128]{2,1,0:T(8,128)(2,1)S(1)} %broadcast_in_dim.8), channel_id=1, replica_groups=mesh['segment'=4,'tm'=2,'z'=8,'y'=4] {'y'}, dimensions={0} | all-to-all | bytes 884736 | tf_op jit(solution)/shard_map/all_to_all | solution.py:304
  117.2 5.2 %collective-permute-start.18 = (bf16[1728,128]{1,0:T(8,128)(2,1)S(1)}, bf16[1728,128]{1,0:T(8,128)(2,1)S(1)}, u32[]{:S(2)}, u32[]{:S(2)}) collective-permute-start(bf16[1728,128]{1,0:T(8,128)(2,1)S(1)} %bitcast.22), channel_id=1, source_target_pairs={{0,32},{32,0},{1,33},{33,1},{2,34},{34,2},{3,35},{35,3},{4,36},{36... | collective-permute-start | bytes 1327112 | tf_op jit(solution)/shard_map/ppermute | solution.py:259
  122.4 1.4 %collective-permute-done.18 = bf16[1728,128]{1,0:T(8,128)(2,1)S(1)} collective-permute-done((bf16[1728,128]{1,0:T(8,128)(2,1)S(1)}, bf16[1728,128]{1,0:T(8,128)(2,1)S(1)}, u32[]{:S(2)}, u32[]{:S(2)}) %collective-permute-start.18) | collective-permute-done | bytes 442400 | tf_op jit(solution)/shard_map/ppermute | solution.py:259
  123.9 1.3 %maximum_convert_fusion = f32[1,3456,128]{2,1,0:T(8,128)} fusion(bf16[1,1728,128]{2,1,0:T(8,128)(2,1)S(1)} %get-tuple-element.20, bf16[1,1728,128]{2,1,0:T(8,128)(2,1)S(1)} %get-tuple-element.19), kind=kLoop, calls=%fused_computation | loop fusion | flops 1769472 | bytes 2654208 | tf_op jit(solution)/shard_map/convert_element_type | solution.py:309
  (46 shorter events, 5.6 us)
Async XLA Ops:
  0.0 5.2 %copy-start = (bf16[1,3456,128]{2,1,0:T(8,128)(2,1)S(1)}, bf16[1,3456,128]{2,1,0:T(8,128)(2,1)}, u32[]{:S(2)}) copy-start(bf16[1,3456,128]{2,1,0:T(8,128)(2,1)} %param.4) | copy-start | bytes 2654212
  1.2 8.0 %collective-permute-start = (bf16[4,10,16,128]{3,2,1,0:T(8,128)(2,1)S(1)}, bf16[4,10,16,128]{3,2,1,0:T(8,128)(2,1)S(1)}, u32[]{:S(2)}, u32[]{:S(2)}) collective-permute-start(bf16[4,10,16,128]{3,2,1,0:T(8,128)(2,1)S(1)} %pad_maximum_fusion), channel_id=1, source_target_pairs={{0,1},{1,2},{2,3},{3,4},{4,5},{5,6},{6,7},{7,8},{8,9},{9,10},{10,1... | collective-permute-start | bytes 491528 | tf_op jit(solution)/shard_map/ppermute | solution.py:280
  5.3 11.3 %collective-permute-start.4 = (bf16[1728,128]{1,0:T(8,128)(2,1)S(1)}, bf16[1728,128]{1,0:T(8,128)(2,1)S(1)}, u32[]{:S(2)}, u32[]{:S(2)}) collective-permute-start(bf16[1728,128]{1,0:T(8,128)(2,1)S(1)} %dynamic-slice_bitcast_fusion), channel_id=1, source_target_pairs={{0,192},{64,0},{128,64},{192,128},{1,193},{65,1},{129,65},{193,129... | collective-permute-start | bytes 1327112 | tf_op jit(solution)/shard_map/ppermute | solution.py:255
  7.8 12.0 %collective-permute-start.3 = (bf16[1728,128]{1,0:T(8,128)(2,1)S(1)}, bf16[1728,128]{1,0:T(8,128)(2,1)S(1)}, u32[]{:S(2)}, u32[]{:S(2)}) collective-permute-start(bf16[1728,128]{1,0:T(8,128)(2,1)S(1)} %dynamic-slice_bitcast_fusion), channel_id=1, source_target_pairs={{0,64},{64,128},{128,192},{192,0},{1,65},{65,129},{129,193},{193,1... | collective-permute-start | bytes 1327112 | tf_op jit(solution)/shard_map/ppermute | solution.py:255
  7.8 6.4 %collective-permute-start.1 = (bf16[4,10,16,128]{3,2,1,0:T(8,128)(2,1)S(1)}, bf16[4,10,16,128]{3,2,1,0:T(8,128)(2,1)S(1)}, u32[]{:S(2)}, u32[]{:S(2)}) collective-permute-start(bf16[4,10,16,128]{3,2,1,0:T(8,128)(2,1)S(1)} %pad_maximum_fusion.1), channel_id=1, source_target_pairs={{1,0},{2,1},{3,2},{4,3},{5,4},{6,5},{7,6},{8,7},{9,8},{10,9},{11,1... | collective-permute-start | bytes 491528 | tf_op jit(solution)/shard_map/ppermute | solution.py:283
  14.3 15.1 %collective-permute-start.2 = (bf16[4,36,16,128]{3,2,1,0:T(8,128)(2,1)S(1)}, bf16[4,36,16,128]{3,2,1,0:T(8,128)(2,1)S(1)}, u32[]{:S(2)}, u32[]{:S(2)}) collective-permute-start(bf16[4,36,16,128]{3,2,1,0:T(8,128)(2,1)S(1)} %slice_dynamic-update-slice_fusion.2.mine), channel_id=1, source_target_pairs={{0,32},{32,0},{1,33},{33,1},{2,34},{34,2},{3,35},{35,3},{4,36},{36... | collective-permute-start | bytes 1769480 | tf_op jit(solution)/shard_map/ppermute | solution.py:259
  16.5 6.2 %collective-permute-start.6 = (bf16[864,128]{1,0:T(8,128)(2,1)S(1)}, bf16[864,128]{1,0:T(8,128)(2,1)}, u32[]{:S(2)}, u32[]{:S(2)}) collective-permute-start(bf16[864,128]{1,0:T(8,128)(2,1)S(1)} %slice.53), channel_id=1, source_target_pairs={{0,192},{64,0},{128,64},{192,128},{1,193},{65,1},{129,65},{193,129... | collective-permute-start | bytes 663560 | tf_op jit(solution)/shard_map/ppermute | solution.py:255
  19.9 6.2 %collective-permute-start.5 = (bf16[864,128]{1,0:T(8,128)(2,1)S(1)}, bf16[864,128]{1,0:T(8,128)(2,1)}, u32[]{:S(2)}, u32[]{:S(2)}) collective-permute-start(bf16[864,128]{1,0:T(8,128)(2,1)S(1)} %slice.52), channel_id=1, source_target_pairs={{0,64},{64,128},{128,192},{192,0},{1,65},{65,129},{129,193},{193,1... | collective-permute-start | bytes 663560 | tf_op jit(solution)/shard_map/ppermute | solution.py:255
  20.0 9.5 %collective-permute-start.8 = (bf16[1728,128]{1,0:T(8,128)(2,1)S(1)}, bf16[1728,128]{1,0:T(8,128)(2,1)S(1)}, u32[]{:S(2)}, u32[]{:S(2)}) collective-permute-start(bf16[1728,128]{1,0:T(8,128)(2,1)S(1)} %collective-permute-done.4.r3), channel_id=1, source_target_pairs={{0,32},{32,0},{1,33},{33,1},{2,34},{34,2},{3,35},{35,3},{4,36},{36... | collective-permute-start | bytes 1327112 | tf_op jit(solution)/shard_map/ppermute | solution.py:259
  22.2 8.6 %collective-permute-start.7 = (bf16[1728,128]{1,0:T(8,128)(2,1)S(1)}, bf16[1728,128]{1,0:T(8,128)(2,1)}, u32[]{:S(2)}, u32[]{:S(2)}) collective-permute-start(bf16[1728,128]{1,0:T(8,128)(2,1)S(1)} %collective-permute-done.3.r1), channel_id=1, source_target_pairs={{0,32},{32,0},{1,33},{33,1},{2,34},{34,2},{3,35},{35,3},{4,36},{36... | collective-permute-start | bytes 1327112 | tf_op jit(solution)/shard_map/ppermute | solution.py:259
  22.7 6.7 %collective-permute-start.10 = (bf16[864,128]{1,0:T(8,128)(2,1)}, bf16[864,128]{1,0:T(8,128)(2,1)}, u32[]{:S(2)}, u32[]{:S(2)}) collective-permute-start(bf16[864,128]{1,0:T(8,128)(2,1)} %collective-permute-done.6.rb), channel_id=1, source_target_pairs={{0,32},{32,0},{1,33},{33,1},{2,34},{34,2},{3,35},{35,3},{4,36},{36... | collective-permute-start | bytes 663560 | tf_op jit(solution)/shard_map/ppermute | solution.py:259
  26.0 4.7 %collective-permute-start.9 = (bf16[864,128]{1,0:T(8,128)(2,1)}, bf16[864,128]{1,0:T(8,128)(2,1)}, u32[]{:S(2)}, u32[]{:S(2)}) collective-permute-start(bf16[864,128]{1,0:T(8,128)(2,1)} %collective-permute-done.5.ra), channel_id=1, source_target_pairs={{0,32},{32,0},{1,33},{33,1},{2,34},{34,2},{3,35},{35,3},{4,36},{36... | collective-permute-start | bytes 663560 | tf_op jit(solution)/shard_map/ppermute | solution.py:259
  45.0 6.7 %collective-permute-start.13 = (bf16[640,128]{1,0:T(8,128)(2,1)S(1)}, bf16[640,128]{1,0:T(8,128)(2,1)S(1)}, u32[]{:S(2)}, u32[]{:S(2)}) collective-permute-start(bf16[640,128]{1,0:T(8,128)(2,1)S(1)} %get-tuple-element.15), channel_id=1, source_target_pairs={{0,64},{64,128},{128,192},{192,0},{1,65},{65,129},{129,193},{193,1... | collective-permute-start | bytes 491528 | tf_op jit(solution)/shard_map/ppermute | solution.py:255
  45.1 6.6 %collective-permute-start.15 = (bf16[640,128]{1,0:T(8,128)(2,1)S(1)}, bf16[640,128]{1,0:T(8,128)(2,1)S(1)}, u32[]{:S(2)}, u32[]{:S(2)}) collective-permute-start(bf16[640,128]{1,0:T(8,128)(2,1)S(1)} %get-tuple-element.16), channel_id=1, source_target_pairs={{0,192},{64,0},{128,64},{192,128},{1,193},{65,1},{129,65},{193,129... | collective-permute-start | bytes 491528 | tf_op jit(solution)/shard_map/ppermute | solution.py:255
  47.7 14.5 %collective-permute-start.11 = (bf16[1280,128]{1,0:T(8,128)(2,1)S(1)}, bf16[1280,128]{1,0:T(8,128)(2,1)S(1)}, u32[]{:S(2)}, u32[]{:S(2)}) collective-permute-start(bf16[1280,128]{1,0:T(8,128)(2,1)S(1)} %get-tuple-element.13), channel_id=1, source_target_pairs={{0,64},{64,128},{128,192},{192,0},{1,65},{65,129},{129,193},{193,1... | collective-permute-start | bytes 983048 | tf_op jit(solution)/shard_map/ppermute | solution.py:255
  47.7 14.5 %collective-permute-start.12 = (bf16[1280,128]{1,0:T(8,128)(2,1)S(1)}, bf16[1280,128]{1,0:T(8,128)(2,1)S(1)}, u32[]{:S(2)}, u32[]{:S(2)}) collective-permute-start(bf16[1280,128]{1,0:T(8,128)(2,1)S(1)} %get-tuple-element.14), channel_id=1, source_target_pairs={{0,192},{64,0},{128,64},{192,128},{1,193},{65,1},{129,65},{193,129... | collective-permute-start | bytes 983048 | tf_op jit(solution)/shard_map/ppermute | solution.py:255
  51.7 10.5 %collective-permute-start.14 = (bf16[640,128]{1,0:T(8,128)(2,1)S(1)}, bf16[640,128]{1,0:T(8,128)(2,1)S(1)}, u32[]{:S(2)}, u32[]{:S(2)}) collective-permute-start(bf16[640,128]{1,0:T(8,128)(2,1)S(1)} %collective-permute-done.13), channel_id=1, source_target_pairs={{0,64},{64,128},{128,192},{192,0},{1,65},{65,129},{129,193},{193,1... | collective-permute-start | bytes 491528 | tf_op jit(solution)/shard_map/ppermute | solution.py:255
  51.7 10.5 %collective-permute-start.16 = (bf16[640,128]{1,0:T(8,128)(2,1)S(1)}, bf16[640,128]{1,0:T(8,128)(2,1)S(1)}, u32[]{:S(2)}, u32[]{:S(2)}) collective-permute-start(bf16[640,128]{1,0:T(8,128)(2,1)S(1)} %collective-permute-done.15), channel_id=1, source_target_pairs={{0,192},{64,0},{128,64},{192,128},{1,193},{65,1},{129,65},{193,129... | collective-permute-start | bytes 491528 | tf_op jit(solution)/shard_map/ppermute | solution.py:255
  65.8 2.7 %collective-permute-start.17 = (bf16[1728,128]{1,0:T(8,128)(2,1)S(1)}, bf16[1728,128]{1,0:T(8,128)(2,1)S(1)}, u32[]{:S(2)}, u32[]{:S(2)}) collective-permute-start(bf16[1728,128]{1,0:T(8,128)(2,1)S(1)} %get-tuple-element.18), channel_id=1, source_target_pairs={{0,32},{32,0},{1,33},{33,1},{2,34},{34,2},{3,35},{35,3},{4,36},{36... | collective-permute-start | bytes 1327112 | tf_op jit(solution)/shard_map/ppermute | solution.py:259
  117.2 6.6 %collective-permute-start.18 = (bf16[1728,128]{1,0:T(8,128)(2,1)S(1)}, bf16[1728,128]{1,0:T(8,128)(2,1)S(1)}, u32[]{:S(2)}, u32[]{:S(2)}) collective-permute-start(bf16[1728,128]{1,0:T(8,128)(2,1)S(1)} %bitcast.22), channel_id=1, source_target_pairs={{0,32},{32,0},{1,33},{33,1},{2,34},{34,2},{3,35},{35,3},{4,36},{36... | collective-permute-start | bytes 1327112 | tf_op jit(solution)/shard_map/ppermute | solution.py:259

commit v4 on v3

--- a/solution.py
+++ b/solution.py
@@ -60,7 +60,7 @@
 
 
 def layers_kernel(
-    total, pos, mine, other, w0, r1, r3, ra, rb, q1, q3, qa, qb, *rest
+    total, pos, mine, other, long, short, w0, r1, r3, ra, rb, q1, q3, qa, qb, *rest
 ):
     o0, o1, oa, ob, o3, wz, wb, cols, fac, grad, part = rest
     seg, tm, first = pos[0], pos[1], pos[2]
@@ -78,17 +78,35 @@
 
     span = OWN + 2 * HALO
     half_fr = FR // 2
-    for ref, which in ((mine, tm), (other, 1 - tm)):
+    band = 2 * OWN
+    near = HALO - OWN
+    upper = 1 - tm
+
+    def put(t, to, rows):
+        cells = rows.shape[0] * COLS
+        at = pl.multiple_of(to * COLS, COLS)
+        cols[0, t * 3 + 1, pl.ds(at, cells)] = rows.reshape(cells, CH)
+
+    def put_grad(t, to, rows):
+        cells = rows.shape[0] * COLS
+        at = pl.multiple_of(to * COLS, COLS)
+        grad[t, pl.ds(at, cells)] = rows.reshape(cells, CH).astype(F32)
+
+    for i, (ref, which) in enumerate(((mine, tm), (other, upper))):
 
         @pl.loop(0, half_fr)
         def _(t):
             frame = which * half_fr + t
-            rows = ref[t, pl.ds(tm * OWN, span)]
-            for lag_c, v in enumerate(shifted(rows.reshape(span * COLS, CH).astype(F32))):
-                cols[0, frame * 3 + lag_c] = v
-            at = 2 * HALO + 2 * OWN + tm * OWN
-            rows = ref[t, pl.ds(at, OWN + 2 * CHALO)]
-            grad[frame] = rows.reshape(-1, CH).astype(F32)
+            side = i * half_fr + t
+            put(frame, tm * (near + band), long[side, :HALO])
+            put(frame, near + upper * OWN, ref[t, :band])
+            put(frame, upper * (HALO + band), short[side])
+            for lag_c, v in enumerate(shifted(cols[0, frame * 3 + 1].astype(F32))):
+                if lag_c != 1:
+                    cols[0, frame * 3 + lag_c] = v
+            rest_rows = band - 1
+            put_grad(frame, upper * CHALO, ref[t, pl.ds(band + tm, rest_rows)])
+            put_grad(frame, tm * rest_rows, long[side, HALO:])
 
     width = (OWN + 2) * COLS
     own_cells = OWN * COLS
@@ -195,6 +213,37 @@
     send[...] = wg[pl.ds(pl.multiple_of((1 - tm) * HALF, CH // 2), HALF)].astype(BF16)
 
 
+def edges_kernel(pos, mine, other, long, short, start):
+    tm = pos[1]
+    start[0] = 0
+    half_fr = FR // 2
+    few = HALO - OWN
+    band = 2 * OWN
+    for i, ref in enumerate((mine, other)):
+        for t in range(half_fr):
+            side = i * half_fr + t
+            long[side, :HALO] = ref[t, pl.ds((1 - tm) * (band - HALO), HALO)]
+            long[side, HALO:] = ref[t, pl.ds(band + (1 - tm) * (band - CHALO), CHALO)]
+            short[side] = ref[t, pl.ds(tm * (band - few), few)]
+
+
+def run_edges(pos, mine, other):
+    return pl.pallas_call(
+        edges_kernel,
+        out_shape=(
+            jax.ShapeDtypeStruct((FR, HALO + CHALO, COLS, CH), BF16),
+            jax.ShapeDtypeStruct((FR, HALO - OWN, COLS, CH), BF16),
+            jax.ShapeDtypeStruct((1,), jnp.int32),
+        ),
+        in_specs=in_vmem(2),
+        out_specs=(pl.BlockSpec(memory_space=pltpu.VMEM),) * 2
+        + (pl.BlockSpec(memory_space=pltpu.SMEM),),
+        compiler_params=pltpu.CompilerParams(vmem_limit_bytes=8 * 2**20),
+        cost_estimate=pl.CostEstimate(flops=0, bytes_accessed=900_000, transcendentals=0),
+        name="edges",
+    )(pos, mine, other)
+
+
 def in_vmem(n):
     return [pl.BlockSpec(memory_space=pltpu.SMEM)] + [pl.BlockSpec(memory_space=pltpu.VMEM)] * n
 
@@ -215,7 +264,7 @@
             pltpu.VMEM((FR, (OWN + 2 * CHALO) * COLS, CH), F32),
             pltpu.VMEM((LAYERS, PART, CH), BF16),
         ],
-        compiler_params=pltpu.CompilerParams(vmem_limit_bytes=44 * 2**20),
+        compiler_params=pltpu.CompilerParams(vmem_limit_bytes=28 * 2**20),
         cost_estimate=pl.CostEstimate(
             flops=9_000_000_000, bytes_accessed=6_000_000, transcendentals=1_000_000
         ),
@@ -239,7 +288,7 @@
             pltpu.VMEM((cells, 3 * CH), BF16),
             pltpu.VMEM((KC, CH), F32),
         ],
-        compiler_params=pltpu.CompilerParams(vmem_limit_bytes=32 * 2**20),
+        compiler_params=pltpu.CompilerParams(vmem_limit_bytes=24 * 2**20),
         cost_estimate=pl.CostEstimate(
             flops=1_800_000_000, bytes_accessed=4_000_000, transcendentals=0
         ),
@@ -270,23 +319,23 @@
     w = weights[0]
     half = lax.dynamic_slice_in_dim(w, tm * HALF, HALF, 0)
     left, right = along(half, 1), along(half, -1)
-    got = [left, right, along(left[: HALF // 2], 1), along(right[HALF // 2 :], -1)]
-    crossed = [swap(g) for g in got]
 
     x = lax.dynamic_index_in_dim(inputs, seg, 0, keepdims=False)
     c = lax.dynamic_index_in_dim(cotangent, seg, 0, keepdims=False)
+    mine = jnp.concatenate([x, c], 1)
+    other = swap(mine)
+    long, short, start = run_edges(pos, mine, other)
     down = [(i, i + 1) for i in range(spaces - 1)]
     up = [(i + 1, i) for i in range(spaces - 1)]
-    before = lax.ppermute(
-        jnp.concatenate([x[:, rows - HALO :], c[:, rows - CHALO :]], 1), ("z", "y"), down
-    )
-    after = lax.ppermute(jnp.concatenate([x[:, :HALO], c[:, :CHALO]], 1), ("z", "y"), up)
-    mine = jnp.concatenate(
-        [before[:, :HALO], x, after[:, :HALO], before[:, HALO:], c, after[:, HALO:]], 1
-    )
-    other = swap(mine)
-
-    parts = run_layers(spaces * rows, pos, mine, other, w, *got, *crossed)
+    both = lambda low, high: low + [(spaces + i, spaces + j) for i, j in high]
+    long = lax.ppermute(long, ("tm", "z", "y"), both(down, up))
+    short = lax.ppermute(short, ("tm", "z", "y"), both(up, down))
+
+    cut = lambda v, at: lax.dynamic_slice_in_dim(v, at + start[0], HALF // 2, 0)
+    got = [left, right, along(cut(left, 0), 1), along(cut(right, HALF // 2), -1)]
+    crossed = [swap(g) for g in got]
+
+    parts = run_layers(spaces * rows, pos, mine, other, long, short, w, *got, *crossed)
     far_a, far_b = along(parts[2], 1), along(parts[3], -1)
     near = [along(parts[1], 1), along(parts[4], -1)]
     keep, send = run_kernel_grad(pos, parts[0], *near, along(far_a, 1), along(far_b, -1))

time: 126 us -> 128 us (1.016)
  between operations: 0.22 us -> 3.62 us
  waiting for transfers between devices: 19.3 us -> 16.7 us
  blocking collectives: 48.3 us -> 49.8 us
    ppermute x10, waiting for transfers between devices: 10.1 us -> 8.63 us  [along(): return lax.ppermute(x, 'segment', ring(LAYERS, by))]
  transfers between devices with their start and end apart: 19 -> 19, of which waited for: 8 -> 7; matrix products, arithmetic and copies ran while one was open for 0% -> 1% of each run, Pallas kernels for 0% -> 1%
where the time goes in v4:
time: 128 us
  blocking collectives  49.8 us (39%)
  starting transfers between devices  35.7 us (28%)
  Pallas kernels  18 us (14%)
  waiting for transfers between devices  16.7 us (13%)
  between operations  3.62 us (3%)
  local copies, waits for them, and re-layouts  2.34 us (2%)
  other arithmetic  1.7 us (1%)
    ppermute x7, starting transfers between devices, swap(): return lax.ppermute(x, 'tm', [(0, 1), (1, 0)])  16 us
    all_to_all x1, blocking collectives, body(): pieces = lax.all_to_all(total.reshape(nz, rows_z, CH), 'z', 0, 0)  15.9 us
    ppermute x10, starting transfers between devices, along(): return lax.ppermute(x, 'segment', ring(LAYERS, by))  15.3 us
    all_to_all x1, blocking collectives, body(): pieces = lax.all_to_all(total.reshape(ny, rows_y, CH), 'y', 0, 0)  14.7 us
    pallas_call x1, Pallas kernels, run_layers(): pl.pallas_call(functools.partial(layers_kernel, total), out_shape=tuple((...  13.4 us
    all_to_all x1, blocking collectives, body(): whole = lax.all_to_all(jnp.broadcast_to(total, (nz, rows_z, CH)), 'z', 0, 0)  10.3 us
    all_to_all x1, blocking collectives, body(): whole = lax.all_to_all(jnp.broadcast_to(whole, (ny, rows_y, CH)), 'y', 0, 0)  8.87 us
    ppermute x10, waiting for transfers between devices, along(): return lax.ppermute(x, 'segment', ring(LAYERS, by))  8.63 us
  transfers between devices with their start and end apart: 19, of which 7 were waited for; matrix products, arithmetic and copies ran while one was open for 1% of the time, Pallas kernels for 1%

profile of v4, /device:TPU:1, one launch (start us, length us, event | category | flops | bytes accessed | tf_op | source)
XLA Modules:
  0.0 127.8 jit_solution(13477277577457020444)
XLA Ops:
  1.1 3.4 %collective-permute-start.4 = (bf16[1728,128]{1,0:T(8,128)(2,1)S(1)}, bf16[1728,128]{1,0:T(8,128)(2,1)S(1)}, u32[]{:S(2)}, u32[]{:S(2)}) collective-permute-start(bf16[1728,128]{1,0:T(8,128)(2,1)S(1)} %dynamic-slice_bitcast_fusion), channel_id=1, source_target_pairs={{0,192},{64,0},{128,64},{192,128},{1,193},{65,1},{129,65},{193,129... | collective-permute-start | bytes 1327112 | tf_op jit(solution)/shard_map/ppermute | solution.py:304
  5.5 2.0 %collective-permute-start = (bf16[4,16,16,128]{3,2,1,0:T(8,128)(2,1)S(1)}, bf16[4,16,16,128]{3,2,1,0:T(8,128)(2,1)S(1)}, u32[]{:S(2)}, u32[]{:S(2)}) collective-permute-start(bf16[4,16,16,128]{3,2,1,0:T(8,128)(2,1)S(1)} %pad_maximum_fusion.mine), channel_id=1, source_target_pairs={{0,32},{32,0},{1,33},{33,1},{2,34},{34,2},{3,35},{35,3},{4,36},{36... | collective-permute-start | bytes 786440 | tf_op jit(solution)/shard_map/ppermute | solution.py:308
  13.4 3.5 %collective-permute-start.6 = (bf16[864,128]{1,0:T(8,128)(2,1)S(1)}, bf16[864,128]{1,0:T(8,128)(2,1)S(1)}, u32[]{:S(2)}, u32[]{:S(2)}) collective-permute-start(bf16[864,128]{1,0:T(8,128)(2,1)S(1)} %constant_dynamic-slice_fusion), channel_id=1, source_target_pairs={{0,192},{64,0},{128,64},{192,128},{1,193},{65,1},{129,65},{193,129... | collective-permute-start | bytes 663560 | tf_op jit(solution)/shard_map/ppermute | solution.py:304
  17.1 1.9 %collective-permute-start.8 = (bf16[1728,128]{1,0:T(8,128)(2,1)S(1)}, bf16[1728,128]{1,0:T(8,128)(2,1)S(1)}, u32[]{:S(2)}, u32[]{:S(2)}) collective-permute-start(bf16[1728,128]{1,0:T(8,128)(2,1)S(1)} %collective-permute-done.4.r3), channel_id=1, source_target_pairs={{0,32},{32,0},{1,33},{33,1},{2,34},{34,2},{3,35},{35,3},{4,36},{36... | collective-permute-start | bytes 1327112 | tf_op jit(solution)/shard_map/ppermute | solution.py:308
  19.1 3.2 %collective-permute-start.2 = (bf16[8,3,16,128]{3,2,1,0:T(8,128)(2,1)S(1)}, bf16[8,3,16,128]{3,2,1,0:T(8,128)(2,1)S(1)}, u32[]{:S(2)}, u32[]{:S(2)}) collective-permute-start(bf16[8,3,16,128]{3,2,1,0:T(8,128)(2,1)S(1)} %get-tuple-element.16), channel_id=1, source_target_pairs={{1,0},{2,1},{3,2},{4,3},{5,4},{6,5},{7,6},{8,7},{9,8},{10,9},{11,1... | collective-permute-start | bytes 294920 | tf_op jit(solution)/shard_map/ppermute | solution.py:332
  22.3 1.6 %collective-permute-done.2.short = bf16[8,3,16,128]{3,2,1,0:T(8,128)(2,1)S(1)} collective-permute-done((bf16[8,3,16,128]{3,2,1,0:T(8,128)(2,1)S(1)}, bf16[8,3,16,128]{3,2,1,0:T(8,128)(2,1)S(1)}, u32[]{:S(2)}, u32[]{:S(2)}) %collective-permute-start.2) | collective-permute-done | bytes 98336 | tf_op jit(solution)/shard_map/ppermute | solution.py:332
  23.9 1.3 %collective-permute-start.1 = (bf16[8,10,16,128]{3,2,1,0:T(8,128)(2,1)S(1)}, bf16[8,10,16,128]{3,2,1,0:T(8,128)(2,1)S(1)}, u32[]{:S(2)}, u32[]{:S(2)}) collective-permute-start(bf16[8,10,16,128]{3,2,1,0:T(8,128)(2,1)S(1)} %get-tuple-element.15), channel_id=1, source_target_pairs={{0,1},{1,2},{2,3},{3,4},{4,5},{5,6},{6,7},{7,8},{8,9},{9,10},{10,1... | collective-permute-start | bytes 983048 | tf_op jit(solution)/shard_map/ppermute | solution.py:331
  25.2 4.4 %collective-permute-start.10 = (bf16[864,128]{1,0:T(8,128)(2,1)S(1)}, bf16[864,128]{1,0:T(8,128)(2,1)S(1)}, u32[]{:S(2)}, u32[]{:S(2)}) collective-permute-start(bf16[864,128]{1,0:T(8,128)(2,1)S(1)} %collective-permute-done.6.rb), channel_id=1, source_target_pairs={{0,32},{32,0},{1,33},{33,1},{2,34},{34,2},{3,35},{35,3},{4,36},{36... | collective-permute-start | bytes 663560 | tf_op jit(solution)/shard_map/ppermute | solution.py:308
  29.9 2.5 %collective-permute-done.1.long = bf16[8,10,16,128]{3,2,1,0:T(8,128)(2,1)S(1)} collective-permute-done((bf16[8,10,16,128]{3,2,1,0:T(8,128)(2,1)S(1)}, bf16[8,10,16,128]{3,2,1,0:T(8,128)(2,1)S(1)}, u32[]{:S(2)}, u32[]{:S(2)}) %collective-permute-start.1) | collective-permute-done | bytes 327712 | tf_op jit(solution)/shard_map/ppermute | solution.py:331
  32.4 13.4 %layers.1 = (bf16[1280,128]{1,0:T(8,128)(2,1)S(1)}, bf16[1280,128]{1,0:T(8,128)(2,1)S(1)}, bf16[640,128]{1,0:T(8,128)(2,1)S(1)}, bf16[640,128]{1,0:T(8,128)(2,1)S(1)}, bf16[1280,128]{1,0:T(8,128)(2,1)S(1)}) custom-call(s32[3]{0:T(128)S(1)} %pad_add_fusion.pos, bf16[4,16,16,128]{3,2,1,0:T(8,128)(2,1)S(1)} %pad_maximum_fusion.mine, ...), custom_call_target="tpu_custom_call" | custom-call | flops 8999999488 | bytes 6000000 | tf_op jit(solution)/shard_map/layers/pallas_call | solution.py:254
  45.9 2.9 %collective-permute-start.15 = (bf16[640,128]{1,0:T(8,128)(2,1)S(1)}, bf16[640,128]{1,0:T(8,128)(2,1)S(1)}, u32[]{:S(2)}, u32[]{:S(2)}) collective-permute-start(bf16[640,128]{1,0:T(8,128)(2,1)S(1)} %get-tuple-element.22), channel_id=1, source_target_pairs={{0,192},{64,0},{128,64},{192,128},{1,193},{65,1},{129,65},{193,129... | collective-permute-start | bytes 491528 | tf_op jit(solution)/shard_map/ppermute | solution.py:304
  48.8 2.7 %collective-permute-start.12 = (bf16[1280,128]{1,0:T(8,128)(2,1)S(1)}, bf16[1280,128]{1,0:T(8,128)(2,1)S(1)}, u32[]{:S(2)}, u32[]{:S(2)}) collective-permute-start(bf16[1280,128]{1,0:T(8,128)(2,1)S(1)} %get-tuple-element.20), channel_id=1, source_target_pairs={{0,192},{64,0},{128,64},{192,128},{1,193},{65,1},{129,65},{193,129... | collective-permute-start | bytes 983048 | tf_op jit(solution)/shard_map/ppermute | solution.py:304
  51.4 2.7 %collective-permute-start.16 = (bf16[640,128]{1,0:T(8,128)(2,1)S(1)}, bf16[640,128]{1,0:T(8,128)(2,1)S(1)}, u32[]{:S(2)}, u32[]{:S(2)}) collective-permute-start(bf16[640,128]{1,0:T(8,128)(2,1)S(1)} %collective-permute-done.15), channel_id=1, source_target_pairs={{0,192},{64,0},{128,64},{192,128},{1,193},{65,1},{129,65},{193,129... | collective-permute-start | bytes 491528 | tf_op jit(solution)/shard_map/ppermute | solution.py:304
  54.1 8.5 %collective-permute-done.14.ea = bf16[640,128]{1,0:T(8,128)(2,1)S(1)} collective-permute-done((bf16[640,128]{1,0:T(8,128)(2,1)S(1)}, bf16[640,128]{1,0:T(8,128)(2,1)S(1)}, u32[]{:S(2)}, u32[]{:S(2)}) %collective-permute-start.14) | collective-permute-done | bytes 163872 | tf_op jit(solution)/shard_map/ppermute | solution.py:304
  62.7 3.5 %kernel_grad.1 = (f32[1728,128]{1,0:T(8,128)S(1)}, bf16[1728,128]{1,0:T(8,128)(2,1)S(1)}) custom-call(s32[3]{0:T(128)S(1)} %pad_add_fusion.pos, bf16[1280,128]{1,0:T(8,128)(2,1)S(1)} %get-tuple-element.18.e0, bf16[1280,128]{1,0:T(8,128)(2,1)S(1)} %collective-permute-done.11.e1, bf16[1280,128]{1,0:T(8,128)(2,1)S(1)} %collective-permute-done.12.e3, ...), custom_call_target="tpu_custom_call" | custom-call | flops 1800000000 | bytes 4000000 | tf_op jit(solution)/shard_map/kernel_grad/pallas_call | solution.py:277
  66.2 2.0 %collective-permute-start.17 = (bf16[1728,128]{1,0:T(8,128)(2,1)S(1)}, bf16[1728,128]{1,0:T(8,128)(2,1)S(1)}, u32[]{:S(2)}, u32[]{:S(2)}) collective-permute-start(bf16[1728,128]{1,0:T(8,128)(2,1)S(1)} %get-tuple-element.24), channel_id=1, source_target_pairs={{0,32},{32,0},{1,33},{33,1},{2,34},{34,2},{3,35},{35,3},{4,36},{36... | collective-permute-start | bytes 1327112 | tf_op jit(solution)/shard_map/ppermute | solution.py:308
  68.3 1.4 %collective-permute-done.17 = bf16[1728,128]{1,0:T(8,128)(2,1)S(1)} collective-permute-done((bf16[1728,128]{1,0:T(8,128)(2,1)S(1)}, bf16[1728,128]{1,0:T(8,128)(2,1)S(1)}, u32[]{:S(2)}, u32[]{:S(2)}) %collective-permute-start.17) | collective-permute-done | bytes 442400 | tf_op jit(solution)/shard_map/ppermute | solution.py:308
  69.8 14.7 %all_to_all.20 = bf16[4,432,128]{2,1,0:T(8,128)(2,1)S(1)} all-to-all(bf16[4,432,128]{2,1,0:T(8,128)(2,1)S(1)} %bitcast.22), channel_id=1, replica_groups=mesh['segment'=4,'tm'=2,'z'=8,'y'=4] {'y'}, dimensions={0} | all-to-all | bytes 884736 | tf_op jit(solution)/shard_map/all_to_all | solution.py:345
  84.5 15.9 %all_to_all.21 = bf16[8,64,128]{2,1,0:T(8,128)(2,1)S(1)} all-to-all(bf16[8,64,128]{2,1,0:T(8,128)(2,1)S(1)} %bitcast.24), channel_id=1, replica_groups=mesh['segment'=4,'tm'=2,'z'=8,'y'=4] {'z'}, dimensions={0} | all-to-all | bytes 262144 | tf_op jit(solution)/shard_map/all_to_all | solution.py:349
  100.5 10.3 %all_to_all.22 = bf16[8,64,128]{2,1,0:T(8,128)(2,1)S(1)} all-to-all(bf16[8,64,128]{2,1,0:T(8,128)(2,1)S(1)} %broadcast_in_dim.7), channel_id=1, replica_groups=mesh['segment'=4,'tm'=2,'z'=8,'y'=4] {'z'}, dimensions={0} | all-to-all | bytes 262144 | tf_op jit(solution)/shard_map/all_to_all | solution.py:351
  110.9 8.9 %all_to_all.23 = bf16[4,432,128]{2,1,0:T(8,128)(2,1)S(1)} all-to-all(bf16[4,432,128]{2,1,0:T(8,128)(2,1)S(1)} %broadcast_in_dim.8), channel_id=1, replica_groups=mesh['segment'=4,'tm'=2,'z'=8,'y'=4] {'y'}, dimensions={0} | all-to-all | bytes 884736 | tf_op jit(solution)/shard_map/all_to_all | solution.py:353
  119.8 5.2 %collective-permute-start.18 = (bf16[1728,128]{1,0:T(8,128)(2,1)S(1)}, bf16[1728,128]{1,0:T(8,128)(2,1)S(1)}, u32[]{:S(2)}, u32[]{:S(2)}) collective-permute-start(bf16[1728,128]{1,0:T(8,128)(2,1)S(1)} %bitcast.23), channel_id=1, source_target_pairs={{0,32},{32,0},{1,33},{33,1},{2,34},{34,2},{3,35},{35,3},{4,36},{36... | collective-permute-start | bytes 1327112 | tf_op jit(solution)/shard_map/ppermute | solution.py:308
  125.0 1.4 %collective-permute-done.18 = bf16[1728,128]{1,0:T(8,128)(2,1)S(1)} collective-permute-done((bf16[1728,128]{1,0:T(8,128)(2,1)S(1)}, bf16[1728,128]{1,0:T(8,128)(2,1)S(1)}, u32[]{:S(2)}, u32[]{:S(2)}) %collective-permute-start.18) | collective-permute-done | bytes 442400 | tf_op jit(solution)/shard_map/ppermute | solution.py:308
  126.5 1.3 %maximum_convert_fusion = f32[1,3456,128]{2,1,0:T(8,128)} fusion(bf16[1,1728,128]{2,1,0:T(8,128)(2,1)S(1)} %get-tuple-element.26, bf16[1,1728,128]{2,1,0:T(8,128)(2,1)S(1)} %get-tuple-element.25), kind=kLoop, calls=%fused_computation | loop fusion | flops 1769472 | bytes 2654208 | tf_op jit(solution)/shard_map/convert_element_type | solution.py:358
  (38 shorter events, 5.5 us)
Async XLA Ops:
  0.0 32.4 %copy-start = (bf16[1,3456,128]{2,1,0:T(8,128)(2,1)S(1)}, bf16[1,3456,128]{2,1,0:T(8,128)(2,1)}, u32[]{:S(2)}) copy-start(bf16[1,3456,128]{2,1,0:T(8,128)(2,1)} %param.4) | copy-start | bytes 2654212
  1.1 12.2 %collective-permute-start.4 = (bf16[1728,128]{1,0:T(8,128)(2,1)S(1)}, bf16[1728,128]{1,0:T(8,128)(2,1)S(1)}, u32[]{:S(2)}, u32[]{:S(2)}) collective-permute-start(bf16[1728,128]{1,0:T(8,128)(2,1)S(1)} %dynamic-slice_bitcast_fusion), channel_id=1, source_target_pairs={{0,192},{64,0},{128,64},{192,128},{1,193},{65,1},{129,65},{193,129... | collective-permute-start | bytes 1327112 | tf_op jit(solution)/shard_map/ppermute | solution.py:304
  4.5 12.4 %collective-permute-start.3 = (bf16[1728,128]{1,0:T(8,128)(2,1)S(1)}, bf16[1728,128]{1,0:T(8,128)(2,1)S(1)}, u32[]{:S(2)}, u32[]{:S(2)}) collective-permute-start(bf16[1728,128]{1,0:T(8,128)(2,1)S(1)} %dynamic-slice_bitcast_fusion), channel_id=1, source_target_pairs={{0,64},{64,128},{128,192},{192,0},{1,65},{65,129},{129,193},{193,1... | collective-permute-start | bytes 1327112 | tf_op jit(solution)/shard_map/ppermute | solution.py:304
  5.5 3.2 %collective-permute-start = (bf16[4,16,16,128]{3,2,1,0:T(8,128)(2,1)S(1)}, bf16[4,16,16,128]{3,2,1,0:T(8,128)(2,1)S(1)}, u32[]{:S(2)}, u32[]{:S(2)}) collective-permute-start(bf16[4,16,16,128]{3,2,1,0:T(8,128)(2,1)S(1)} %pad_maximum_fusion.mine), channel_id=1, source_target_pairs={{0,32},{32,0},{1,33},{33,1},{2,34},{34,2},{3,35},{35,3},{4,36},{36... | collective-permute-start | bytes 786440 | tf_op jit(solution)/shard_map/ppermute | solution.py:308
  13.4 11.8 %collective-permute-start.6 = (bf16[864,128]{1,0:T(8,128)(2,1)S(1)}, bf16[864,128]{1,0:T(8,128)(2,1)S(1)}, u32[]{:S(2)}, u32[]{:S(2)}) collective-permute-start(bf16[864,128]{1,0:T(8,128)(2,1)S(1)} %constant_dynamic-slice_fusion), channel_id=1, source_target_pairs={{0,192},{64,0},{128,64},{192,128},{1,193},{65,1},{129,65},{193,129... | collective-permute-start | bytes 663560 | tf_op jit(solution)/shard_map/ppermute | solution.py:304
  17.0 12.6 %collective-permute-start.5 = (bf16[864,128]{1,0:T(8,128)(2,1)S(1)}, bf16[864,128]{1,0:T(8,128)(2,1)S(1)}, u32[]{:S(2)}, u32[]{:S(2)}) collective-permute-start(bf16[864,128]{1,0:T(8,128)(2,1)S(1)} %constant_dynamic-slice_fusion.1), channel_id=1, source_target_pairs={{0,64},{64,128},{128,192},{192,0},{1,65},{65,129},{129,193},{193,1... | collective-permute-start | bytes 663560 | tf_op jit(solution)/shard_map/ppermute | solution.py:304
  17.1 15.3 %collective-permute-start.8 = (bf16[1728,128]{1,0:T(8,128)(2,1)S(1)}, bf16[1728,128]{1,0:T(8,128)(2,1)S(1)}, u32[]{:S(2)}, u32[]{:S(2)}) collective-permute-start(bf16[1728,128]{1,0:T(8,128)(2,1)S(1)} %collective-permute-done.4.r3), channel_id=1, source_target_pairs={{0,32},{32,0},{1,33},{33,1},{2,34},{34,2},{3,35},{35,3},{4,36},{36... | collective-permute-start | bytes 1327112 | tf_op jit(solution)/shard_map/ppermute | solution.py:308
  19.0 13.4 %collective-permute-start.7 = (bf16[1728,128]{1,0:T(8,128)(2,1)S(1)}, bf16[1728,128]{1,0:T(8,128)(2,1)S(1)}, u32[]{:S(2)}, u32[]{:S(2)}) collective-permute-start(bf16[1728,128]{1,0:T(8,128)(2,1)S(1)} %collective-permute-done.3.r1), channel_id=1, source_target_pairs={{0,32},{32,0},{1,33},{33,1},{2,34},{34,2},{3,35},{35,3},{4,36},{36... | collective-permute-start | bytes 1327112 | tf_op jit(solution)/shard_map/ppermute | solution.py:308
  19.1 4.8 %collective-permute-start.2 = (bf16[8,3,16,128]{3,2,1,0:T(8,128)(2,1)S(1)}, bf16[8,3,16,128]{3,2,1,0:T(8,128)(2,1)S(1)}, u32[]{:S(2)}, u32[]{:S(2)}) collective-permute-start(bf16[8,3,16,128]{3,2,1,0:T(8,128)(2,1)S(1)} %get-tuple-element.16), channel_id=1, source_target_pairs={{1,0},{2,1},{3,2},{4,3},{5,4},{6,5},{7,6},{8,7},{9,8},{10,9},{11,1... | collective-permute-start | bytes 294920 | tf_op jit(solution)/shard_map/ppermute | solution.py:332
  23.9 8.5 %collective-permute-start.1 = (bf16[8,10,16,128]{3,2,1,0:T(8,128)(2,1)S(1)}, bf16[8,10,16,128]{3,2,1,0:T(8,128)(2,1)S(1)}, u32[]{:S(2)}, u32[]{:S(2)}) collective-permute-start(bf16[8,10,16,128]{3,2,1,0:T(8,128)(2,1)S(1)} %get-tuple-element.15), channel_id=1, source_target_pairs={{0,1},{1,2},{2,3},{3,4},{4,5},{5,6},{6,7},{7,8},{8,9},{9,10},{10,1... | collective-permute-start | bytes 983048 | tf_op jit(solution)/shard_map/ppermute | solution.py:331
  25.2 7.2 %collective-permute-start.10 = (bf16[864,128]{1,0:T(8,128)(2,1)S(1)}, bf16[864,128]{1,0:T(8,128)(2,1)S(1)}, u32[]{:S(2)}, u32[]{:S(2)}) collective-permute-start(bf16[864,128]{1,0:T(8,128)(2,1)S(1)} %collective-permute-done.6.rb), channel_id=1, source_target_pairs={{0,32},{32,0},{1,33},{33,1},{2,34},{34,2},{3,35},{35,3},{4,36},{36... | collective-permute-start | bytes 663560 | tf_op jit(solution)/shard_map/ppermute | solution.py:308
  29.6 2.8 %collective-permute-start.9 = (bf16[864,128]{1,0:T(8,128)(2,1)S(1)}, bf16[864,128]{1,0:T(8,128)(2,1)S(1)}, u32[]{:S(2)}, u32[]{:S(2)}) collective-permute-start(bf16[864,128]{1,0:T(8,128)(2,1)S(1)} %collective-permute-done.5.ra), channel_id=1, source_target_pairs={{0,32},{32,0},{1,33},{33,1},{2,34},{34,2},{3,35},{35,3},{4,36},{36... | collective-permute-start | bytes 663560 | tf_op jit(solution)/shard_map/ppermute | solution.py:308
  45.8 5.6 %collective-permute-start.13 = (bf16[640,128]{1,0:T(8,128)(2,1)S(1)}, bf16[640,128]{1,0:T(8,128)(2,1)S(1)}, u32[]{:S(2)}, u32[]{:S(2)}) collective-permute-start(bf16[640,128]{1,0:T(8,128)(2,1)S(1)} %get-tuple-element.21), channel_id=1, source_target_pairs={{0,64},{64,128},{128,192},{192,0},{1,65},{65,129},{129,193},{193,1... | collective-permute-start | bytes 491528 | tf_op jit(solution)/shard_map/ppermute | solution.py:304
  45.9 5.5 %collective-permute-start.15 = (bf16[640,128]{1,0:T(8,128)(2,1)S(1)}, bf16[640,128]{1,0:T(8,128)(2,1)S(1)}, u32[]{:S(2)}, u32[]{:S(2)}) collective-permute-start(bf16[640,128]{1,0:T(8,128)(2,1)S(1)} %get-tuple-element.22), channel_id=1, source_target_pairs={{0,192},{64,0},{128,64},{192,128},{1,193},{65,1},{129,65},{193,129... | collective-permute-start | bytes 491528 | tf_op jit(solution)/shard_map/ppermute | solution.py:304
  48.8 13.9 %collective-permute-start.11 = (bf16[1280,128]{1,0:T(8,128)(2,1)S(1)}, bf16[1280,128]{1,0:T(8,128)(2,1)S(1)}, u32[]{:S(2)}, u32[]{:S(2)}) collective-permute-start(bf16[1280,128]{1,0:T(8,128)(2,1)S(1)} %get-tuple-element.19), channel_id=1, source_target_pairs={{0,64},{64,128},{128,192},{192,0},{1,65},{65,129},{129,193},{193,1... | collective-permute-start | bytes 983048 | tf_op jit(solution)/shard_map/ppermute | solution.py:304
  48.8 13.9 %collective-permute-start.12 = (bf16[1280,128]{1,0:T(8,128)(2,1)S(1)}, bf16[1280,128]{1,0:T(8,128)(2,1)S(1)}, u32[]{:S(2)}, u32[]{:S(2)}) collective-permute-start(bf16[1280,128]{1,0:T(8,128)(2,1)S(1)} %get-tuple-element.20), channel_id=1, source_target_pairs={{0,192},{64,0},{128,64},{192,128},{1,193},{65,1},{129,65},{193,129... | collective-permute-start | bytes 983048 | tf_op jit(solution)/shard_map/ppermute | solution.py:304
  51.4 11.2 %collective-permute-start.14 = (bf16[640,128]{1,0:T(8,128)(2,1)S(1)}, bf16[640,128]{1,0:T(8,128)(2,1)S(1)}, u32[]{:S(2)}, u32[]{:S(2)}) collective-permute-start(bf16[640,128]{1,0:T(8,128)(2,1)S(1)} %collective-permute-done.13), channel_id=1, source_target_pairs={{0,64},{64,128},{128,192},{192,0},{1,65},{65,129},{129,193},{193,1... | collective-permute-start | bytes 491528 | tf_op jit(solution)/shard_map/ppermute | solution.py:304
  51.4 11.2 %collective-permute-start.16 = (bf16[640,128]{1,0:T(8,128)(2,1)S(1)}, bf16[640,128]{1,0:T(8,128)(2,1)S(1)}, u32[]{:S(2)}, u32[]{:S(2)}) collective-permute-start(bf16[640,128]{1,0:T(8,128)(2,1)S(1)} %collective-permute-done.15), channel_id=1, source_target_pairs={{0,192},{64,0},{128,64},{192,128},{1,193},{65,1},{129,65},{193,129... | collective-permute-start | bytes 491528 | tf_op jit(solution)/shard_map/ppermute | solution.py:304
  66.2 3.5 %collective-permute-start.17 = (bf16[1728,128]{1,0:T(8,128)(2,1)S(1)}, bf16[1728,128]{1,0:T(8,128)(2,1)S(1)}, u32[]{:S(2)}, u32[]{:S(2)}) collective-permute-start(bf16[1728,128]{1,0:T(8,128)(2,1)S(1)} %get-tuple-element.24), channel_id=1, source_target_pairs={{0,32},{32,0},{1,33},{33,1},{2,34},{34,2},{3,35},{35,3},{4,36},{36... | collective-permute-start | bytes 1327112 | tf_op jit(solution)/shard_map/ppermute | solution.py:308
  119.8 6.6 %collective-permute-start.18 = (bf16[1728,128]{1,0:T(8,128)(2,1)S(1)}, bf16[1728,128]{1,0:T(8,128)(2,1)S(1)}, u32[]{:S(2)}, u32[]{:S(2)}) collective-permute-start(bf16[1728,128]{1,0:T(8,128)(2,1)S(1)} %bitcast.23), channel_id=1, source_target_pairs={{0,32},{32,0},{1,33},{33,1},{2,34},{34,2},{3,35},{35,3},{4,36},{36... | collective-permute-start | bytes 1327112 | tf_op jit(solution)/shard_map/ppermute | solution.py:308

commit v5 on v4

--- a/solution.py
+++ b/solution.py
@@ -213,9 +213,8 @@
     send[...] = wg[pl.ds(pl.multiple_of((1 - tm) * HALF, CH // 2), HALF)].astype(BF16)
 
 
-def edges_kernel(pos, mine, other, long, short, start):
+def edges_kernel(pos, mine, other, long, short):
     tm = pos[1]
-    start[0] = 0
     half_fr = FR // 2
     few = HALO - OWN
     band = 2 * OWN
@@ -233,15 +232,29 @@
         out_shape=(
             jax.ShapeDtypeStruct((FR, HALO + CHALO, COLS, CH), BF16),
             jax.ShapeDtypeStruct((FR, HALO - OWN, COLS, CH), BF16),
-            jax.ShapeDtypeStruct((1,), jnp.int32),
         ),
         in_specs=in_vmem(2),
-        out_specs=(pl.BlockSpec(memory_space=pltpu.VMEM),) * 2
-        + (pl.BlockSpec(memory_space=pltpu.SMEM),),
+        out_specs=(pl.BlockSpec(memory_space=pltpu.VMEM),) * 2,
         compiler_params=pltpu.CompilerParams(vmem_limit_bytes=8 * 2**20),
         cost_estimate=pl.CostEstimate(flops=0, bytes_accessed=900_000, transcendentals=0),
         name="edges",
     )(pos, mine, other)
+
+
+def zero_kernel(after, start):
+    del after
+    start[0] = 0
+
+
+def zero_after(x):
+    return pl.pallas_call(
+        zero_kernel,
+        out_shape=jax.ShapeDtypeStruct((1,), jnp.int32),
+        in_specs=[pl.BlockSpec(memory_space=pltpu.VMEM)],
+        out_specs=pl.BlockSpec(memory_space=pltpu.SMEM),
+        compiler_params=pltpu.CompilerParams(vmem_limit_bytes=4 * 2**20),
+        name="zero_after",
+    )(x)[0]
 
 
 def in_vmem(n):
@@ -324,16 +337,19 @@
     c = lax.dynamic_index_in_dim(cotangent, seg, 0, keepdims=False)
     mine = jnp.concatenate([x, c], 1)
     other = swap(mine)
-    long, short, start = run_edges(pos, mine, other)
+    long, short = run_edges(pos, mine, other)
     down = [(i, i + 1) for i in range(spaces - 1)]
     up = [(i + 1, i) for i in range(spaces - 1)]
     both = lambda low, high: low + [(spaces + i, spaces + j) for i, j in high]
     long = lax.ppermute(long, ("tm", "z", "y"), both(down, up))
     short = lax.ppermute(short, ("tm", "z", "y"), both(up, down))
 
-    cut = lambda v, at: lax.dynamic_slice_in_dim(v, at + start[0], HALF // 2, 0)
+    start = zero_after(short)
+    late = zero_after(long)
+    cut = lambda v, at: lax.dynamic_slice_in_dim(v, at + start, HALF // 2, 0)
     got = [left, right, along(cut(left, 0), 1), along(cut(right, HALF // 2), -1)]
-    crossed = [swap(g) for g in got]
+    held = [lax.dynamic_slice_in_dim(jnp.pad(g, ((0, 16), (0, 0))), late, HALF // 2, 0) for g in got[2:]]
+    crossed = [swap(g) for g in got[:2] + held]
 
     parts = run_layers(spaces * rows, pos, mine, other, long, short, w, *got, *crossed)
     far_a, far_b = along(parts[2], 1), along(parts[3], -1)

time: 128 us -> 127 us (level)
  starting transfers between devices: 35.7 us -> 32.2 us
  local copies, waits for them, and re-layouts: 2.34 us -> 4.53 us
  between operations: 3.62 us -> 5.54 us
  waiting for transfers between devices: 16.7 us -> 14.8 us
    ppermute x1, waiting for transfers between devices: 2.5 us -> 0.01 us  [body(): long = lax.ppermute(long, ('tm', 'z', 'y'), both(down, up))]
    ppermute x7, starting transfers between devices: 16 us -> 13.9 us  [swap(): return lax.ppermute(x, 'tm', [(0, 1), (1, 0)])]
    ppermute x10, waiting for transfers between devices: 8.63 us -> 10.2 us  [along(): return lax.ppermute(x, 'segment', ring(LAYERS, by))]
    dynamic_slice x2 -> x4, local copies, waits for them, and re-layouts: 0.13 us -> 1.64 us  [the longest x2 1.51 us: body(): cut = lambda v, at: lax.dynamic_slice_in_dim(v, at + start, HALF // 2, 0)]
    ppermute x10, starting transfers between devices: 15.3 us -> 13.8 us  [along(): return lax.ppermute(x, 'segment', ring(LAYERS, by))]
    ppermute x1, waiting for transfers between devices: 1.62 us -> 0.32 us  [body(): short = lax.ppermute(short, ('tm', 'z', 'y'), both(up, down))]
  transfers between devices with their start and end apart: 19 -> 19, of which waited for: 7 -> 9; matrix products, arithmetic and copies ran while one was open for 1% -> 2% of each run, Pallas kernels for 1% -> 1%
where the time goes in v5:
time: 127 us
  blocking collectives  49.1 us (39%)
  starting transfers between devices  32.2 us (25%)
  Pallas kernels  19.2 us (15%)
  waiting for transfers between devices  14.8 us (12%)
  between operations  5.54 us (4%)
  local copies, waits for them, and re-layouts  4.53 us (4%)
  other arithmetic  1.72 us (1%)
    all_to_all x1, blocking collectives, body(): pieces = lax.all_to_all(total.reshape(nz, rows_z, CH), 'z', 0, 0)  15.9 us
    pallas_call x1, Pallas kernels, run_layers(): pl.pallas_call(functools.partial(layers_kernel, total), out_shape=tuple((...  14 us
    all_to_all x1, blocking collectives, body(): pieces = lax.all_to_all(total.reshape(ny, rows_y, CH), 'y', 0, 0)  13.9 us
    ppermute x7, starting transfers between devices, swap(): return lax.ppermute(x, 'tm', [(0, 1), (1, 0)])  13.9 us
    ppermute x10, starting transfers between devices, along(): return lax.ppermute(x, 'segment', ring(LAYERS, by))  13.8 us
    all_to_all x1, blocking collectives, body(): whole = lax.all_to_all(jnp.broadcast_to(total, (nz, rows_z, CH)), 'z', 0, 0)  10.3 us
    ppermute x10, waiting for transfers between devices, along(): return lax.ppermute(x, 'segment', ring(LAYERS, by))  10.2 us
    all_to_all x1, blocking collectives, body(): whole = lax.all_to_all(jnp.broadcast_to(whole, (ny, rows_y, CH)), 'y', 0, 0)  8.87 us
  transfers between devices with their start and end apart: 19, of which 9 were waited for; matrix products, arithmetic and copies ran while one was open for 2% of the time, Pallas kernels for 1%

profile of v5, /device:TPU:1, one launch (start us, length us, event | category | flops | bytes accessed | tf_op | source)
XLA Modules:
  0.0 127.0 jit_solution(7009020720253592821)
XLA Ops:
  0.0 1.8 %dynamic-slice_bitcast_fusion = bf16[1728,128]{1,0:T(8,128)(2,1)} fusion(bf16[1,3456,128]{2,1,0:T(8,128)(2,1)} %param.4, s32[]{:T(128)S(6)} %select_n.32), kind=kLoop, calls=%fused_computation.4 | loop fusion | bytes 884740 | tf_op jit(solution)/shard_map/dynamic_slice | solution.py:333
  1.8 3.3 %collective-permute-start.4 = (bf16[1728,128]{1,0:T(8,128)(2,1)}, bf16[1728,128]{1,0:T(8,128)(2,1)S(1)}, u32[]{:S(2)}, u32[]{:S(2)}) collective-permute-start(bf16[1728,128]{1,0:T(8,128)(2,1)} %dynamic-slice_bitcast_fusion), channel_id=1, source_target_pairs={{0,192},{64,0},{128,64},{192,128},{1,193},{65,1},{129,65},{193,129... | collective-permute-start | bytes 1327112 | tf_op jit(solution)/shard_map/ppermute | solution.py:317
  8.9 3.2 %collective-permute-start.2 = (bf16[8,3,16,128]{3,2,1,0:T(8,128)(2,1)S(1)}, bf16[8,3,16,128]{3,2,1,0:T(8,128)(2,1)S(1)}, u32[]{:S(2)}, u32[]{:S(2)}) collective-permute-start(bf16[8,3,16,128]{3,2,1,0:T(8,128)(2,1)S(1)} %get-tuple-element.15), channel_id=1, source_target_pairs={{1,0},{2,1},{3,2},{4,3},{5,4},{6,5},{7,6},{8,7},{9,8},{10,9},{11,1... | collective-permute-start | bytes 294920 | tf_op jit(solution)/shard_map/ppermute | solution.py:345
  12.1 1.3 %collective-permute-start.1 = (bf16[8,10,16,128]{3,2,1,0:T(8,128)(2,1)S(1)}, bf16[8,10,16,128]{3,2,1,0:T(8,128)(2,1)S(1)}, u32[]{:S(2)}, u32[]{:S(2)}) collective-permute-start(bf16[8,10,16,128]{3,2,1,0:T(8,128)(2,1)S(1)} %get-tuple-element.14), channel_id=1, source_target_pairs={{0,1},{1,2},{2,3},{3,4},{4,5},{5,6},{6,7},{7,8},{8,9},{9,10},{10,1... | collective-permute-start | bytes 983048 | tf_op jit(solution)/shard_map/ppermute | solution.py:344
  17.8 1.6 %collective-permute-start.6 = (bf16[864,128]{1,0:T(8,128)(2,1)}, bf16[864,128]{1,0:T(8,128)(2,1)S(1)}, u32[]{:S(2)}, u32[]{:S(2)}) collective-permute-start(bf16[864,128]{1,0:T(8,128)(2,1)} %constant_dynamic-slice_fusion), channel_id=1, source_target_pairs={{0,192},{64,0},{128,64},{192,128},{1,193},{65,1},{129,65},{193,129... | collective-permute-start | bytes 663560 | tf_op jit(solution)/shard_map/ppermute | solution.py:317
  21.1 2.3 %collective-permute-start.8 = (bf16[1728,128]{1,0:T(8,128)(2,1)S(1)}, bf16[1728,128]{1,0:T(8,128)(2,1)}, u32[]{:S(2)}, u32[]{:S(2)}) collective-permute-start(bf16[1728,128]{1,0:T(8,128)(2,1)S(1)} %collective-permute-done.4.r3), channel_id=1, source_target_pairs={{0,32},{32,0},{1,33},{33,1},{2,34},{34,2},{3,35},{35,3},{4,36},{36... | collective-permute-start | bytes 1327112 | tf_op jit(solution)/shard_map/ppermute | solution.py:321
  27.4 3.5 %collective-permute-start.9 = (bf16[864,128]{1,0:T(8,128)(2,1)S(1)}, bf16[864,128]{1,0:T(8,128)(2,1)S(1)}, u32[]{:S(2)}, u32[]{:S(2)}) collective-permute-start(bf16[864,128]{1,0:T(8,128)(2,1)S(1)} %pad_dynamic-slice_fusion.1), channel_id=1, source_target_pairs={{0,32},{32,0},{1,33},{33,1},{2,34},{34,2},{3,35},{35,3},{4,36},{36... | collective-permute-start | bytes 663560 | tf_op jit(solution)/shard_map/ppermute | solution.py:321
  30.9 1.1 collective-permute-done.9.qa
  32.0 14.0 %layers.1 = (bf16[1280,128]{1,0:T(8,128)(2,1)S(1)}, bf16[1280,128]{1,0:T(8,128)(2,1)S(1)}, bf16[640,128]{1,0:T(8,128)(2,1)S(1)}, bf16[640,128]{1,0:T(8,128)(2,1)S(1)}, bf16[1280,128]{1,0:T(8,128)(2,1)S(1)}) custom-call(s32[3]{0:T(128)S(1)} %pad_add_fusion.pos, bf16[4,16,16,128]{3,2,1,0:T(8,128)(2,1)S(1)} %pad_maximum_fusion.mine, ...), custom_call_target="tpu_custom_call" | custom-call | flops 8999999488 | bytes 6000000 | tf_op jit(solution)/shard_map/layers/pallas_call | solution.py:267
  46.1 2.7 %collective-permute-start.15 = (bf16[640,128]{1,0:T(8,128)(2,1)S(1)}, bf16[640,128]{1,0:T(8,128)(2,1)S(1)}, u32[]{:S(2)}, u32[]{:S(2)}) collective-permute-start(bf16[640,128]{1,0:T(8,128)(2,1)S(1)} %get-tuple-element.20), channel_id=1, source_target_pairs={{0,192},{64,0},{128,64},{192,128},{1,193},{65,1},{129,65},{193,129... | collective-permute-start | bytes 491528 | tf_op jit(solution)/shard_map/ppermute | solution.py:317
  48.8 2.7 %collective-permute-start.12 = (bf16[1280,128]{1,0:T(8,128)(2,1)S(1)}, bf16[1280,128]{1,0:T(8,128)(2,1)S(1)}, u32[]{:S(2)}, u32[]{:S(2)}) collective-permute-start(bf16[1280,128]{1,0:T(8,128)(2,1)S(1)} %get-tuple-element.18), channel_id=1, source_target_pairs={{0,192},{64,0},{128,64},{192,128},{1,193},{65,1},{129,65},{193,129... | collective-permute-start | bytes 983048 | tf_op jit(solution)/shard_map/ppermute | solution.py:317
  51.5 1.3 %collective-permute-done.13 = bf16[640,128]{1,0:T(8,128)(2,1)S(1)} collective-permute-done((bf16[640,128]{1,0:T(8,128)(2,1)S(1)}, bf16[640,128]{1,0:T(8,128)(2,1)S(1)}, u32[]{:S(2)}, u32[]{:S(2)}) %collective-permute-start.13) | collective-permute-done | bytes 163872 | tf_op jit(solution)/shard_map/ppermute | solution.py:317
  52.8 2.7 %collective-permute-start.16 = (bf16[640,128]{1,0:T(8,128)(2,1)S(1)}, bf16[640,128]{1,0:T(8,128)(2,1)S(1)}, u32[]{:S(2)}, u32[]{:S(2)}) collective-permute-start(bf16[640,128]{1,0:T(8,128)(2,1)S(1)} %collective-permute-done.15), channel_id=1, source_target_pairs={{0,192},{64,0},{128,64},{192,128},{1,193},{65,1},{129,65},{193,129... | collective-permute-start | bytes 491528 | tf_op jit(solution)/shard_map/ppermute | solution.py:317
  55.4 7.9 %collective-permute-done.14.ea = bf16[640,128]{1,0:T(8,128)(2,1)S(1)} collective-permute-done((bf16[640,128]{1,0:T(8,128)(2,1)S(1)}, bf16[640,128]{1,0:T(8,128)(2,1)S(1)}, u32[]{:S(2)}, u32[]{:S(2)}) %collective-permute-start.14) | collective-permute-done | bytes 163872 | tf_op jit(solution)/shard_map/ppermute | solution.py:317
  63.3 3.6 %kernel_grad.1 = (f32[1728,128]{1,0:T(8,128)S(1)}, bf16[1728,128]{1,0:T(8,128)(2,1)S(1)}) custom-call(s32[3]{0:T(128)S(1)} %pad_add_fusion.pos, bf16[1280,128]{1,0:T(8,128)(2,1)S(1)} %get-tuple-element.16.e0, bf16[1280,128]{1,0:T(8,128)(2,1)S(1)} %collective-permute-done.11.e1, bf16[1280,128]{1,0:T(8,128)(2,1)S(1)} %collective-permute-done.12.e3, ...), custom_call_target="tpu_custom_call" | custom-call | flops 1800000000 | bytes 4000000 | tf_op jit(solution)/shard_map/kernel_grad/pallas_call | solution.py:290
  66.9 1.3 %collective-permute-start.17 = (bf16[1728,128]{1,0:T(8,128)(2,1)S(1)}, bf16[1728,128]{1,0:T(8,128)(2,1)S(1)}, u32[]{:S(2)}, u32[]{:S(2)}) collective-permute-start(bf16[1728,128]{1,0:T(8,128)(2,1)S(1)} %get-tuple-element.22), channel_id=1, source_target_pairs={{0,32},{32,0},{1,33},{33,1},{2,34},{34,2},{3,35},{35,3},{4,36},{36... | collective-permute-start | bytes 1327112 | tf_op jit(solution)/shard_map/ppermute | solution.py:321
  68.1 1.4 %collective-permute-done.17 = bf16[1728,128]{1,0:T(8,128)(2,1)S(1)} collective-permute-done((bf16[1728,128]{1,0:T(8,128)(2,1)S(1)}, bf16[1728,128]{1,0:T(8,128)(2,1)S(1)}, u32[]{:S(2)}, u32[]{:S(2)}) %collective-permute-start.17) | collective-permute-done | bytes 442400 | tf_op jit(solution)/shard_map/ppermute | solution.py:321
  69.7 13.9 %all_to_all.20 = bf16[4,432,128]{2,1,0:T(8,128)(2,1)S(1)} all-to-all(bf16[4,432,128]{2,1,0:T(8,128)(2,1)S(1)} %bitcast.23), channel_id=1, replica_groups=mesh['segment'=4,'tm'=2,'z'=8,'y'=4] {'y'}, dimensions={0} | all-to-all | bytes 884736 | tf_op jit(solution)/shard_map/all_to_all | solution.py:361
  83.7 15.9 %all_to_all.21 = bf16[8,64,128]{2,1,0:T(8,128)(2,1)S(1)} all-to-all(bf16[8,64,128]{2,1,0:T(8,128)(2,1)S(1)} %bitcast.25), channel_id=1, replica_groups=mesh['segment'=4,'tm'=2,'z'=8,'y'=4] {'z'}, dimensions={0} | all-to-all | bytes 262144 | tf_op jit(solution)/shard_map/all_to_all | solution.py:365
  99.7 10.3 %all_to_all.22 = bf16[8,64,128]{2,1,0:T(8,128)(2,1)S(1)} all-to-all(bf16[8,64,128]{2,1,0:T(8,128)(2,1)S(1)} %broadcast_in_dim.7), channel_id=1, replica_groups=mesh['segment'=4,'tm'=2,'z'=8,'y'=4] {'z'}, dimensions={0} | all-to-all | bytes 262144 | tf_op jit(solution)/shard_map/all_to_all | solution.py:367
  110.1 8.9 %all_to_all.23 = bf16[4,432,128]{2,1,0:T(8,128)(2,1)S(1)} all-to-all(bf16[4,432,128]{2,1,0:T(8,128)(2,1)S(1)} %broadcast_in_dim.8), channel_id=1, replica_groups=mesh['segment'=4,'tm'=2,'z'=8,'y'=4] {'y'}, dimensions={0} | all-to-all | bytes 884736 | tf_op jit(solution)/shard_map/all_to_all | solution.py:369
  119.0 5.2 %collective-permute-start.18 = (bf16[1728,128]{1,0:T(8,128)(2,1)S(1)}, bf16[1728,128]{1,0:T(8,128)(2,1)S(1)}, u32[]{:S(2)}, u32[]{:S(2)}) collective-permute-start(bf16[1728,128]{1,0:T(8,128)(2,1)S(1)} %bitcast.24), channel_id=1, source_target_pairs={{0,32},{32,0},{1,33},{33,1},{2,34},{34,2},{3,35},{35,3},{4,36},{36... | collective-permute-start | bytes 1327112 | tf_op jit(solution)/shard_map/ppermute | solution.py:321
  124.2 1.4 %collective-permute-done.18 = bf16[1728,128]{1,0:T(8,128)(2,1)S(1)} collective-permute-done((bf16[1728,128]{1,0:T(8,128)(2,1)S(1)}, bf16[1728,128]{1,0:T(8,128)(2,1)S(1)}, u32[]{:S(2)}, u32[]{:S(2)}) %collective-permute-start.18) | collective-permute-done | bytes 442400 | tf_op jit(solution)/shard_map/ppermute | solution.py:321
  125.7 1.3 %maximum_convert_fusion = f32[1,3456,128]{2,1,0:T(8,128)} fusion(bf16[1,1728,128]{2,1,0:T(8,128)(2,1)S(1)} %get-tuple-element.24, bf16[1,1728,128]{2,1,0:T(8,128)(2,1)S(1)} %get-tuple-element.23), kind=kLoop, calls=%fused_computation | loop fusion | flops 1769472 | bytes 2654208 | tf_op jit(solution)/shard_map/convert_element_type | solution.py:374
  (42 shorter events, 8.9 us)
Async XLA Ops:
  1.8 15.3 %collective-permute-start.4 = (bf16[1728,128]{1,0:T(8,128)(2,1)}, bf16[1728,128]{1,0:T(8,128)(2,1)S(1)}, u32[]{:S(2)}, u32[]{:S(2)}) collective-permute-start(bf16[1728,128]{1,0:T(8,128)(2,1)} %dynamic-slice_bitcast_fusion), channel_id=1, source_target_pairs={{0,192},{64,0},{128,64},{192,128},{1,193},{65,1},{129,65},{193,129... | collective-permute-start | bytes 1327112 | tf_op jit(solution)/shard_map/ppermute | solution.py:317
  6.1 25.9 %copy-start = (bf16[1,3456,128]{2,1,0:T(8,128)(2,1)S(1)}, bf16[1,3456,128]{2,1,0:T(8,128)(2,1)}, u32[]{:S(2)}) copy-start(bf16[1,3456,128]{2,1,0:T(8,128)(2,1)} %param.4) | copy-start | bytes 2654212
  6.1 2.2 %collective-permute-start = (bf16[4,16,16,128]{3,2,1,0:T(8,128)(2,1)S(1)}, bf16[4,16,16,128]{3,2,1,0:T(8,128)(2,1)S(1)}, u32[]{:S(2)}, u32[]{:S(2)}) collective-permute-start(bf16[4,16,16,128]{3,2,1,0:T(8,128)(2,1)S(1)} %pad_maximum_fusion.mine), channel_id=1, source_target_pairs={{0,32},{32,0},{1,33},{33,1},{2,34},{34,2},{3,35},{35,3},{4,36},{36... | collective-permute-start | bytes 786440 | tf_op jit(solution)/shard_map/ppermute | solution.py:321
  7.2 13.2 %collective-permute-start.3 = (bf16[1728,128]{1,0:T(8,128)(2,1)}, bf16[1728,128]{1,0:T(8,128)(2,1)S(1)}, u32[]{:S(2)}, u32[]{:S(2)}) collective-permute-start(bf16[1728,128]{1,0:T(8,128)(2,1)} %dynamic-slice_bitcast_fusion), channel_id=1, source_target_pairs={{0,64},{64,128},{128,192},{192,0},{1,65},{65,129},{129,193},{193,1... | collective-permute-start | bytes 1327112 | tf_op jit(solution)/shard_map/ppermute | solution.py:317
  8.9 4.8 %collective-permute-start.2 = (bf16[8,3,16,128]{3,2,1,0:T(8,128)(2,1)S(1)}, bf16[8,3,16,128]{3,2,1,0:T(8,128)(2,1)S(1)}, u32[]{:S(2)}, u32[]{:S(2)}) collective-permute-start(bf16[8,3,16,128]{3,2,1,0:T(8,128)(2,1)S(1)} %get-tuple-element.15), channel_id=1, source_target_pairs={{1,0},{2,1},{3,2},{4,3},{5,4},{6,5},{7,6},{8,7},{9,8},{10,9},{11,1... | collective-permute-start | bytes 294920 | tf_op jit(solution)/shard_map/ppermute | solution.py:345
  12.1 11.2 %collective-permute-start.1 = (bf16[8,10,16,128]{3,2,1,0:T(8,128)(2,1)S(1)}, bf16[8,10,16,128]{3,2,1,0:T(8,128)(2,1)S(1)}, u32[]{:S(2)}, u32[]{:S(2)}) collective-permute-start(bf16[8,10,16,128]{3,2,1,0:T(8,128)(2,1)S(1)} %get-tuple-element.14), channel_id=1, source_target_pairs={{0,1},{1,2},{2,3},{3,4},{4,5},{5,6},{6,7},{7,8},{8,9},{9,10},{10,1... | collective-permute-start | bytes 983048 | tf_op jit(solution)/shard_map/ppermute | solution.py:344
  17.8 8.0 %collective-permute-start.6 = (bf16[864,128]{1,0:T(8,128)(2,1)}, bf16[864,128]{1,0:T(8,128)(2,1)S(1)}, u32[]{:S(2)}, u32[]{:S(2)}) collective-permute-start(bf16[864,128]{1,0:T(8,128)(2,1)} %constant_dynamic-slice_fusion), channel_id=1, source_target_pairs={{0,192},{64,0},{128,64},{192,128},{1,193},{65,1},{129,65},{193,129... | collective-permute-start | bytes 663560 | tf_op jit(solution)/shard_map/ppermute | solution.py:317
  21.1 6.2 %collective-permute-start.5 = (bf16[864,128]{1,0:T(8,128)(2,1)}, bf16[864,128]{1,0:T(8,128)(2,1)S(1)}, u32[]{:S(2)}, u32[]{:S(2)}) collective-permute-start(bf16[864,128]{1,0:T(8,128)(2,1)} %constant_dynamic-slice_fusion.1), channel_id=1, source_target_pairs={{0,64},{64,128},{128,192},{192,0},{1,65},{65,129},{129,193},{193,1... | collective-permute-start | bytes 663560 | tf_op jit(solution)/shard_map/ppermute | solution.py:317
  21.1 9.8 %collective-permute-start.8 = (bf16[1728,128]{1,0:T(8,128)(2,1)S(1)}, bf16[1728,128]{1,0:T(8,128)(2,1)}, u32[]{:S(2)}, u32[]{:S(2)}) collective-permute-start(bf16[1728,128]{1,0:T(8,128)(2,1)S(1)} %collective-permute-done.4.r3), channel_id=1, source_target_pairs={{0,32},{32,0},{1,33},{33,1},{2,34},{34,2},{3,35},{35,3},{4,36},{36... | collective-permute-start | bytes 1327112 | tf_op jit(solution)/shard_map/ppermute | solution.py:321
  23.4 8.6 %collective-permute-start.7 = (bf16[1728,128]{1,0:T(8,128)(2,1)S(1)}, bf16[1728,128]{1,0:T(8,128)(2,1)}, u32[]{:S(2)}, u32[]{:S(2)}) collective-permute-start(bf16[1728,128]{1,0:T(8,128)(2,1)S(1)} %collective-permute-done.3.r1), channel_id=1, source_target_pairs={{0,32},{32,0},{1,33},{33,1},{2,34},{34,2},{3,35},{35,3},{4,36},{36... | collective-permute-start | bytes 1327112 | tf_op jit(solution)/shard_map/ppermute | solution.py:321
  25.9 5.0 %collective-permute-start.10 = (bf16[864,128]{1,0:T(8,128)(2,1)S(1)}, bf16[864,128]{1,0:T(8,128)(2,1)S(1)}, u32[]{:S(2)}, u32[]{:S(2)}) collective-permute-start(bf16[864,128]{1,0:T(8,128)(2,1)S(1)} %pad_dynamic-slice_fusion), channel_id=1, source_target_pairs={{0,32},{32,0},{1,33},{33,1},{2,34},{34,2},{3,35},{35,3},{4,36},{36... | collective-permute-start | bytes 663560 | tf_op jit(solution)/shard_map/ppermute | solution.py:321
  27.4 4.6 %collective-permute-start.9 = (bf16[864,128]{1,0:T(8,128)(2,1)S(1)}, bf16[864,128]{1,0:T(8,128)(2,1)S(1)}, u32[]{:S(2)}, u32[]{:S(2)}) collective-permute-start(bf16[864,128]{1,0:T(8,128)(2,1)S(1)} %pad_dynamic-slice_fusion.1), channel_id=1, source_target_pairs={{0,32},{32,0},{1,33},{33,1},{2,34},{34,2},{3,35},{35,3},{4,36},{36... | collective-permute-start | bytes 663560 | tf_op jit(solution)/shard_map/ppermute | solution.py:321
  46.0 6.7 %collective-permute-start.13 = (bf16[640,128]{1,0:T(8,128)(2,1)S(1)}, bf16[640,128]{1,0:T(8,128)(2,1)S(1)}, u32[]{:S(2)}, u32[]{:S(2)}) collective-permute-start(bf16[640,128]{1,0:T(8,128)(2,1)S(1)} %get-tuple-element.19), channel_id=1, source_target_pairs={{0,64},{64,128},{128,192},{192,0},{1,65},{65,129},{129,193},{193,1... | collective-permute-start | bytes 491528 | tf_op jit(solution)/shard_map/ppermute | solution.py:317
  46.1 6.6 %collective-permute-start.15 = (bf16[640,128]{1,0:T(8,128)(2,1)S(1)}, bf16[640,128]{1,0:T(8,128)(2,1)S(1)}, u32[]{:S(2)}, u32[]{:S(2)}) collective-permute-start(bf16[640,128]{1,0:T(8,128)(2,1)S(1)} %get-tuple-element.20), channel_id=1, source_target_pairs={{0,192},{64,0},{128,64},{192,128},{1,193},{65,1},{129,65},{193,129... | collective-permute-start | bytes 491528 | tf_op jit(solution)/shard_map/ppermute | solution.py:317
  48.8 14.5 %collective-permute-start.11 = (bf16[1280,128]{1,0:T(8,128)(2,1)S(1)}, bf16[1280,128]{1,0:T(8,128)(2,1)S(1)}, u32[]{:S(2)}, u32[]{:S(2)}) collective-permute-start(bf16[1280,128]{1,0:T(8,128)(2,1)S(1)} %get-tuple-element.17), channel_id=1, source_target_pairs={{0,64},{64,128},{128,192},{192,0},{1,65},{65,129},{129,193},{193,1... | collective-permute-start | bytes 983048 | tf_op jit(solution)/shard_map/ppermute | solution.py:317
  48.8 14.5 %collective-permute-start.12 = (bf16[1280,128]{1,0:T(8,128)(2,1)S(1)}, bf16[1280,128]{1,0:T(8,128)(2,1)S(1)}, u32[]{:S(2)}, u32[]{:S(2)}) collective-permute-start(bf16[1280,128]{1,0:T(8,128)(2,1)S(1)} %get-tuple-element.18), channel_id=1, source_target_pairs={{0,192},{64,0},{128,64},{192,128},{1,193},{65,1},{129,65},{193,129... | collective-permute-start | bytes 983048 | tf_op jit(solution)/shard_map/ppermute | solution.py:317
  52.7 10.5 %collective-permute-start.14 = (bf16[640,128]{1,0:T(8,128)(2,1)S(1)}, bf16[640,128]{1,0:T(8,128)(2,1)S(1)}, u32[]{:S(2)}, u32[]{:S(2)}) collective-permute-start(bf16[640,128]{1,0:T(8,128)(2,1)S(1)} %collective-permute-done.13), channel_id=1, source_target_pairs={{0,64},{64,128},{128,192},{192,0},{1,65},{65,129},{129,193},{193,1... | collective-permute-start | bytes 491528 | tf_op jit(solution)/shard_map/ppermute | solution.py:317
  52.8 10.5 %collective-permute-start.16 = (bf16[640,128]{1,0:T(8,128)(2,1)S(1)}, bf16[640,128]{1,0:T(8,128)(2,1)S(1)}, u32[]{:S(2)}, u32[]{:S(2)}) collective-permute-start(bf16[640,128]{1,0:T(8,128)(2,1)S(1)} %collective-permute-done.15), channel_id=1, source_target_pairs={{0,192},{64,0},{128,64},{192,128},{1,193},{65,1},{129,65},{193,129... | collective-permute-start | bytes 491528 | tf_op jit(solution)/shard_map/ppermute | solution.py:317
  66.9 2.7 %collective-permute-start.17 = (bf16[1728,128]{1,0:T(8,128)(2,1)S(1)}, bf16[1728,128]{1,0:T(8,128)(2,1)S(1)}, u32[]{:S(2)}, u32[]{:S(2)}) collective-permute-start(bf16[1728,128]{1,0:T(8,128)(2,1)S(1)} %get-tuple-element.22), channel_id=1, source_target_pairs={{0,32},{32,0},{1,33},{33,1},{2,34},{34,2},{3,35},{35,3},{4,36},{36... | collective-permute-start | bytes 1327112 | tf_op jit(solution)/shard_map/ppermute | solution.py:321
  119.0 6.6 %collective-permute-start.18 = (bf16[1728,128]{1,0:T(8,128)(2,1)S(1)}, bf16[1728,128]{1,0:T(8,128)(2,1)S(1)}, u32[]{:S(2)}, u32[]{:S(2)}) collective-permute-start(bf16[1728,128]{1,0:T(8,128)(2,1)S(1)} %bitcast.24), channel_id=1, source_target_pairs={{0,32},{32,0},{1,33},{33,1},{2,34},{34,2},{3,35},{35,3},{4,36},{36... | collective-permute-start | bytes 1327112 | tf_op jit(solution)/shard_map/ppermute | solution.py:321

commit v6 on v3

--- a/solution.py
+++ b/solution.py
@@ -163,36 +163,81 @@
         out[...] = part[lax.rem(seg + d, LAYERS), lo : lo + out.shape[0]]
 
 
-def kernel_grad_kernel(pos, e0, e1, e3, ea, eb, keep, send, e2, x9, d3, wg):
+def kernel_grad_kernel(pos, e0, e1, e3, ea, eb, keep, send, e2, cols, deltas, wg):
     tm = pos[1]
     e2[: PART // 2] = ea[...]
     e2[PART // 2 :] = eb[...]
     cells = OWN * COLS
     width = cells + 2 * COLS
-    nothing = jnp.zeros((cells, CH), BF16)
+    total = LAYERS * FR * cells
     for m, e in enumerate((e0, e1, e2, e3)):
         for t in range(FR):
-            at = (m * FR + t) * cells
-            frame = e[t * width : (t + 1) * width].astype(F32)
-            for lag_c, v in enumerate(shifted(frame)):
-                for lag_r in range(3):
-                    tap = (lag_r * 3 + lag_c) * CH
-                    x9[at : at + cells, tap : tap + CH] = v[lag_r * COLS : lag_r * COLS + cells]
-            for lag_t in range(3):
-                src = t + 2 - lag_t
-                row = HID + src * cells
-                d3[at : at + cells, lag_t * CH : (lag_t + 1) * CH] = (
-                    e[row : row + cells] if src < FR else nothing
-                )
-    out = lax.dot_general(
-        d3[...], x9[...], (((0,), (0,)), ((), ())), preferred_element_type=F32
-    )
+            frame = e[t * width : (t + 1) * width]
+            before, _, after = shifted(frame.astype(F32))
+            for lag_c, v in enumerate((before, frame, after)):
+                cols[lag_c, m * FR + t] = v
+            deltas[m, t] = e[HID + t * cells : HID + (t + 1) * cells]
+        for t in (FR, FR + 1):
+            deltas[m, t] = jnp.zeros((cells, CH), BF16)
+    x9 = jnp.concatenate(
+        [
+            cols[lag_c, :, lag_r * COLS : lag_r * COLS + cells].reshape(total, CH)
+            for lag_r in range(3)
+            for lag_c in range(3)
+        ],
+        1,
+    )
+    d3 = jnp.concatenate(
+        [deltas[:, 2 - lag_t : 2 - lag_t + FR].reshape(total, CH) for lag_t in range(3)], 1
+    )
+    out = lax.dot_general(d3, x9, (((0,), (0,)), ((), ())), preferred_element_type=F32)
     for lag_t in range(3):
         for tap in range(9):
             at = (lag_t * 9 + tap) * CH
             wg[at : at + CH] = out[lag_t * CH : (lag_t + 1) * CH, tap * CH : (tap + 1) * CH].T
     keep[...] = wg[pl.ds(pl.multiple_of(tm * HALF, CH // 2), HALF)]
     send[...] = wg[pl.ds(pl.multiple_of((1 - tm) * HALF, CH // 2), HALF)].astype(BF16)
+
+
+def zero_kernel(*refs):
+    refs[-1][0] = 0
+
+
+def zero_after(*arrays):
+    return pl.pallas_call(
+        zero_kernel,
+        out_shape=jax.ShapeDtypeStruct((1,), jnp.int32),
+        in_specs=[pl.BlockSpec(memory_space=pltpu.VMEM)] * len(arrays),
+        out_specs=pl.BlockSpec(memory_space=pltpu.SMEM),
+        compiler_params=pltpu.CompilerParams(vmem_limit_bytes=4 * 2**20),
+        name="zero_after",
+    )(*arrays)
+
+
+def join_kernel(start, before, after, x, c, out):
+    at = start[0]
+    rows = x.shape[1]
+    for t in range(FR // 2):
+        for to, n, ref, lo in (
+            (0, HALO, before, 0),
+            (HALO, rows, x, 0),
+            (HALO + rows, HALO, after, 0),
+            (2 * HALO + rows, CHALO, before, HALO),
+            (2 * HALO + CHALO + rows, rows, c, 0),
+            (2 * HALO + CHALO + 2 * rows, CHALO, after, HALO),
+        ):
+            out[t, pl.ds(at + to, n)] = ref[t, lo : lo + n]
+
+
+def run_join(start, *arrays):
+    return pl.pallas_call(
+        join_kernel,
+        out_shape=jax.ShapeDtypeStruct((FR // 2, 4 * OWN + 2 * HALO + 2 * CHALO, COLS, CH), BF16),
+        in_specs=in_vmem(4),
+        out_specs=pl.BlockSpec(memory_space=pltpu.VMEM),
+        compiler_params=pltpu.CompilerParams(vmem_limit_bytes=8 * 2**20),
+        name="join",
+    )(start, *arrays)
 
 
 def in_vmem(n):
@@ -215,7 +260,7 @@
             pltpu.VMEM((FR, (OWN + 2 * CHALO) * COLS, CH), F32),
             pltpu.VMEM((LAYERS, PART, CH), BF16),
         ],
-        compiler_params=pltpu.CompilerParams(vmem_limit_bytes=44 * 2**20),
+        compiler_params=pltpu.CompilerParams(vmem_limit_bytes=28 * 2**20),
         cost_estimate=pl.CostEstimate(
             flops=9_000_000_000, bytes_accessed=6_000_000, transcendentals=1_000_000
         ),
@@ -224,7 +269,6 @@
 
 
 def run_kernel_grad(pos, *arrays):
-    cells = LAYERS * FR * OWN * COLS
     return pl.pallas_call(
         kernel_grad_kernel,
         out_shape=(
@@ -235,11 +279,11 @@
         out_specs=(pl.BlockSpec(memory_space=pltpu.VMEM),) * 2,
         scratch_shapes=[
             pltpu.VMEM((PART, CH), BF16),
-            pltpu.VMEM((cells, PLANE), BF16),
-            pltpu.VMEM((cells, 3 * CH), BF16),
+            pltpu.VMEM((3, LAYERS * FR, (OWN + 2) * COLS, CH), BF16),
+            pltpu.VMEM((LAYERS, FR + 2, OWN * COLS, CH), BF16),
             pltpu.VMEM((KC, CH), F32),
         ],
-        compiler_params=pltpu.CompilerParams(vmem_limit_bytes=32 * 2**20),
+        compiler_params=pltpu.CompilerParams(vmem_limit_bytes=24 * 2**20),
         cost_estimate=pl.CostEstimate(
             flops=1_800_000_000, bytes_accessed=4_000_000, transcendentals=0
         ),
@@ -271,6 +315,7 @@
     half = lax.dynamic_slice_in_dim(w, tm * HALF, HALF, 0)
     left, right = along(half, 1), along(half, -1)
     got = [left, right, along(left[: HALF // 2], 1), along(right[HALF // 2 :], -1)]
+    start = zero_after(*got[2:])
     crossed = [swap(g) for g in got]
 
     x = lax.dynamic_index_in_dim(inputs, seg, 0, keepdims=False)
@@ -281,9 +326,7 @@
         jnp.concatenate([x[:, rows - HALO :], c[:, rows - CHALO :]], 1), ("z", "y"), down
     )
     after = lax.ppermute(jnp.concatenate([x[:, :HALO], c[:, :CHALO]], 1), ("z", "y"), up)
-    mine = jnp.concatenate(
-        [before[:, :HALO], x, after[:, :HALO], before[:, HALO:], c, after[:, HALO:]], 1
-    )
+    mine = run_join(start, before, after, x, c)
     other = swap(mine)
 
     parts = run_layers(spaces * rows, pos, mine, other, w, *got, *crossed)

time: 126 us -> 126 us (level)
  starting transfers between devices: 36.5 us -> 30.1 us
  waiting for transfers between devices: 19.3 us -> 23.9 us
    ppermute x10, waiting for transfers between devices: 10.1 us -> 18.5 us  [along(): return lax.ppermute(x, 'segment', ring(LAYERS, by))]
    ppermute x7, starting transfers between devices: 17.1 us -> 10.4 us  [swap(): return lax.ppermute(x, 'tm', [(0, 1), (1, 0)])]
    ppermute x1, waiting for transfers between devices: 5 us -> 0.01 us  [body(): lax.ppermute(jnp.concatenate([x[:, :HALO], c[:, :CHALO]], 1), ('z', 'y'),...]
  transfers between devices with their start and end apart: 19 -> 19, of which waited for: 8 -> 9; matrix products, arithmetic and copies ran while one was open for 0% -> 1% of each run, Pallas kernels for 0% -> 0%
where the time goes in v6:
time: 126 us; the launch traced here: 125 us
  blocking collectives  48.8 us (39%)
  starting transfers between devices  30.1 us (24%)
  waiting for transfers between devices  23.9 us (19%)
  Pallas kernels  18.5 us (15%)
  local copies, waits for them, and re-layouts  2.2 us (2%)
  other arithmetic  1.73 us (1%)
    ppermute x10, waiting for transfers between devices, along(): return lax.ppermute(x, 'segment', ring(LAYERS, by))  18.5 us
    all_to_all x1, blocking collectives, body(): pieces = lax.all_to_all(total.reshape(nz, rows_z, CH), 'z', 0, 0)  15.9 us
    ppermute x10, starting transfers between devices, along(): return lax.ppermute(x, 'segment', ring(LAYERS, by))  15.1 us
    pallas_call x1, Pallas kernels, run_layers(): pl.pallas_call(functools.partial(layers_kernel, total), out_shape=tuple((...  14.1 us
    all_to_all x1, blocking collectives, body(): pieces = lax.all_to_all(total.reshape(ny, rows_y, CH), 'y', 0, 0)  13.7 us
    ppermute x7, starting transfers between devices, swap(): return lax.ppermute(x, 'tm', [(0, 1), (1, 0)])  10.4 us
    all_to_all x1, blocking collectives, body(): whole = lax.all_to_all(jnp.broadcast_to(total, (nz, rows_z, CH)), 'z', 0, 0)  10.3 us
    all_to_all x1, blocking collectives, body(): whole = lax.all_to_all(jnp.broadcast_to(whole, (ny, rows_y, CH)), 'y', 0, 0)  8.87 us
  transfers between devices with their start and end apart: 19, of which 9 were waited for; matrix products, arithmetic and copies ran while one was open for 1% of the time, Pallas kernels for 0%

profile of v6, /device:TPU:1, one launch (start us, length us, event | category | flops | bytes accessed | tf_op | source)
XLA Modules:
  0.0 125.4 jit_solution(13452845322633505197)
XLA Ops:
  1.0 3.4 %collective-permute-start.2 = (bf16[1728,128]{1,0:T(8,128)(2,1)S(1)}, bf16[1728,128]{1,0:T(8,128)(2,1)S(1)}, u32[]{:S(2)}, u32[]{:S(2)}) collective-permute-start(bf16[1728,128]{1,0:T(8,128)(2,1)S(1)} %dynamic-slice_bitcast_fusion), channel_id=1, source_target_pairs={{0,192},{64,0},{128,64},{192,128},{1,193},{65,1},{129,65},{193,129... | collective-permute-start | bytes 1327112 | tf_op jit(solution)/shard_map/ppermute | solution.py:299
  5.5 3.3 %collective-permute-start.4 = (bf16[4,10,16,128]{3,2,1,0:T(8,128)(2,1)S(1)}, bf16[4,10,16,128]{3,2,1,0:T(8,128)(2,1)S(1)}, u32[]{:S(2)}, u32[]{:S(2)}) collective-permute-start(bf16[4,10,16,128]{3,2,1,0:T(8,128)(2,1)S(1)} %pad_maximum_fusion), channel_id=1, source_target_pairs={{0,1},{1,2},{2,3},{3,4},{4,5},{5,6},{6,7},{7,8},{8,9},{9,10},{10,1... | collective-permute-start | bytes 491528 | tf_op jit(solution)/shard_map/ppermute | solution.py:325
  8.9 4.4 %collective-permute-done.2.r3 = bf16[1728,128]{1,0:T(8,128)(2,1)S(1)} collective-permute-done((bf16[1728,128]{1,0:T(8,128)(2,1)S(1)}, bf16[1728,128]{1,0:T(8,128)(2,1)S(1)}, u32[]{:S(2)}, u32[]{:S(2)}) %collective-permute-start.2) | collective-permute-done | bytes 442400 | tf_op jit(solution)/shard_map/ppermute | solution.py:299
  13.3 3.5 %collective-permute-start.3 = (bf16[864,128]{1,0:T(8,128)(2,1)S(1)}, bf16[864,128]{1,0:T(8,128)(2,1)S(1)}, u32[]{:S(2)}, u32[]{:S(2)}) collective-permute-start(bf16[864,128]{1,0:T(8,128)(2,1)S(1)} %slice.29), channel_id=1, source_target_pairs={{0,192},{64,0},{128,64},{192,128},{1,193},{65,1},{129,65},{193,129... | collective-permute-start | bytes 663560 | tf_op jit(solution)/shard_map/ppermute | solution.py:299
  16.9 1.3 %collective-permute-start.5 = (bf16[4,10,16,128]{3,2,1,0:T(8,128)(2,1)S(1)}, bf16[4,10,16,128]{3,2,1,0:T(8,128)(2,1)S(1)}, u32[]{:S(2)}, u32[]{:S(2)}) collective-permute-start(bf16[4,10,16,128]{3,2,1,0:T(8,128)(2,1)S(1)} %pad_maximum_fusion.1), channel_id=1, source_target_pairs={{1,0},{2,1},{3,2},{4,3},{5,4},{6,5},{7,6},{8,7},{9,8},{10,9},{11,1... | collective-permute-start | bytes 491528 | tf_op jit(solution)/shard_map/ppermute | solution.py:328
  18.2 1.7 %collective-permute-done.3.refs_1_.rb = bf16[864,128]{1,0:T(8,128)(2,1)S(1)} collective-permute-done((bf16[864,128]{1,0:T(8,128)(2,1)S(1)}, bf16[864,128]{1,0:T(8,128)(2,1)S(1)}, u32[]{:S(2)}, u32[]{:S(2)}) %collective-permute-start.3) | collective-permute-done | bytes 221216 | tf_op jit(solution)/shard_map/ppermute | solution.py:299
  19.9 3.2 %collective-permute-done.1.refs_0_.ra = bf16[864,128]{1,0:T(8,128)(2,1)S(1)} collective-permute-done((bf16[864,128]{1,0:T(8,128)(2,1)S(1)}, bf16[864,128]{1,0:T(8,128)(2,1)S(1)}, u32[]{:S(2)}, u32[]{:S(2)}) %collective-permute-start.1) | collective-permute-done | bytes 221216 | tf_op jit(solution)/shard_map/ppermute | solution.py:299
  24.3 2.8 %collective-permute-start.6 = (bf16[4,36,16,128]{3,2,1,0:T(8,128)(2,1)S(1)}, bf16[4,36,16,128]{3,2,1,0:T(8,128)(2,1)S(1)}, u32[]{:S(2)}, u32[]{:S(2)}) collective-permute-start(bf16[4,36,16,128]{3,2,1,0:T(8,128)(2,1)S(1)} %join.1.mine), channel_id=1, source_target_pairs={{0,32},{32,0},{1,33},{33,1},{2,34},{34,2},{3,35},{35,3},{4,36},{36... | collective-permute-start | bytes 1769480 | tf_op jit(solution)/shard_map/ppermute | solution.py:303
  28.3 2.2 %collective-permute-done.10.qb = bf16[864,128]{1,0:T(8,128)(2,1)} collective-permute-done((bf16[864,128]{1,0:T(8,128)(2,1)S(1)}, bf16[864,128]{1,0:T(8,128)(2,1)}, u32[]{:S(2)}, u32[]{:S(2)}) %collective-permute-start.10) | collective-permute-done | bytes 221216 | tf_op jit(solution)/shard_map/ppermute | solution.py:303
  30.8 14.1 %layers.1 = (bf16[1280,128]{1,0:T(8,128)(2,1)S(1)}, bf16[1280,128]{1,0:T(8,128)(2,1)S(1)}, bf16[640,128]{1,0:T(8,128)(2,1)S(1)}, bf16[640,128]{1,0:T(8,128)(2,1)S(1)}, bf16[1280,128]{1,0:T(8,128)(2,1)S(1)}) custom-call(s32[3]{0:T(128)S(1)} %pad_add_fusion.pos, bf16[4,36,16,128]{3,2,1,0:T(8,128)(2,1)S(1)} %join.1.mine, ...), custom_call_target="tpu_custom_call" | custom-call | flops 8999999488 | bytes 6000000 | tf_op jit(solution)/shard_map/layers/pallas_call | solution.py:250
  45.0 2.7 %collective-permute-start.15 = (bf16[640,128]{1,0:T(8,128)(2,1)S(1)}, bf16[640,128]{1,0:T(8,128)(2,1)S(1)}, u32[]{:S(2)}, u32[]{:S(2)}) collective-permute-start(bf16[640,128]{1,0:T(8,128)(2,1)S(1)} %get-tuple-element.16), channel_id=1, source_target_pairs={{0,192},{64,0},{128,64},{192,128},{1,193},{65,1},{129,65},{193,129... | collective-permute-start | bytes 491528 | tf_op jit(solution)/shard_map/ppermute | solution.py:299
  47.7 2.7 %collective-permute-start.12 = (bf16[1280,128]{1,0:T(8,128)(2,1)S(1)}, bf16[1280,128]{1,0:T(8,128)(2,1)S(1)}, u32[]{:S(2)}, u32[]{:S(2)}) collective-permute-start(bf16[1280,128]{1,0:T(8,128)(2,1)S(1)} %get-tuple-element.14), channel_id=1, source_target_pairs={{0,192},{64,0},{128,64},{192,128},{1,193},{65,1},{129,65},{193,129... | collective-permute-start | bytes 983048 | tf_op jit(solution)/shard_map/ppermute | solution.py:299
  51.6 2.7 %collective-permute-start.16 = (bf16[640,128]{1,0:T(8,128)(2,1)S(1)}, bf16[640,128]{1,0:T(8,128)(2,1)S(1)}, u32[]{:S(2)}, u32[]{:S(2)}) collective-permute-start(bf16[640,128]{1,0:T(8,128)(2,1)S(1)} %collective-permute-done.15), channel_id=1, source_target_pairs={{0,192},{64,0},{128,64},{192,128},{1,193},{65,1},{129,65},{193,129... | collective-permute-start | bytes 491528 | tf_op jit(solution)/shard_map/ppermute | solution.py:299
  54.3 7.9 %collective-permute-done.14.ea = bf16[640,128]{1,0:T(8,128)(2,1)S(1)} collective-permute-done((bf16[640,128]{1,0:T(8,128)(2,1)S(1)}, bf16[640,128]{1,0:T(8,128)(2,1)S(1)}, u32[]{:S(2)}, u32[]{:S(2)}) %collective-permute-start.14) | collective-permute-done | bytes 163872 | tf_op jit(solution)/shard_map/ppermute | solution.py:299
  62.2 3.3 %kernel_grad.1 = (f32[1728,128]{1,0:T(8,128)S(1)}, bf16[1728,128]{1,0:T(8,128)(2,1)S(1)}) custom-call(s32[3]{0:T(128)S(1)} %pad_add_fusion.pos, bf16[1280,128]{1,0:T(8,128)(2,1)S(1)} %get-tuple-element.12.e0, bf16[1280,128]{1,0:T(8,128)(2,1)S(1)} %collective-permute-done.11.e1, bf16[1280,128]{1,0:T(8,128)(2,1)S(1)} %collective-permute-done.12.e3, ...), custom_call_target="tpu_custom_call" | custom-call | flops 1800000000 | bytes 4000000 | tf_op jit(solution)/shard_map/kernel_grad/pallas_call | solution.py:272
  65.5 1.3 %collective-permute-start.17 = (bf16[1728,128]{1,0:T(8,128)(2,1)S(1)}, bf16[1728,128]{1,0:T(8,128)(2,1)S(1)}, u32[]{:S(2)}, u32[]{:S(2)}) collective-permute-start(bf16[1728,128]{1,0:T(8,128)(2,1)S(1)} %get-tuple-element.18), channel_id=1, source_target_pairs={{0,32},{32,0},{1,33},{33,1},{2,34},{34,2},{3,35},{35,3},{4,36},{36... | collective-permute-start | bytes 1327112 | tf_op jit(solution)/shard_map/ppermute | solution.py:303
  66.8 1.4 %collective-permute-done.17 = bf16[1728,128]{1,0:T(8,128)(2,1)S(1)} collective-permute-done((bf16[1728,128]{1,0:T(8,128)(2,1)S(1)}, bf16[1728,128]{1,0:T(8,128)(2,1)S(1)}, u32[]{:S(2)}, u32[]{:S(2)}) %collective-permute-start.17) | collective-permute-done | bytes 442400 | tf_op jit(solution)/shard_map/ppermute | solution.py:303
  68.3 13.7 %all_to_all.20 = bf16[4,432,128]{2,1,0:T(8,128)(2,1)S(1)} all-to-all(bf16[4,432,128]{2,1,0:T(8,128)(2,1)S(1)} %bitcast.21), channel_id=1, replica_groups=mesh['segment'=4,'tm'=2,'z'=8,'y'=4] {'y'}, dimensions={0} | all-to-all | bytes 884736 | tf_op jit(solution)/shard_map/all_to_all | solution.py:339
  82.1 15.9 %all_to_all.21 = bf16[8,64,128]{2,1,0:T(8,128)(2,1)S(1)} all-to-all(bf16[8,64,128]{2,1,0:T(8,128)(2,1)S(1)} %bitcast.23), channel_id=1, replica_groups=mesh['segment'=4,'tm'=2,'z'=8,'y'=4] {'z'}, dimensions={0} | all-to-all | bytes 262144 | tf_op jit(solution)/shard_map/all_to_all | solution.py:343
  98.1 10.3 %all_to_all.22 = bf16[8,64,128]{2,1,0:T(8,128)(2,1)S(1)} all-to-all(bf16[8,64,128]{2,1,0:T(8,128)(2,1)S(1)} %broadcast_in_dim.7), channel_id=1, replica_groups=mesh['segment'=4,'tm'=2,'z'=8,'y'=4] {'z'}, dimensions={0} | all-to-all | bytes 262144 | tf_op jit(solution)/shard_map/all_to_all | solution.py:345
  108.5 8.9 %all_to_all.23 = bf16[4,432,128]{2,1,0:T(8,128)(2,1)S(1)} all-to-all(bf16[4,432,128]{2,1,0:T(8,128)(2,1)S(1)} %broadcast_in_dim.8), channel_id=1, replica_groups=mesh['segment'=4,'tm'=2,'z'=8,'y'=4] {'y'}, dimensions={0} | all-to-all | bytes 884736 | tf_op jit(solution)/shard_map/all_to_all | solution.py:347
  117.4 5.2 %collective-permute-start.18 = (bf16[1728,128]{1,0:T(8,128)(2,1)S(1)}, bf16[1728,128]{1,0:T(8,128)(2,1)S(1)}, u32[]{:S(2)}, u32[]{:S(2)}) collective-permute-start(bf16[1728,128]{1,0:T(8,128)(2,1)S(1)} %bitcast.22), channel_id=1, source_target_pairs={{0,32},{32,0},{1,33},{33,1},{2,34},{34,2},{3,35},{35,3},{4,36},{36... | collective-permute-start | bytes 1327112 | tf_op jit(solution)/shard_map/ppermute | solution.py:303
  122.6 1.4 %collective-permute-done.18 = bf16[1728,128]{1,0:T(8,128)(2,1)S(1)} collective-permute-done((bf16[1728,128]{1,0:T(8,128)(2,1)S(1)}, bf16[1728,128]{1,0:T(8,128)(2,1)S(1)}, u32[]{:S(2)}, u32[]{:S(2)}) %collective-permute-start.18) | collective-permute-done | bytes 442400 | tf_op jit(solution)/shard_map/ppermute | solution.py:303
  124.1 1.3 %maximum_convert_fusion = f32[1,3456,128]{2,1,0:T(8,128)} fusion(bf16[1,1728,128]{2,1,0:T(8,128)(2,1)S(1)} %get-tuple-element.20, bf16[1,1728,128]{2,1,0:T(8,128)(2,1)S(1)} %get-tuple-element.19), kind=kLoop, calls=%fused_computation | loop fusion | flops 1769472 | bytes 2654208 | tf_op jit(solution)/shard_map/convert_element_type | solution.py:352
  (42 shorter events, 6.5 us)
Async XLA Ops:
  1.0 12.2 %collective-permute-start.2 = (bf16[1728,128]{1,0:T(8,128)(2,1)S(1)}, bf16[1728,128]{1,0:T(8,128)(2,1)S(1)}, u32[]{:S(2)}, u32[]{:S(2)}) collective-permute-start(bf16[1728,128]{1,0:T(8,128)(2,1)S(1)} %dynamic-slice_bitcast_fusion), channel_id=1, source_target_pairs={{0,192},{64,0},{128,64},{192,128},{1,193},{65,1},{129,65},{193,129... | collective-permute-start | bytes 1327112 | tf_op jit(solution)/shard_map/ppermute | solution.py:299
  4.4 12.3 %collective-permute-start = (bf16[1728,128]{1,0:T(8,128)(2,1)S(1)}, bf16[1728,128]{1,0:T(8,128)(2,1)S(1)}, u32[]{:S(2)}, u32[]{:S(2)}) collective-permute-start(bf16[1728,128]{1,0:T(8,128)(2,1)S(1)} %dynamic-slice_bitcast_fusion), channel_id=1, source_target_pairs={{0,64},{64,128},{128,192},{192,0},{1,65},{65,129},{129,193},{193,1... | collective-permute-start | bytes 1327112 | tf_op jit(solution)/shard_map/ppermute | solution.py:299
  5.4 25.4 %copy-start = (bf16[1,3456,128]{2,1,0:T(8,128)(2,1)S(1)}, bf16[1,3456,128]{2,1,0:T(8,128)(2,1)}, u32[]{:S(2)}) copy-start(bf16[1,3456,128]{2,1,0:T(8,128)(2,1)} %param.4) | copy-start | bytes 2654212
  5.5 18.2 %collective-permute-start.4 = (bf16[4,10,16,128]{3,2,1,0:T(8,128)(2,1)S(1)}, bf16[4,10,16,128]{3,2,1,0:T(8,128)(2,1)S(1)}, u32[]{:S(2)}, u32[]{:S(2)}) collective-permute-start(bf16[4,10,16,128]{3,2,1,0:T(8,128)(2,1)S(1)} %pad_maximum_fusion), channel_id=1, source_target_pairs={{0,1},{1,2},{2,3},{3,4},{4,5},{5,6},{6,7},{7,8},{8,9},{9,10},{10,1... | collective-permute-start | bytes 491528 | tf_op jit(solution)/shard_map/ppermute | solution.py:325
  13.3 6.7 %collective-permute-start.3 = (bf16[864,128]{1,0:T(8,128)(2,1)S(1)}, bf16[864,128]{1,0:T(8,128)(2,1)S(1)}, u32[]{:S(2)}, u32[]{:S(2)}) collective-permute-start(bf16[864,128]{1,0:T(8,128)(2,1)S(1)} %slice.29), channel_id=1, source_target_pairs={{0,192},{64,0},{128,64},{192,128},{1,193},{65,1},{129,65},{193,129... | collective-permute-start | bytes 663560 | tf_op jit(solution)/shard_map/ppermute | solution.py:299
  16.8 6.4 %collective-permute-start.1 = (bf16[864,128]{1,0:T(8,128)(2,1)S(1)}, bf16[864,128]{1,0:T(8,128)(2,1)S(1)}, u32[]{:S(2)}, u32[]{:S(2)}) collective-permute-start(bf16[864,128]{1,0:T(8,128)(2,1)S(1)} %slice.28), channel_id=1, source_target_pairs={{0,64},{64,128},{128,192},{192,0},{1,65},{65,129},{129,193},{193,1... | collective-permute-start | bytes 663560 | tf_op jit(solution)/shard_map/ppermute | solution.py:299
  16.9 6.8 %collective-permute-start.5 = (bf16[4,10,16,128]{3,2,1,0:T(8,128)(2,1)S(1)}, bf16[4,10,16,128]{3,2,1,0:T(8,128)(2,1)S(1)}, u32[]{:S(2)}, u32[]{:S(2)}) collective-permute-start(bf16[4,10,16,128]{3,2,1,0:T(8,128)(2,1)S(1)} %pad_maximum_fusion.1), channel_id=1, source_target_pairs={{1,0},{2,1},{3,2},{4,3},{5,4},{6,5},{7,6},{8,7},{9,8},{10,9},{11,1... | collective-permute-start | bytes 491528 | tf_op jit(solution)/shard_map/ppermute | solution.py:328
  24.3 6.5 %collective-permute-start.6 = (bf16[4,36,16,128]{3,2,1,0:T(8,128)(2,1)S(1)}, bf16[4,36,16,128]{3,2,1,0:T(8,128)(2,1)S(1)}, u32[]{:S(2)}, u32[]{:S(2)}) collective-permute-start(bf16[4,36,16,128]{3,2,1,0:T(8,128)(2,1)S(1)} %join.1.mine), channel_id=1, source_target_pairs={{0,32},{32,0},{1,33},{33,1},{2,34},{34,2},{3,35},{35,3},{4,36},{36... | collective-permute-start | bytes 1769480 | tf_op jit(solution)/shard_map/ppermute | solution.py:303
  27.2 3.3 %collective-permute-start.8 = (bf16[1728,128]{1,0:T(8,128)(2,1)S(1)}, bf16[1728,128]{1,0:T(8,128)(2,1)}, u32[]{:S(2)}, u32[]{:S(2)}) collective-permute-start(bf16[1728,128]{1,0:T(8,128)(2,1)S(1)} %collective-permute-done.2.r3), channel_id=1, source_target_pairs={{0,32},{32,0},{1,33},{33,1},{2,34},{34,2},{3,35},{35,3},{4,36},{36... | collective-permute-start | bytes 1327112 | tf_op jit(solution)/shard_map/ppermute | solution.py:303
  27.3 3.6 %collective-permute-start.7 = (bf16[1728,128]{1,0:T(8,128)(2,1)S(1)}, bf16[1728,128]{1,0:T(8,128)(2,1)}, u32[]{:S(2)}, u32[]{:S(2)}) collective-permute-start(bf16[1728,128]{1,0:T(8,128)(2,1)S(1)} %collective-permute-done.r1), channel_id=1, source_target_pairs={{0,32},{32,0},{1,33},{33,1},{2,34},{34,2},{3,35},{35,3},{4,36},{36... | collective-permute-start | bytes 1327112 | tf_op jit(solution)/shard_map/ppermute | solution.py:303
  27.7 2.8 %collective-permute-start.10 = (bf16[864,128]{1,0:T(8,128)(2,1)S(1)}, bf16[864,128]{1,0:T(8,128)(2,1)}, u32[]{:S(2)}, u32[]{:S(2)}) collective-permute-start(bf16[864,128]{1,0:T(8,128)(2,1)S(1)} %collective-permute-done.3.refs_1_.rb), channel_id=1, source_target_pairs={{0,32},{32,0},{1,33},{33,1},{2,34},{34,2},{3,35},{35,3},{4,36},{36... | collective-permute-start | bytes 663560 | tf_op jit(solution)/shard_map/ppermute | solution.py:303
  27.8 3.0 %collective-permute-start.9 = (bf16[864,128]{1,0:T(8,128)(2,1)S(1)}, bf16[864,128]{1,0:T(8,128)(2,1)}, u32[]{:S(2)}, u32[]{:S(2)}) collective-permute-start(bf16[864,128]{1,0:T(8,128)(2,1)S(1)} %collective-permute-done.1.refs_0_.ra), channel_id=1, source_target_pairs={{0,32},{32,0},{1,33},{33,1},{2,34},{34,2},{3,35},{35,3},{4,36},{36... | collective-permute-start | bytes 663560 | tf_op jit(solution)/shard_map/ppermute | solution.py:303
  44.9 6.7 %collective-permute-start.13 = (bf16[640,128]{1,0:T(8,128)(2,1)S(1)}, bf16[640,128]{1,0:T(8,128)(2,1)S(1)}, u32[]{:S(2)}, u32[]{:S(2)}) collective-permute-start(bf16[640,128]{1,0:T(8,128)(2,1)S(1)} %get-tuple-element.15), channel_id=1, source_target_pairs={{0,64},{64,128},{128,192},{192,0},{1,65},{65,129},{129,193},{193,1... | collective-permute-start | bytes 491528 | tf_op jit(solution)/shard_map/ppermute | solution.py:299
  45.0 6.6 %collective-permute-start.15 = (bf16[640,128]{1,0:T(8,128)(2,1)S(1)}, bf16[640,128]{1,0:T(8,128)(2,1)S(1)}, u32[]{:S(2)}, u32[]{:S(2)}) collective-permute-start(bf16[640,128]{1,0:T(8,128)(2,1)S(1)} %get-tuple-element.16), channel_id=1, source_target_pairs={{0,192},{64,0},{128,64},{192,128},{1,193},{65,1},{129,65},{193,129... | collective-permute-start | bytes 491528 | tf_op jit(solution)/shard_map/ppermute | solution.py:299
  47.7 14.5 %collective-permute-start.11 = (bf16[1280,128]{1,0:T(8,128)(2,1)S(1)}, bf16[1280,128]{1,0:T(8,128)(2,1)S(1)}, u32[]{:S(2)}, u32[]{:S(2)}) collective-permute-start(bf16[1280,128]{1,0:T(8,128)(2,1)S(1)} %get-tuple-element.13), channel_id=1, source_target_pairs={{0,64},{64,128},{128,192},{192,0},{1,65},{65,129},{129,193},{193,1... | collective-permute-start | bytes 983048 | tf_op jit(solution)/shard_map/ppermute | solution.py:299
  47.7 14.5 %collective-permute-start.12 = (bf16[1280,128]{1,0:T(8,128)(2,1)S(1)}, bf16[1280,128]{1,0:T(8,128)(2,1)S(1)}, u32[]{:S(2)}, u32[]{:S(2)}) collective-permute-start(bf16[1280,128]{1,0:T(8,128)(2,1)S(1)} %get-tuple-element.14), channel_id=1, source_target_pairs={{0,192},{64,0},{128,64},{192,128},{1,193},{65,1},{129,65},{193,129... | collective-permute-start | bytes 983048 | tf_op jit(solution)/shard_map/ppermute | solution.py:299
  51.6 10.5 %collective-permute-start.14 = (bf16[640,128]{1,0:T(8,128)(2,1)S(1)}, bf16[640,128]{1,0:T(8,128)(2,1)S(1)}, u32[]{:S(2)}, u32[]{:S(2)}) collective-permute-start(bf16[640,128]{1,0:T(8,128)(2,1)S(1)} %collective-permute-done.13), channel_id=1, source_target_pairs={{0,64},{64,128},{128,192},{192,0},{1,65},{65,129},{129,193},{193,1... | collective-permute-start | bytes 491528 | tf_op jit(solution)/shard_map/ppermute | solution.py:299
  51.6 10.5 %collective-permute-start.16 = (bf16[640,128]{1,0:T(8,128)(2,1)S(1)}, bf16[640,128]{1,0:T(8,128)(2,1)S(1)}, u32[]{:S(2)}, u32[]{:S(2)}) collective-permute-start(bf16[640,128]{1,0:T(8,128)(2,1)S(1)} %collective-permute-done.15), channel_id=1, source_target_pairs={{0,192},{64,0},{128,64},{192,128},{1,193},{65,1},{129,65},{193,129... | collective-permute-start | bytes 491528 | tf_op jit(solution)/shard_map/ppermute | solution.py:299
  65.5 2.7 %collective-permute-start.17 = (bf16[1728,128]{1,0:T(8,128)(2,1)S(1)}, bf16[1728,128]{1,0:T(8,128)(2,1)S(1)}, u32[]{:S(2)}, u32[]{:S(2)}) collective-permute-start(bf16[1728,128]{1,0:T(8,128)(2,1)S(1)} %get-tuple-element.18), channel_id=1, source_target_pairs={{0,32},{32,0},{1,33},{33,1},{2,34},{34,2},{3,35},{35,3},{4,36},{36... | collective-permute-start | bytes 1327112 | tf_op jit(solution)/shard_map/ppermute | solution.py:303
  117.4 6.6 %collective-permute-start.18 = (bf16[1728,128]{1,0:T(8,128)(2,1)S(1)}, bf16[1728,128]{1,0:T(8,128)(2,1)S(1)}, u32[]{:S(2)}, u32[]{:S(2)}) collective-permute-start(bf16[1728,128]{1,0:T(8,128)(2,1)S(1)} %bitcast.22), channel_id=1, source_target_pairs={{0,32},{32,0},{1,33},{33,1},{2,34},{34,2},{3,35},{35,3},{4,36},{36... | collective-permute-start | bytes 1327112 | tf_op jit(solution)/shard_map/ppermute | solution.py:303

commit v7 on v6

--- a/solution.py
+++ b/solution.py
@@ -62,7 +62,7 @@
 def layers_kernel(
     total, pos, mine, other, w0, r1, r3, ra, rb, q1, q3, qa, qb, *rest
 ):
-    o0, o1, oa, ob, o3, wz, wb, cols, fac, grad, part = rest
+    part, wz, wb, cols, fac, grad = rest
     seg, tm, first = pos[0], pos[1], pos[2]
     step = PLANE + KC
     zero = jnp.zeros((PLANE, CH), BF16)
@@ -159,18 +159,14 @@
                         grad[t, :cells] = new
                     set_delta(l - 1, t, new * fac[l - 1, t, :cells], dst)
 
-    for d, lo, out in ((0, 0, o0), (1, 0, o1), (2, 0, oa), (2, PART // 2, ob), (3, 0, o3)):
-        out[...] = part[lax.rem(seg + d, LAYERS), lo : lo + out.shape[0]]
-
-
-def kernel_grad_kernel(pos, e0, e1, e3, ea, eb, keep, send, e2, cols, deltas, wg):
+
+def kernel_grad_kernel(pos, parts, keep, send, cols, deltas, wg):
     tm = pos[1]
-    e2[: PART // 2] = ea[...]
-    e2[PART // 2 :] = eb[...]
     cells = OWN * COLS
     width = cells + 2 * COLS
     total = LAYERS * FR * cells
-    for m, e in enumerate((e0, e1, e2, e3)):
+    for m in range(LAYERS):
+        e = parts.at[m]
         for t in range(FR):
             frame = e[t * width : (t + 1) * width]
             before, _, after = shifted(frame.astype(F32))
@@ -246,19 +242,17 @@
 
 def run_layers(total, pos, *arrays):
     span = OWN + 2 * HALO
-    lengths = (PART, PART, PART // 2, PART // 2, PART)
     return pl.pallas_call(
         functools.partial(layers_kernel, total),
-        out_shape=tuple(jax.ShapeDtypeStruct((n, CH), BF16) for n in lengths),
+        out_shape=jax.ShapeDtypeStruct((LAYERS, PART, CH), BF16),
         in_specs=in_vmem(len(arrays)),
-        out_specs=(pl.BlockSpec(memory_space=pltpu.VMEM),) * len(lengths),
+        out_specs=pl.BlockSpec(memory_space=pltpu.VMEM),
         scratch_shapes=[
             pltpu.VMEM((PLANE + LAYERS * (PLANE + KC), CH), BF16),
             pltpu.VMEM((PLANE + (LAYERS - 1) * (PLANE + KC), CH), BF16),
             pltpu.VMEM((2, FR * 3, span * COLS, CH), BF16),
             pltpu.VMEM((LAYERS - 1, FR, (OWN + 2 * CHALO) * COLS, CH), F32),
             pltpu.VMEM((FR, (OWN + 2 * CHALO) * COLS, CH), F32),
-            pltpu.VMEM((LAYERS, PART, CH), BF16),
         ],
         compiler_params=pltpu.CompilerParams(vmem_limit_bytes=28 * 2**20),
         cost_estimate=pl.CostEstimate(
@@ -278,7 +272,6 @@
         in_specs=in_vmem(len(arrays)),
         out_specs=(pl.BlockSpec(memory_space=pltpu.VMEM),) * 2,
         scratch_shapes=[
-            pltpu.VMEM((PART, CH), BF16),
             pltpu.VMEM((3, LAYERS * FR, (OWN + 2) * COLS, CH), BF16),
             pltpu.VMEM((LAYERS, FR + 2, OWN * COLS, CH), BF16),
             pltpu.VMEM((KC, CH), F32),
@@ -330,9 +323,8 @@
     other = swap(mine)
 
     parts = run_layers(spaces * rows, pos, mine, other, w, *got, *crossed)
-    far_a, far_b = along(parts[2], 1), along(parts[3], -1)
-    near = [along(parts[1], 1), along(parts[4], -1)]
-    keep, send = run_kernel_grad(pos, parts[0], *near, along(far_a, 1), along(far_b, -1))
+    parts = lax.all_to_all(parts, "segment", 0, 0)
+    keep, send = run_kernel_grad(pos, parts)
 
     total = (keep + swap(send).astype(F32)).astype(BF16)
     rows_y = HALF // ny

time: 126 us -> 130 us (1.032)
  blocking collectives: 48.8 us -> 69.6 us
  waiting for transfers between devices: 23.9 us -> 14.8 us
  starting transfers between devices: 30.1 us -> 22.6 us
    all_to_all x0 -> x1, blocking collectives: none -> 20.5 us  [body(): parts = lax.all_to_all(parts, 'segment', 0, 0)]
    ppermute x10 -> x4, waiting for transfers between devices: 18.5 us -> 9.37 us  [along(): return lax.ppermute(x, 'segment', ring(LAYERS, by))]
    ppermute x10 -> x4, starting transfers between devices: 15.1 us -> 6.96 us  [along(): return lax.ppermute(x, 'segment', ring(LAYERS, by))]
  transfers between devices with their start and end apart: 19 -> 13, of which waited for: 9 -> 7; matrix products, arithmetic and copies ran while one was open for 1% -> 1% of each run, Pallas kernels for 0% -> 0%
where the time goes in v7:
time: 130 us; the launch traced here: 129 us
  blocking collectives  69.6 us (54%)
  starting transfers between devices  22.6 us (17%)
  Pallas kernels  18.3 us (14%)
  waiting for transfers between devices  14.8 us (11%)
  local copies, waits for them, and re-layouts  2.2 us (2%)
  other arithmetic  1.73 us (1%)
    all_to_all x1, blocking collectives, body(): parts = lax.all_to_all(parts, 'segment', 0, 0)  20.5 us
    all_to_all x1, blocking collectives, body(): pieces = lax.all_to_all(total.reshape(nz, rows_z, CH), 'z', 0, 0)  15.9 us
    pallas_call x1, Pallas kernels, run_layers(): pl.pallas_call(functools.partial(layers_kernel, total), out_shape=jax.Sha...  14 us
    all_to_all x1, blocking collectives, body(): pieces = lax.all_to_all(total.reshape(ny, rows_y, CH), 'y', 0, 0)  14 us
    ppermute x7, starting transfers between devices, swap(): return lax.ppermute(x, 'tm', [(0, 1), (1, 0)])  11 us
    all_to_all x1, blocking collectives, body(): whole = lax.all_to_all(jnp.broadcast_to(total, (nz, rows_z, CH)), 'z', 0, 0)  10.3 us
    ppermute x4, waiting for transfers between devices, along(): return lax.ppermute(x, 'segment', ring(LAYERS, by))  9.37 us
    all_to_all x1, blocking collectives, body(): whole = lax.all_to_all(jnp.broadcast_to(whole, (ny, rows_y, CH)), 'y', 0, 0)  8.87 us
  transfers between devices with their start and end apart: 13, of which 7 were waited for; matrix products, arithmetic and copies ran while one was open for 1% of the time, Pallas kernels for 0%

profile of v7, /device:TPU:1, one launch (start us, length us, event | category | flops | bytes accessed | tf_op | source)
XLA Modules:
  0.0 129.4 jit_solution(12963666830748286868)
XLA Ops:
  0.0 1.0 dynamic-slice_bitcast_fusion
  1.0 3.4 %collective-permute-start.2 = (bf16[1728,128]{1,0:T(8,128)(2,1)S(1)}, bf16[1728,128]{1,0:T(8,128)(2,1)S(1)}, u32[]{:S(2)}, u32[]{:S(2)}) collective-permute-start(bf16[1728,128]{1,0:T(8,128)(2,1)S(1)} %dynamic-slice_bitcast_fusion), channel_id=1, source_target_pairs={{0,192},{64,0},{128,64},{192,128},{1,193},{65,1},{129,65},{193,129... | collective-permute-start | bytes 1327112 | tf_op jit(solution)/shard_map/ppermute | solution.py:292
  4.4 1.0 dynamic-slice_bitcast_fusion.1
  5.5 3.3 %collective-permute-start.4 = (bf16[4,10,16,128]{3,2,1,0:T(8,128)(2,1)S(1)}, bf16[4,10,16,128]{3,2,1,0:T(8,128)(2,1)S(1)}, u32[]{:S(2)}, u32[]{:S(2)}) collective-permute-start(bf16[4,10,16,128]{3,2,1,0:T(8,128)(2,1)S(1)} %pad_maximum_fusion), channel_id=1, source_target_pairs={{0,1},{1,2},{2,3},{3,4},{4,5},{5,6},{6,7},{7,8},{8,9},{9,10},{10,1... | collective-permute-start | bytes 491528 | tf_op jit(solution)/shard_map/ppermute | solution.py:318
  8.9 4.4 %collective-permute-done.2.r3 = bf16[1728,128]{1,0:T(8,128)(2,1)S(1)} collective-permute-done((bf16[1728,128]{1,0:T(8,128)(2,1)S(1)}, bf16[1728,128]{1,0:T(8,128)(2,1)S(1)}, u32[]{:S(2)}, u32[]{:S(2)}) %collective-permute-start.2) | collective-permute-done | bytes 442400 | tf_op jit(solution)/shard_map/ppermute | solution.py:292
  13.3 3.5 %collective-permute-start.3 = (bf16[864,128]{1,0:T(8,128)(2,1)S(1)}, bf16[864,128]{1,0:T(8,128)(2,1)S(1)}, u32[]{:S(2)}, u32[]{:S(2)}) collective-permute-start(bf16[864,128]{1,0:T(8,128)(2,1)S(1)} %slice.29), channel_id=1, source_target_pairs={{0,192},{64,0},{128,64},{192,128},{1,193},{65,1},{129,65},{193,129... | collective-permute-start | bytes 663560 | tf_op jit(solution)/shard_map/ppermute | solution.py:292
  16.9 1.3 collective-permute-start.5
  18.2 1.7 %collective-permute-done.3.refs_1_.rb = bf16[864,128]{1,0:T(8,128)(2,1)S(1)} collective-permute-done((bf16[864,128]{1,0:T(8,128)(2,1)S(1)}, bf16[864,128]{1,0:T(8,128)(2,1)S(1)}, u32[]{:S(2)}, u32[]{:S(2)}) %collective-permute-start.3) | collective-permute-done | bytes 221216 | tf_op jit(solution)/shard_map/ppermute | solution.py:292
  19.9 3.2 %collective-permute-done.1.refs_0_.ra = bf16[864,128]{1,0:T(8,128)(2,1)S(1)} collective-permute-done((bf16[864,128]{1,0:T(8,128)(2,1)S(1)}, bf16[864,128]{1,0:T(8,128)(2,1)S(1)}, u32[]{:S(2)}, u32[]{:S(2)}) %collective-permute-start.1) | collective-permute-done | bytes 221216 | tf_op jit(solution)/shard_map/ppermute | solution.py:292
  23.7 0.6 join.1.mine
  24.3 2.8 %collective-permute-start.6 = (bf16[4,36,16,128]{3,2,1,0:T(8,128)(2,1)S(1)}, bf16[4,36,16,128]{3,2,1,0:T(8,128)(2,1)S(1)}, u32[]{:S(2)}, u32[]{:S(2)}) collective-permute-start(bf16[4,36,16,128]{3,2,1,0:T(8,128)(2,1)S(1)} %join.1.mine), channel_id=1, source_target_pairs={{0,32},{32,0},{1,33},{33,1},{2,34},{34,2},{3,35},{35,3},{4,36},{36... | collective-permute-start | bytes 1769480 | tf_op jit(solution)/shard_map/ppermute | solution.py:296
  28.3 2.2 %collective-permute-done.10.qb = bf16[864,128]{1,0:T(8,128)(2,1)} collective-permute-done((bf16[864,128]{1,0:T(8,128)(2,1)S(1)}, bf16[864,128]{1,0:T(8,128)(2,1)}, u32[]{:S(2)}, u32[]{:S(2)}) %collective-permute-start.10) | collective-permute-done | bytes 221216 | tf_op jit(solution)/shard_map/ppermute | solution.py:296
  30.8 14.0 %layers.1 = bf16[4,1280,128]{2,1,0:T(8,128)(2,1)S(1)} custom-call(s32[3]{0:T(128)S(1)} %pad_add_fusion.pos, bf16[4,36,16,128]{3,2,1,0:T(8,128)(2,1)S(1)} %join.1.mine, bf16[4,36,16,128]{3,2,1,0:T(8,128)(2,1)S(1)} %collective-permute-done.6.other, bf16[3456,128]{1,0:T(8,128)(2,1)S(1)} %bitcast.20, bf16[1728,128]{1,0:T(8,128)(2,1)S(1)} %collective-permute-done.r1, ...), custom_call_target="tpu_custom_call" | custom-call | flops 8999999488 | bytes 6000000 | tf_op jit(solution)/shard_map/layers/pallas_call | solution.py:245
  44.8 20.5 %all_to_all.25.parts = bf16[4,1280,128]{2,1,0:T(8,128)(2,1)S(1)} all-to-all(bf16[4,1280,128]{2,1,0:T(8,128)(2,1)S(1)} %layers.1), channel_id=1, replica_groups=mesh['segment'=4,'tm'=2,'z'=8,'y'=4] {'segment'}, dimensions={0} | all-to-all | bytes 2621440 | tf_op jit(solution)/shard_map/all_to_all | solution.py:326
  65.3 3.3 %kernel_grad.1 = (f32[1728,128]{1,0:T(8,128)S(1)}, bf16[1728,128]{1,0:T(8,128)(2,1)S(1)}) custom-call(s32[3]{0:T(128)S(1)} %pad_add_fusion.pos, bf16[4,1280,128]{2,1,0:T(8,128)(2,1)S(1)} %all_to_all.25.parts), custom_call_target="tpu_custom_call" | custom-call | flops 1800000000 | bytes 4000000 | tf_op jit(solution)/shard_map/kernel_grad/pallas_call | solution.py:266
  68.6 1.9 %collective-permute-start.11 = (bf16[1728,128]{1,0:T(8,128)(2,1)S(1)}, bf16[1728,128]{1,0:T(8,128)(2,1)S(1)}, u32[]{:S(2)}, u32[]{:S(2)}) collective-permute-start(bf16[1728,128]{1,0:T(8,128)(2,1)S(1)} %get-tuple-element.8), channel_id=1, source_target_pairs={{0,32},{32,0},{1,33},{33,1},{2,34},{34,2},{3,35},{35,3},{4,36},{36... | collective-permute-start | bytes 1327112 | tf_op jit(solution)/shard_map/ppermute | solution.py:296
  70.5 1.4 %collective-permute-done.11 = bf16[1728,128]{1,0:T(8,128)(2,1)S(1)} collective-permute-done((bf16[1728,128]{1,0:T(8,128)(2,1)S(1)}, bf16[1728,128]{1,0:T(8,128)(2,1)S(1)}, u32[]{:S(2)}, u32[]{:S(2)}) %collective-permute-start.11) | collective-permute-done | bytes 442400 | tf_op jit(solution)/shard_map/ppermute | solution.py:296
  72.1 14.0 %all_to_all.26 = bf16[4,432,128]{2,1,0:T(8,128)(2,1)S(1)} all-to-all(bf16[4,432,128]{2,1,0:T(8,128)(2,1)S(1)} %bitcast.21), channel_id=1, replica_groups=mesh['segment'=4,'tm'=2,'z'=8,'y'=4] {'y'}, dimensions={0} | all-to-all | bytes 884736 | tf_op jit(solution)/shard_map/all_to_all | solution.py:331
  86.1 15.9 %all_to_all.27 = bf16[8,64,128]{2,1,0:T(8,128)(2,1)S(1)} all-to-all(bf16[8,64,128]{2,1,0:T(8,128)(2,1)S(1)} %bitcast.23), channel_id=1, replica_groups=mesh['segment'=4,'tm'=2,'z'=8,'y'=4] {'z'}, dimensions={0} | all-to-all | bytes 262144 | tf_op jit(solution)/shard_map/all_to_all | solution.py:335
  102.1 10.3 %all_to_all.28 = bf16[8,64,128]{2,1,0:T(8,128)(2,1)S(1)} all-to-all(bf16[8,64,128]{2,1,0:T(8,128)(2,1)S(1)} %broadcast_in_dim.7), channel_id=1, replica_groups=mesh['segment'=4,'tm'=2,'z'=8,'y'=4] {'z'}, dimensions={0} | all-to-all | bytes 262144 | tf_op jit(solution)/shard_map/all_to_all | solution.py:337
  112.5 8.9 %all_to_all.29 = bf16[4,432,128]{2,1,0:T(8,128)(2,1)S(1)} all-to-all(bf16[4,432,128]{2,1,0:T(8,128)(2,1)S(1)} %broadcast_in_dim.8), channel_id=1, replica_groups=mesh['segment'=4,'tm'=2,'z'=8,'y'=4] {'y'}, dimensions={0} | all-to-all | bytes 884736 | tf_op jit(solution)/shard_map/all_to_all | solution.py:339
  121.4 5.2 %collective-permute-start.12 = (bf16[1728,128]{1,0:T(8,128)(2,1)S(1)}, bf16[1728,128]{1,0:T(8,128)(2,1)S(1)}, u32[]{:S(2)}, u32[]{:S(2)}) collective-permute-start(bf16[1728,128]{1,0:T(8,128)(2,1)S(1)} %bitcast.22), channel_id=1, source_target_pairs={{0,32},{32,0},{1,33},{33,1},{2,34},{34,2},{3,35},{35,3},{4,36},{36... | collective-permute-start | bytes 1327112 | tf_op jit(solution)/shard_map/ppermute | solution.py:296
  126.6 1.4 %collective-permute-done.12 = bf16[1728,128]{1,0:T(8,128)(2,1)S(1)} collective-permute-done((bf16[1728,128]{1,0:T(8,128)(2,1)S(1)}, bf16[1728,128]{1,0:T(8,128)(2,1)S(1)}, u32[]{:S(2)}, u32[]{:S(2)}) %collective-permute-start.12) | collective-permute-done | bytes 442400 | tf_op jit(solution)/shard_map/ppermute | solution.py:296
  128.1 1.3 %maximum_convert_fusion = f32[1,3456,128]{2,1,0:T(8,128)} fusion(bf16[1,1728,128]{2,1,0:T(8,128)(2,1)S(1)} %get-tuple-element.10, bf16[1,1728,128]{2,1,0:T(8,128)(2,1)S(1)} %get-tuple-element.9), kind=kLoop, calls=%fused_computation | loop fusion | flops 1769472 | bytes 2654208 | tf_op jit(solution)/shard_map/convert_element_type | solution.py:344
  (31 shorter events, 2.5 us)
Async XLA Ops:
  1.0 12.2 %collective-permute-start.2 = (bf16[1728,128]{1,0:T(8,128)(2,1)S(1)}, bf16[1728,128]{1,0:T(8,128)(2,1)S(1)}, u32[]{:S(2)}, u32[]{:S(2)}) collective-permute-start(bf16[1728,128]{1,0:T(8,128)(2,1)S(1)} %dynamic-slice_bitcast_fusion), channel_id=1, source_target_pairs={{0,192},{64,0},{128,64},{192,128},{1,193},{65,1},{129,65},{193,129... | collective-permute-start | bytes 1327112 | tf_op jit(solution)/shard_map/ppermute | solution.py:292
  4.4 12.3 %collective-permute-start = (bf16[1728,128]{1,0:T(8,128)(2,1)S(1)}, bf16[1728,128]{1,0:T(8,128)(2,1)S(1)}, u32[]{:S(2)}, u32[]{:S(2)}) collective-permute-start(bf16[1728,128]{1,0:T(8,128)(2,1)S(1)} %dynamic-slice_bitcast_fusion), channel_id=1, source_target_pairs={{0,64},{64,128},{128,192},{192,0},{1,65},{65,129},{129,193},{193,1... | collective-permute-start | bytes 1327112 | tf_op jit(solution)/shard_map/ppermute | solution.py:292
  5.4 25.4 %copy-start = (bf16[1,3456,128]{2,1,0:T(8,128)(2,1)S(1)}, bf16[1,3456,128]{2,1,0:T(8,128)(2,1)}, u32[]{:S(2)}) copy-start(bf16[1,3456,128]{2,1,0:T(8,128)(2,1)} %param.4) | copy-start | bytes 2654212
  5.5 18.2 %collective-permute-start.4 = (bf16[4,10,16,128]{3,2,1,0:T(8,128)(2,1)S(1)}, bf16[4,10,16,128]{3,2,1,0:T(8,128)(2,1)S(1)}, u32[]{:S(2)}, u32[]{:S(2)}) collective-permute-start(bf16[4,10,16,128]{3,2,1,0:T(8,128)(2,1)S(1)} %pad_maximum_fusion), channel_id=1, source_target_pairs={{0,1},{1,2},{2,3},{3,4},{4,5},{5,6},{6,7},{7,8},{8,9},{9,10},{10,1... | collective-permute-start | bytes 491528 | tf_op jit(solution)/shard_map/ppermute | solution.py:318
  13.3 6.7 %collective-permute-start.3 = (bf16[864,128]{1,0:T(8,128)(2,1)S(1)}, bf16[864,128]{1,0:T(8,128)(2,1)S(1)}, u32[]{:S(2)}, u32[]{:S(2)}) collective-permute-start(bf16[864,128]{1,0:T(8,128)(2,1)S(1)} %slice.29), channel_id=1, source_target_pairs={{0,192},{64,0},{128,64},{192,128},{1,193},{65,1},{129,65},{193,129... | collective-permute-start | bytes 663560 | tf_op jit(solution)/shard_map/ppermute | solution.py:292
  16.8 6.4 %collective-permute-start.1 = (bf16[864,128]{1,0:T(8,128)(2,1)S(1)}, bf16[864,128]{1,0:T(8,128)(2,1)S(1)}, u32[]{:S(2)}, u32[]{:S(2)}) collective-permute-start(bf16[864,128]{1,0:T(8,128)(2,1)S(1)} %slice.28), channel_id=1, source_target_pairs={{0,64},{64,128},{128,192},{192,0},{1,65},{65,129},{129,193},{193,1... | collective-permute-start | bytes 663560 | tf_op jit(solution)/shard_map/ppermute | solution.py:292
  16.9 6.8 %collective-permute-start.5 = (bf16[4,10,16,128]{3,2,1,0:T(8,128)(2,1)S(1)}, bf16[4,10,16,128]{3,2,1,0:T(8,128)(2,1)S(1)}, u32[]{:S(2)}, u32[]{:S(2)}) collective-permute-start(bf16[4,10,16,128]{3,2,1,0:T(8,128)(2,1)S(1)} %pad_maximum_fusion.1), channel_id=1, source_target_pairs={{1,0},{2,1},{3,2},{4,3},{5,4},{6,5},{7,6},{8,7},{9,8},{10,9},{11,1... | collective-permute-start | bytes 491528 | tf_op jit(solution)/shard_map/ppermute | solution.py:321
  24.3 6.5 %collective-permute-start.6 = (bf16[4,36,16,128]{3,2,1,0:T(8,128)(2,1)S(1)}, bf16[4,36,16,128]{3,2,1,0:T(8,128)(2,1)S(1)}, u32[]{:S(2)}, u32[]{:S(2)}) collective-permute-start(bf16[4,36,16,128]{3,2,1,0:T(8,128)(2,1)S(1)} %join.1.mine), channel_id=1, source_target_pairs={{0,32},{32,0},{1,33},{33,1},{2,34},{34,2},{3,35},{35,3},{4,36},{36... | collective-permute-start | bytes 1769480 | tf_op jit(solution)/shard_map/ppermute | solution.py:296
  27.2 3.3 %collective-permute-start.8 = (bf16[1728,128]{1,0:T(8,128)(2,1)S(1)}, bf16[1728,128]{1,0:T(8,128)(2,1)}, u32[]{:S(2)}, u32[]{:S(2)}) collective-permute-start(bf16[1728,128]{1,0:T(8,128)(2,1)S(1)} %collective-permute-done.2.r3), channel_id=1, source_target_pairs={{0,32},{32,0},{1,33},{33,1},{2,34},{34,2},{3,35},{35,3},{4,36},{36... | collective-permute-start | bytes 1327112 | tf_op jit(solution)/shard_map/ppermute | solution.py:296
  27.3 3.6 %collective-permute-start.7 = (bf16[1728,128]{1,0:T(8,128)(2,1)S(1)}, bf16[1728,128]{1,0:T(8,128)(2,1)}, u32[]{:S(2)}, u32[]{:S(2)}) collective-permute-start(bf16[1728,128]{1,0:T(8,128)(2,1)S(1)} %collective-permute-done.r1), channel_id=1, source_target_pairs={{0,32},{32,0},{1,33},{33,1},{2,34},{34,2},{3,35},{35,3},{4,36},{36... | collective-permute-start | bytes 1327112 | tf_op jit(solution)/shard_map/ppermute | solution.py:296
  27.7 2.8 %collective-permute-start.10 = (bf16[864,128]{1,0:T(8,128)(2,1)S(1)}, bf16[864,128]{1,0:T(8,128)(2,1)}, u32[]{:S(2)}, u32[]{:S(2)}) collective-permute-start(bf16[864,128]{1,0:T(8,128)(2,1)S(1)} %collective-permute-done.3.refs_1_.rb), channel_id=1, source_target_pairs={{0,32},{32,0},{1,33},{33,1},{2,34},{34,2},{3,35},{35,3},{4,36},{36... | collective-permute-start | bytes 663560 | tf_op jit(solution)/shard_map/ppermute | solution.py:296
  27.8 3.0 %collective-permute-start.9 = (bf16[864,128]{1,0:T(8,128)(2,1)S(1)}, bf16[864,128]{1,0:T(8,128)(2,1)}, u32[]{:S(2)}, u32[]{:S(2)}) collective-permute-start(bf16[864,128]{1,0:T(8,128)(2,1)S(1)} %collective-permute-done.1.refs_0_.ra), channel_id=1, source_target_pairs={{0,32},{32,0},{1,33},{33,1},{2,34},{34,2},{3,35},{35,3},{4,36},{36... | collective-permute-start | bytes 663560 | tf_op jit(solution)/shard_map/ppermute | solution.py:296
  68.6 3.3 %collective-permute-start.11 = (bf16[1728,128]{1,0:T(8,128)(2,1)S(1)}, bf16[1728,128]{1,0:T(8,128)(2,1)S(1)}, u32[]{:S(2)}, u32[]{:S(2)}) collective-permute-start(bf16[1728,128]{1,0:T(8,128)(2,1)S(1)} %get-tuple-element.8), channel_id=1, source_target_pairs={{0,32},{32,0},{1,33},{33,1},{2,34},{34,2},{3,35},{35,3},{4,36},{36... | collective-permute-start | bytes 1327112 | tf_op jit(solution)/shard_map/ppermute | solution.py:296
  121.4 6.6 %collective-permute-start.12 = (bf16[1728,128]{1,0:T(8,128)(2,1)S(1)}, bf16[1728,128]{1,0:T(8,128)(2,1)S(1)}, u32[]{:S(2)}, u32[]{:S(2)}) collective-permute-start(bf16[1728,128]{1,0:T(8,128)(2,1)S(1)} %bitcast.22), channel_id=1, source_target_pairs={{0,32},{32,0},{1,33},{33,1},{2,34},{34,2},{3,35},{35,3},{4,36},{36... | collective-permute-start | bytes 1327112 | tf_op jit(solution)/shard_map/ppermute | solution.py:296

commit v8 on v3

--- a/solution.py
+++ b/solution.py
@@ -163,30 +163,34 @@
         out[...] = part[lax.rem(seg + d, LAYERS), lo : lo + out.shape[0]]
 
 
-def kernel_grad_kernel(pos, e0, e1, e3, ea, eb, keep, send, e2, x9, d3, wg):
+def kernel_grad_kernel(pos, e0, e1, e3, ea, eb, keep, send, e2, cols, deltas, wg):
     tm = pos[1]
     e2[: PART // 2] = ea[...]
     e2[PART // 2 :] = eb[...]
     cells = OWN * COLS
     width = cells + 2 * COLS
-    nothing = jnp.zeros((cells, CH), BF16)
+    total = LAYERS * FR * cells
     for m, e in enumerate((e0, e1, e2, e3)):
         for t in range(FR):
-            at = (m * FR + t) * cells
-            frame = e[t * width : (t + 1) * width].astype(F32)
-            for lag_c, v in enumerate(shifted(frame)):
-                for lag_r in range(3):
-                    tap = (lag_r * 3 + lag_c) * CH
-                    x9[at : at + cells, tap : tap + CH] = v[lag_r * COLS : lag_r * COLS + cells]
-            for lag_t in range(3):
-                src = t + 2 - lag_t
-                row = HID + src * cells
-                d3[at : at + cells, lag_t * CH : (lag_t + 1) * CH] = (
-                    e[row : row + cells] if src < FR else nothing
-                )
-    out = lax.dot_general(
-        d3[...], x9[...], (((0,), (0,)), ((), ())), preferred_element_type=F32
-    )
+            frame = e[t * width : (t + 1) * width]
+            before, _, after = shifted(frame.astype(F32))
+            for lag_c, v in enumerate((before, frame, after)):
+                cols[lag_c, m * FR + t] = v
+            deltas[m, t] = e[HID + t * cells : HID + (t + 1) * cells]
+        for t in (FR, FR + 1):
+            deltas[m, t] = jnp.zeros((cells, CH), BF16)
+    x9 = jnp.concatenate(
+        [
+            cols[lag_c, :, lag_r * COLS : lag_r * COLS + cells].reshape(total, CH)
+            for lag_r in range(3)
+            for lag_c in range(3)
+        ],
+        1,
+    )
+    d3 = jnp.concatenate(
+        [deltas[:, 2 - lag_t : 2 - lag_t + FR].reshape(total, CH) for lag_t in range(3)], 1
+    )
+    out = lax.dot_general(d3, x9, (((0,), (0,)), ((), ())), preferred_element_type=F32)
     for lag_t in range(3):
         for tap in range(9):
             at = (lag_t * 9 + tap) * CH
@@ -224,7 +228,6 @@
 
 
 def run_kernel_grad(pos, *arrays):
-    cells = LAYERS * FR * OWN * COLS
     return pl.pallas_call(
         kernel_grad_kernel,
         out_shape=(
@@ -235,8 +238,8 @@
         out_specs=(pl.BlockSpec(memory_space=pltpu.VMEM),) * 2,
         scratch_shapes=[
             pltpu.VMEM((PART, CH), BF16),
-            pltpu.VMEM((cells, PLANE), BF16),
-            pltpu.VMEM((cells, 3 * CH), BF16),
+            pltpu.VMEM((3, LAYERS * FR, (OWN + 2) * COLS, CH), BF16),
+            pltpu.VMEM((LAYERS, FR + 2, OWN * COLS, CH), BF16),
             pltpu.VMEM((KC, CH), F32),
         ],
         compiler_params=pltpu.CompilerParams(vmem_limit_bytes=32 * 2**20),

time: 126 us -> 125 us (level)
  no operation moved by 1% of the time
where the time goes in v8:
time: 125 us
  blocking collectives  48.3 us (39%)
  starting transfers between devices  36.5 us (29%)
  waiting for transfers between devices  19.3 us (15%)
  Pallas kernels  17.5 us (14%)
  other arithmetic  1.73 us (1%)
  local copies, waits for them, and re-layouts  1.36 us (1%)
    ppermute x7, starting transfers between devices, swap(): return lax.ppermute(x, 'tm', [(0, 1), (1, 0)])  17.1 us
    all_to_all x1, blocking collectives, body(): pieces = lax.all_to_all(total.reshape(nz, rows_z, CH), 'z', 0, 0)  15.7 us
    pallas_call x1, Pallas kernels, run_layers(): pl.pallas_call(functools.partial(layers_kernel, total), out_shape=tuple((...  14.2 us
    ppermute x10, starting transfers between devices, along(): return lax.ppermute(x, 'segment', ring(LAYERS, by))  14 us
    all_to_all x1, blocking collectives, body(): pieces = lax.all_to_all(total.reshape(ny, rows_y, CH), 'y', 0, 0)  13.4 us
    all_to_all x1, blocking collectives, body(): whole = lax.all_to_all(jnp.broadcast_to(total, (nz, rows_z, CH)), 'z', 0, 0)  10.3 us
    ppermute x10, waiting for transfers between devices, along(): return lax.ppermute(x, 'segment', ring(LAYERS, by))  10.1 us
    all_to_all x1, blocking collectives, body(): whole = lax.all_to_all(jnp.broadcast_to(whole, (ny, rows_y, CH)), 'y', 0, 0)  8.87 us
  transfers between devices with their start and end apart: 19, of which 8 were waited for; matrix products, arithmetic and copies ran while one was open for 0% of the time, Pallas kernels for 0%

profile of v8, /device:TPU:1, one launch (start us, length us, event | category | flops | bytes accessed | tf_op | source)
XLA Modules:
  0.0 125.0 jit_solution(13961556722289396282)
XLA Ops:
  1.2 4.0 %collective-permute-start = (bf16[4,10,16,128]{3,2,1,0:T(8,128)(2,1)S(1)}, bf16[4,10,16,128]{3,2,1,0:T(8,128)(2,1)S(1)}, u32[]{:S(2)}, u32[]{:S(2)}) collective-permute-start(bf16[4,10,16,128]{3,2,1,0:T(8,128)(2,1)S(1)} %pad_maximum_fusion), channel_id=1, source_target_pairs={{0,1},{1,2},{2,3},{3,4},{4,5},{5,6},{6,7},{7,8},{8,9},{9,10},{10,1... | collective-permute-start | bytes 491528 | tf_op jit(solution)/shard_map/ppermute | solution.py:283
  5.3 2.6 %collective-permute-start.4 = (bf16[1728,128]{1,0:T(8,128)(2,1)S(1)}, bf16[1728,128]{1,0:T(8,128)(2,1)S(1)}, u32[]{:S(2)}, u32[]{:S(2)}) collective-permute-start(bf16[1728,128]{1,0:T(8,128)(2,1)S(1)} %dynamic-slice_bitcast_fusion), channel_id=1, source_target_pairs={{0,192},{64,0},{128,64},{192,128},{1,193},{65,1},{129,65},{193,129... | collective-permute-start | bytes 1327112 | tf_op jit(solution)/shard_map/ppermute | solution.py:258
  7.8 1.3 %collective-permute-start.1 = (bf16[4,10,16,128]{3,2,1,0:T(8,128)(2,1)S(1)}, bf16[4,10,16,128]{3,2,1,0:T(8,128)(2,1)S(1)}, u32[]{:S(2)}, u32[]{:S(2)}) collective-permute-start(bf16[4,10,16,128]{3,2,1,0:T(8,128)(2,1)S(1)} %pad_maximum_fusion.1), channel_id=1, source_target_pairs={{1,0},{2,1},{3,2},{4,3},{5,4},{6,5},{7,6},{8,7},{9,8},{10,9},{11,1... | collective-permute-start | bytes 491528 | tf_op jit(solution)/shard_map/ppermute | solution.py:286
  9.2 5.0 %collective-permute-done.1 = bf16[4,10,16,128]{3,2,1,0:T(8,128)(2,1)S(1)} collective-permute-done((bf16[4,10,16,128]{3,2,1,0:T(8,128)(2,1)S(1)}, bf16[4,10,16,128]{3,2,1,0:T(8,128)(2,1)S(1)}, u32[]{:S(2)}, u32[]{:S(2)}) %collective-permute-start.1) | collective-permute-done | bytes 163872 | tf_op jit(solution)/shard_map/ppermute | solution.py:286
  14.3 2.2 %collective-permute-start.2 = (bf16[4,36,16,128]{3,2,1,0:T(8,128)(2,1)S(1)}, bf16[4,36,16,128]{3,2,1,0:T(8,128)(2,1)S(1)}, u32[]{:S(2)}, u32[]{:S(2)}) collective-permute-start(bf16[4,36,16,128]{3,2,1,0:T(8,128)(2,1)S(1)} %slice_dynamic-update-slice_fusion.2.mine), channel_id=1, source_target_pairs={{0,32},{32,0},{1,33},{33,1},{2,34},{34,2},{3,35},{35,3},{4,36},{36... | collective-permute-start | bytes 1769480 | tf_op jit(solution)/shard_map/ppermute | solution.py:262
  16.5 3.3 %collective-permute-start.6 = (bf16[864,128]{1,0:T(8,128)(2,1)S(1)}, bf16[864,128]{1,0:T(8,128)(2,1)}, u32[]{:S(2)}, u32[]{:S(2)}) collective-permute-start(bf16[864,128]{1,0:T(8,128)(2,1)S(1)} %slice.53), channel_id=1, source_target_pairs={{0,192},{64,0},{128,64},{192,128},{1,193},{65,1},{129,65},{193,129... | collective-permute-start | bytes 663560 | tf_op jit(solution)/shard_map/ppermute | solution.py:258
  20.0 2.2 %collective-permute-start.8 = (bf16[1728,128]{1,0:T(8,128)(2,1)S(1)}, bf16[1728,128]{1,0:T(8,128)(2,1)S(1)}, u32[]{:S(2)}, u32[]{:S(2)}) collective-permute-start(bf16[1728,128]{1,0:T(8,128)(2,1)S(1)} %collective-permute-done.4.r3), channel_id=1, source_target_pairs={{0,32},{32,0},{1,33},{33,1},{2,34},{34,2},{3,35},{35,3},{4,36},{36... | collective-permute-start | bytes 1327112 | tf_op jit(solution)/shard_map/ppermute | solution.py:262
  22.7 2.8 %collective-permute-start.10 = (bf16[864,128]{1,0:T(8,128)(2,1)}, bf16[864,128]{1,0:T(8,128)(2,1)}, u32[]{:S(2)}, u32[]{:S(2)}) collective-permute-start(bf16[864,128]{1,0:T(8,128)(2,1)} %collective-permute-done.6.rb), channel_id=1, source_target_pairs={{0,32},{32,0},{1,33},{33,1},{2,34},{34,2},{3,35},{35,3},{4,36},{36... | collective-permute-start | bytes 663560 | tf_op jit(solution)/shard_map/ppermute | solution.py:262
  26.0 3.3 %collective-permute-start.9 = (bf16[864,128]{1,0:T(8,128)(2,1)}, bf16[864,128]{1,0:T(8,128)(2,1)}, u32[]{:S(2)}, u32[]{:S(2)}) collective-permute-start(bf16[864,128]{1,0:T(8,128)(2,1)} %collective-permute-done.5.ra), channel_id=1, source_target_pairs={{0,32},{32,0},{1,33},{33,1},{2,34},{34,2},{3,35},{35,3},{4,36},{36... | collective-permute-start | bytes 663560 | tf_op jit(solution)/shard_map/ppermute | solution.py:262
  29.4 1.4 %collective-permute-done.9.qa = bf16[864,128]{1,0:T(8,128)(2,1)} collective-permute-done((bf16[864,128]{1,0:T(8,128)(2,1)}, bf16[864,128]{1,0:T(8,128)(2,1)}, u32[]{:S(2)}, u32[]{:S(2)}) %collective-permute-start.9) | collective-permute-done | bytes 221216 | tf_op jit(solution)/shard_map/ppermute | solution.py:262
  30.8 14.2 %layers.1 = (bf16[1280,128]{1,0:T(8,128)(2,1)S(1)}, bf16[1280,128]{1,0:T(8,128)(2,1)S(1)}, bf16[640,128]{1,0:T(8,128)(2,1)S(1)}, bf16[640,128]{1,0:T(8,128)(2,1)S(1)}, bf16[1280,128]{1,0:T(8,128)(2,1)S(1)}) custom-call(s32[3]{0:T(128)S(1)} %pad_add_fusion.pos, bf16[4,36,16,128]{3,2,1,0:T(8,128)(2,1)S(1)} %slice_dynamic-update-slice_fusion.2.mine, ...), custom_call_target="tpu_custom_call" | custom-call | flops 8999999488 | bytes 6000000 | tf_op jit(solution)/shard_map/layers/pallas_call | solution.py:209
  45.1 2.7 %collective-permute-start.15 = (bf16[640,128]{1,0:T(8,128)(2,1)S(1)}, bf16[640,128]{1,0:T(8,128)(2,1)S(1)}, u32[]{:S(2)}, u32[]{:S(2)}) collective-permute-start(bf16[640,128]{1,0:T(8,128)(2,1)S(1)} %get-tuple-element.16), channel_id=1, source_target_pairs={{0,192},{64,0},{128,64},{192,128},{1,193},{65,1},{129,65},{193,129... | collective-permute-start | bytes 491528 | tf_op jit(solution)/shard_map/ppermute | solution.py:258
  47.7 2.7 %collective-permute-start.12 = (bf16[1280,128]{1,0:T(8,128)(2,1)S(1)}, bf16[1280,128]{1,0:T(8,128)(2,1)S(1)}, u32[]{:S(2)}, u32[]{:S(2)}) collective-permute-start(bf16[1280,128]{1,0:T(8,128)(2,1)S(1)} %get-tuple-element.14), channel_id=1, source_target_pairs={{0,192},{64,0},{128,64},{192,128},{1,193},{65,1},{129,65},{193,129... | collective-permute-start | bytes 983048 | tf_op jit(solution)/shard_map/ppermute | solution.py:258
  51.7 2.7 %collective-permute-start.16 = (bf16[640,128]{1,0:T(8,128)(2,1)S(1)}, bf16[640,128]{1,0:T(8,128)(2,1)S(1)}, u32[]{:S(2)}, u32[]{:S(2)}) collective-permute-start(bf16[640,128]{1,0:T(8,128)(2,1)S(1)} %collective-permute-done.15), channel_id=1, source_target_pairs={{0,192},{64,0},{128,64},{192,128},{1,193},{65,1},{129,65},{193,129... | collective-permute-start | bytes 491528 | tf_op jit(solution)/shard_map/ppermute | solution.py:258
  54.4 7.9 %collective-permute-done.14.ea = bf16[640,128]{1,0:T(8,128)(2,1)S(1)} collective-permute-done((bf16[640,128]{1,0:T(8,128)(2,1)S(1)}, bf16[640,128]{1,0:T(8,128)(2,1)S(1)}, u32[]{:S(2)}, u32[]{:S(2)}) %collective-permute-start.14) | collective-permute-done | bytes 163872 | tf_op jit(solution)/shard_map/ppermute | solution.py:258
  62.2 3.3 %kernel_grad.1 = (f32[1728,128]{1,0:T(8,128)S(1)}, bf16[1728,128]{1,0:T(8,128)(2,1)S(1)}) custom-call(s32[3]{0:T(128)S(1)} %pad_add_fusion.pos, bf16[1280,128]{1,0:T(8,128)(2,1)S(1)} %get-tuple-element.12.e0, bf16[1280,128]{1,0:T(8,128)(2,1)S(1)} %collective-permute-done.11.e1, bf16[1280,128]{1,0:T(8,128)(2,1)S(1)} %collective-permute-done.12.e3, ...), custom_call_target="tpu_custom_call" | custom-call | flops 1800000000 | bytes 4000000 | tf_op jit(solution)/shard_map/kernel_grad/pallas_call | solution.py:231
  66.8 1.4 %collective-permute-done.17 = bf16[1728,128]{1,0:T(8,128)(2,1)S(1)} collective-permute-done((bf16[1728,128]{1,0:T(8,128)(2,1)S(1)}, bf16[1728,128]{1,0:T(8,128)(2,1)S(1)}, u32[]{:S(2)}, u32[]{:S(2)}) %collective-permute-start.17) | collective-permute-done | bytes 442400 | tf_op jit(solution)/shard_map/ppermute | solution.py:262
  68.4 13.4 %all_to_all.20 = bf16[4,432,128]{2,1,0:T(8,128)(2,1)S(1)} all-to-all(bf16[4,432,128]{2,1,0:T(8,128)(2,1)S(1)} %bitcast.21), channel_id=1, replica_groups=mesh['segment'=4,'tm'=2,'z'=8,'y'=4] {'y'}, dimensions={0} | all-to-all | bytes 884736 | tf_op jit(solution)/shard_map/all_to_all | solution.py:299
  81.9 15.7 %all_to_all.21 = bf16[8,64,128]{2,1,0:T(8,128)(2,1)S(1)} all-to-all(bf16[8,64,128]{2,1,0:T(8,128)(2,1)S(1)} %bitcast.23), channel_id=1, replica_groups=mesh['segment'=4,'tm'=2,'z'=8,'y'=4] {'z'}, dimensions={0} | all-to-all | bytes 262144 | tf_op jit(solution)/shard_map/all_to_all | solution.py:303
  97.7 10.3 %all_to_all.22 = bf16[8,64,128]{2,1,0:T(8,128)(2,1)S(1)} all-to-all(bf16[8,64,128]{2,1,0:T(8,128)(2,1)S(1)} %broadcast_in_dim.7), channel_id=1, replica_groups=mesh['segment'=4,'tm'=2,'z'=8,'y'=4] {'z'}, dimensions={0} | all-to-all | bytes 262144 | tf_op jit(solution)/shard_map/all_to_all | solution.py:305
  108.1 8.9 %all_to_all.23 = bf16[4,432,128]{2,1,0:T(8,128)(2,1)S(1)} all-to-all(bf16[4,432,128]{2,1,0:T(8,128)(2,1)S(1)} %broadcast_in_dim.8), channel_id=1, replica_groups=mesh['segment'=4,'tm'=2,'z'=8,'y'=4] {'y'}, dimensions={0} | all-to-all | bytes 884736 | tf_op jit(solution)/shard_map/all_to_all | solution.py:307
  117.0 5.2 %collective-permute-start.18 = (bf16[1728,128]{1,0:T(8,128)(2,1)S(1)}, bf16[1728,128]{1,0:T(8,128)(2,1)S(1)}, u32[]{:S(2)}, u32[]{:S(2)}) collective-permute-start(bf16[1728,128]{1,0:T(8,128)(2,1)S(1)} %bitcast.22), channel_id=1, source_target_pairs={{0,32},{32,0},{1,33},{33,1},{2,34},{34,2},{3,35},{35,3},{4,36},{36... | collective-permute-start | bytes 1327112 | tf_op jit(solution)/shard_map/ppermute | solution.py:262
  122.2 1.4 %collective-permute-done.18 = bf16[1728,128]{1,0:T(8,128)(2,1)S(1)} collective-permute-done((bf16[1728,128]{1,0:T(8,128)(2,1)S(1)}, bf16[1728,128]{1,0:T(8,128)(2,1)S(1)}, u32[]{:S(2)}, u32[]{:S(2)}) %collective-permute-start.18) | collective-permute-done | bytes 442400 | tf_op jit(solution)/shard_map/ppermute | solution.py:262
  123.7 1.3 %maximum_convert_fusion = f32[1,3456,128]{2,1,0:T(8,128)} fusion(bf16[1,1728,128]{2,1,0:T(8,128)(2,1)S(1)} %get-tuple-element.20, bf16[1,1728,128]{2,1,0:T(8,128)(2,1)S(1)} %get-tuple-element.19), kind=kLoop, calls=%fused_computation | loop fusion | flops 1769472 | bytes 2654208 | tf_op jit(solution)/shard_map/convert_element_type | solution.py:312
  (46 shorter events, 5.6 us)
Async XLA Ops:
  0.0 5.2 %copy-start = (bf16[1,3456,128]{2,1,0:T(8,128)(2,1)S(1)}, bf16[1,3456,128]{2,1,0:T(8,128)(2,1)}, u32[]{:S(2)}) copy-start(bf16[1,3456,128]{2,1,0:T(8,128)(2,1)} %param.4) | copy-start | bytes 2654212
  1.2 8.0 %collective-permute-start = (bf16[4,10,16,128]{3,2,1,0:T(8,128)(2,1)S(1)}, bf16[4,10,16,128]{3,2,1,0:T(8,128)(2,1)S(1)}, u32[]{:S(2)}, u32[]{:S(2)}) collective-permute-start(bf16[4,10,16,128]{3,2,1,0:T(8,128)(2,1)S(1)} %pad_maximum_fusion), channel_id=1, source_target_pairs={{0,1},{1,2},{2,3},{3,4},{4,5},{5,6},{6,7},{7,8},{8,9},{9,10},{10,1... | collective-permute-start | bytes 491528 | tf_op jit(solution)/shard_map/ppermute | solution.py:283
  5.3 11.3 %collective-permute-start.4 = (bf16[1728,128]{1,0:T(8,128)(2,1)S(1)}, bf16[1728,128]{1,0:T(8,128)(2,1)S(1)}, u32[]{:S(2)}, u32[]{:S(2)}) collective-permute-start(bf16[1728,128]{1,0:T(8,128)(2,1)S(1)} %dynamic-slice_bitcast_fusion), channel_id=1, source_target_pairs={{0,192},{64,0},{128,64},{192,128},{1,193},{65,1},{129,65},{193,129... | collective-permute-start | bytes 1327112 | tf_op jit(solution)/shard_map/ppermute | solution.py:258
  7.8 12.0 %collective-permute-start.3 = (bf16[1728,128]{1,0:T(8,128)(2,1)S(1)}, bf16[1728,128]{1,0:T(8,128)(2,1)S(1)}, u32[]{:S(2)}, u32[]{:S(2)}) collective-permute-start(bf16[1728,128]{1,0:T(8,128)(2,1)S(1)} %dynamic-slice_bitcast_fusion), channel_id=1, source_target_pairs={{0,64},{64,128},{128,192},{192,0},{1,65},{65,129},{129,193},{193,1... | collective-permute-start | bytes 1327112 | tf_op jit(solution)/shard_map/ppermute | solution.py:258
  7.8 6.4 %collective-permute-start.1 = (bf16[4,10,16,128]{3,2,1,0:T(8,128)(2,1)S(1)}, bf16[4,10,16,128]{3,2,1,0:T(8,128)(2,1)S(1)}, u32[]{:S(2)}, u32[]{:S(2)}) collective-permute-start(bf16[4,10,16,128]{3,2,1,0:T(8,128)(2,1)S(1)} %pad_maximum_fusion.1), channel_id=1, source_target_pairs={{1,0},{2,1},{3,2},{4,3},{5,4},{6,5},{7,6},{8,7},{9,8},{10,9},{11,1... | collective-permute-start | bytes 491528 | tf_op jit(solution)/shard_map/ppermute | solution.py:286
  14.3 15.1 %collective-permute-start.2 = (bf16[4,36,16,128]{3,2,1,0:T(8,128)(2,1)S(1)}, bf16[4,36,16,128]{3,2,1,0:T(8,128)(2,1)S(1)}, u32[]{:S(2)}, u32[]{:S(2)}) collective-permute-start(bf16[4,36,16,128]{3,2,1,0:T(8,128)(2,1)S(1)} %slice_dynamic-update-slice_fusion.2.mine), channel_id=1, source_target_pairs={{0,32},{32,0},{1,33},{33,1},{2,34},{34,2},{3,35},{35,3},{4,36},{36... | collective-permute-start | bytes 1769480 | tf_op jit(solution)/shard_map/ppermute | solution.py:262
  16.5 6.2 %collective-permute-start.6 = (bf16[864,128]{1,0:T(8,128)(2,1)S(1)}, bf16[864,128]{1,0:T(8,128)(2,1)}, u32[]{:S(2)}, u32[]{:S(2)}) collective-permute-start(bf16[864,128]{1,0:T(8,128)(2,1)S(1)} %slice.53), channel_id=1, source_target_pairs={{0,192},{64,0},{128,64},{192,128},{1,193},{65,1},{129,65},{193,129... | collective-permute-start | bytes 663560 | tf_op jit(solution)/shard_map/ppermute | solution.py:258
  19.9 6.2 %collective-permute-start.5 = (bf16[864,128]{1,0:T(8,128)(2,1)S(1)}, bf16[864,128]{1,0:T(8,128)(2,1)}, u32[]{:S(2)}, u32[]{:S(2)}) collective-permute-start(bf16[864,128]{1,0:T(8,128)(2,1)S(1)} %slice.52), channel_id=1, source_target_pairs={{0,64},{64,128},{128,192},{192,0},{1,65},{65,129},{129,193},{193,1... | collective-permute-start | bytes 663560 | tf_op jit(solution)/shard_map/ppermute | solution.py:258
  20.0 9.5 %collective-permute-start.8 = (bf16[1728,128]{1,0:T(8,128)(2,1)S(1)}, bf16[1728,128]{1,0:T(8,128)(2,1)S(1)}, u32[]{:S(2)}, u32[]{:S(2)}) collective-permute-start(bf16[1728,128]{1,0:T(8,128)(2,1)S(1)} %collective-permute-done.4.r3), channel_id=1, source_target_pairs={{0,32},{32,0},{1,33},{33,1},{2,34},{34,2},{3,35},{35,3},{4,36},{36... | collective-permute-start | bytes 1327112 | tf_op jit(solution)/shard_map/ppermute | solution.py:262
  22.2 8.6 %collective-permute-start.7 = (bf16[1728,128]{1,0:T(8,128)(2,1)S(1)}, bf16[1728,128]{1,0:T(8,128)(2,1)}, u32[]{:S(2)}, u32[]{:S(2)}) collective-permute-start(bf16[1728,128]{1,0:T(8,128)(2,1)S(1)} %collective-permute-done.3.r1), channel_id=1, source_target_pairs={{0,32},{32,0},{1,33},{33,1},{2,34},{34,2},{3,35},{35,3},{4,36},{36... | collective-permute-start | bytes 1327112 | tf_op jit(solution)/shard_map/ppermute | solution.py:262
  22.7 6.7 %collective-permute-start.10 = (bf16[864,128]{1,0:T(8,128)(2,1)}, bf16[864,128]{1,0:T(8,128)(2,1)}, u32[]{:S(2)}, u32[]{:S(2)}) collective-permute-start(bf16[864,128]{1,0:T(8,128)(2,1)} %collective-permute-done.6.rb), channel_id=1, source_target_pairs={{0,32},{32,0},{1,33},{33,1},{2,34},{34,2},{3,35},{35,3},{4,36},{36... | collective-permute-start | bytes 663560 | tf_op jit(solution)/shard_map/ppermute | solution.py:262
  26.0 4.7 %collective-permute-start.9 = (bf16[864,128]{1,0:T(8,128)(2,1)}, bf16[864,128]{1,0:T(8,128)(2,1)}, u32[]{:S(2)}, u32[]{:S(2)}) collective-permute-start(bf16[864,128]{1,0:T(8,128)(2,1)} %collective-permute-done.5.ra), channel_id=1, source_target_pairs={{0,32},{32,0},{1,33},{33,1},{2,34},{34,2},{3,35},{35,3},{4,36},{36... | collective-permute-start | bytes 663560 | tf_op jit(solution)/shard_map/ppermute | solution.py:262
  45.0 6.7 %collective-permute-start.13 = (bf16[640,128]{1,0:T(8,128)(2,1)S(1)}, bf16[640,128]{1,0:T(8,128)(2,1)S(1)}, u32[]{:S(2)}, u32[]{:S(2)}) collective-permute-start(bf16[640,128]{1,0:T(8,128)(2,1)S(1)} %get-tuple-element.15), channel_id=1, source_target_pairs={{0,64},{64,128},{128,192},{192,0},{1,65},{65,129},{129,193},{193,1... | collective-permute-start | bytes 491528 | tf_op jit(solution)/shard_map/ppermute | solution.py:258
  45.1 6.6 %collective-permute-start.15 = (bf16[640,128]{1,0:T(8,128)(2,1)S(1)}, bf16[640,128]{1,0:T(8,128)(2,1)S(1)}, u32[]{:S(2)}, u32[]{:S(2)}) collective-permute-start(bf16[640,128]{1,0:T(8,128)(2,1)S(1)} %get-tuple-element.16), channel_id=1, source_target_pairs={{0,192},{64,0},{128,64},{192,128},{1,193},{65,1},{129,65},{193,129... | collective-permute-start | bytes 491528 | tf_op jit(solution)/shard_map/ppermute | solution.py:258
  47.7 14.5 %collective-permute-start.11 = (bf16[1280,128]{1,0:T(8,128)(2,1)S(1)}, bf16[1280,128]{1,0:T(8,128)(2,1)S(1)}, u32[]{:S(2)}, u32[]{:S(2)}) collective-permute-start(bf16[1280,128]{1,0:T(8,128)(2,1)S(1)} %get-tuple-element.13), channel_id=1, source_target_pairs={{0,64},{64,128},{128,192},{192,0},{1,65},{65,129},{129,193},{193,1... | collective-permute-start | bytes 983048 | tf_op jit(solution)/shard_map/ppermute | solution.py:258
  47.7 14.5 %collective-permute-start.12 = (bf16[1280,128]{1,0:T(8,128)(2,1)S(1)}, bf16[1280,128]{1,0:T(8,128)(2,1)S(1)}, u32[]{:S(2)}, u32[]{:S(2)}) collective-permute-start(bf16[1280,128]{1,0:T(8,128)(2,1)S(1)} %get-tuple-element.14), channel_id=1, source_target_pairs={{0,192},{64,0},{128,64},{192,128},{1,193},{65,1},{129,65},{193,129... | collective-permute-start | bytes 983048 | tf_op jit(solution)/shard_map/ppermute | solution.py:258
  51.7 10.5 %collective-permute-start.14 = (bf16[640,128]{1,0:T(8,128)(2,1)S(1)}, bf16[640,128]{1,0:T(8,128)(2,1)S(1)}, u32[]{:S(2)}, u32[]{:S(2)}) collective-permute-start(bf16[640,128]{1,0:T(8,128)(2,1)S(1)} %collective-permute-done.13), channel_id=1, source_target_pairs={{0,64},{64,128},{128,192},{192,0},{1,65},{65,129},{129,193},{193,1... | collective-permute-start | bytes 491528 | tf_op jit(solution)/shard_map/ppermute | solution.py:258
  51.7 10.5 %collective-permute-start.16 = (bf16[640,128]{1,0:T(8,128)(2,1)S(1)}, bf16[640,128]{1,0:T(8,128)(2,1)S(1)}, u32[]{:S(2)}, u32[]{:S(2)}) collective-permute-start(bf16[640,128]{1,0:T(8,128)(2,1)S(1)} %collective-permute-done.15), channel_id=1, source_target_pairs={{0,192},{64,0},{128,64},{192,128},{1,193},{65,1},{129,65},{193,129... | collective-permute-start | bytes 491528 | tf_op jit(solution)/shard_map/ppermute | solution.py:258
  65.6 2.7 %collective-permute-start.17 = (bf16[1728,128]{1,0:T(8,128)(2,1)S(1)}, bf16[1728,128]{1,0:T(8,128)(2,1)S(1)}, u32[]{:S(2)}, u32[]{:S(2)}) collective-permute-start(bf16[1728,128]{1,0:T(8,128)(2,1)S(1)} %get-tuple-element.18), channel_id=1, source_target_pairs={{0,32},{32,0},{1,33},{33,1},{2,34},{34,2},{3,35},{35,3},{4,36},{36... | collective-permute-start | bytes 1327112 | tf_op jit(solution)/shard_map/ppermute | solution.py:262
  117.0 6.6 %collective-permute-start.18 = (bf16[1728,128]{1,0:T(8,128)(2,1)S(1)}, bf16[1728,128]{1,0:T(8,128)(2,1)S(1)}, u32[]{:S(2)}, u32[]{:S(2)}) collective-permute-start(bf16[1728,128]{1,0:T(8,128)(2,1)S(1)} %bitcast.22), channel_id=1, source_target_pairs={{0,32},{32,0},{1,33},{33,1},{2,34},{34,2},{3,35},{35,3},{4,36},{36... | collective-permute-start | bytes 1327112 | tf_op jit(solution)/shard_map/ppermute | solution.py:262
